TPU v7x, 32 devices: a whole 2x2x4 slice. The times are simulated.
32 devices in a mesh: groups: 2 (over y), lat: 4 (over z), layer: 2 (over x), tok: 2 (over core).
Axes of the slice: x: 2, y: 2, z: 4, core: 2. Of those that a mesh axis runs over, the one named last changes fastest.
Arguments:
- tokens: bfloat16 [1024, 2, 2304], P(('groups', 'lat'), 'layer'), parts along dimension 0, may hold values from -6 to 6
- w_enc: bfloat16 [2, 2304, 8192], P('layer', None, ('lat', 'tok')), may hold values from -0.09375 to 0.09375
- b_enc: float32 [8192], P(('lat', 'tok')), may hold values from -3 to 3
- w_dec: bfloat16 [2, 8192, 2304], P('layer', ('lat', 'tok')), may hold values from -0.25 to 0.25
- b_dec: float32 [2, 2304], P('layer'), may hold values from -3 to 3
- block_ids: int32 [8, 16], P('groups'), parts along dimension 0, may hold values from 0 to 127, as said below
- counts: int32 [8], P('groups'), parts along dimension 0, may hold values from 8 to 16, as said below
Outputs:
- residual: bfloat16 [1024, 2, 2304], P(('groups', 'lat'), 'layer'), parts along dimension 0
- scale_grad: float32 [16384], P(('groups', 'lat', 'tok')), parts along dimension 0
There are 2 independent parts, one for each index of `groups`. A program takes and returns all parts, laid end to end along the dimension named above; an argument that names none is the same for every part. Nothing has to cross between parts.
Inputs may be any that keep to these rules, and one draw needn't show every extreme that they name: `block_ids`: within one token block the 16 slots name distinct latent blocks; of the blocks k * 16 to (k + 1) * 16 - 1 of one latent shard k, at most 3 are named by live slots of one token block, and in every token block some shard has exactly 3. `counts`: some token block has all 16 slots live.
All inputs are finite; a program needn't handle non-finite values.
Results may differ from a plain program's by a relative error of at most 0.013.
Values may be sent and summed in bfloat16 or wider, within the bound.
No kernel may reach another device: no remote copies, remote signals or barrier semaphores. Data moves between devices by JAX's collectives and lax.ppermute only.
A program may use at most 64 MiB of HBM per device.

v0:
```python
import jax
import jax.numpy as jnp
from jax import lax
from jax.sharding import PartitionSpec as P

LATBLK = 64
TBLK = 128
CAP = 3


def on_device(tokens, w_enc, b_enc, w_dec, b_dec, block_ids, counts):
    own_rows, layers_here, width = tokens.shape
    latents_here = w_enc.shape[2]
    device_blocks = latents_here // LATBLK
    block_total, slot_total = block_ids.shape
    slot_width = CAP * LATBLK
    tok_size = lax.axis_size("tok")
    cycle_place = lax.axis_index("lat") * tok_size + lax.axis_index("tok")
    live = jnp.arange(slot_total, dtype=jnp.int32)[None, :] < counts[:, None]
    mine = live & (block_ids // device_blocks == cycle_place)
    position = jnp.cumsum(mine.astype(jnp.int32), axis=1) - 1
    select = (
        mine[:, :, None] & (position[:, :, None] == jnp.arange(CAP, dtype=jnp.int32)[None, None, :])
    ).astype(jnp.int32)
    local_pick = jnp.sum(select * (block_ids % device_blocks)[:, :, None], axis=1)
    filled = jnp.sum(select, axis=1) > 0
    enc_blocks = w_enc.reshape(layers_here, width, device_blocks, LATBLK)
    dec_blocks = w_dec.reshape(layers_here, device_blocks, LATBLK, width)

    def enc_select(pick):
        return jnp.take(enc_blocks, pick, axis=2).reshape(layers_here, width, slot_width)

    def dec_select(pick):
        return jnp.take(dec_blocks, pick, axis=1).reshape(layers_here, slot_width, width)

    def over_blocks(piece, block_fn):
        count = piece.shape[0]
        block_count = count // TBLK
        grouped = piece.reshape((block_count, TBLK) + piece.shape[1:])

        def apply_one(pair):
            return block_fn(pair[0], pair[1])

        result = lax.map(apply_one, (grouped, local_pick))
        return result.reshape((count,) + result.shape[2:])

    def encode_block(token_block, pick):
        return jnp.einsum(
            "tld,ldk->tk", token_block, enc_select(pick), preferred_element_type=jnp.float32
        )

    pre_part = over_blocks(lax.all_gather(tokens, "lat", axis=0, tiled=True), encode_block).reshape(
        block_total, TBLK, slot_width
    )
    bias_pick = jnp.take(b_enc.reshape(device_blocks, LATBLK), local_pick, axis=0).reshape(
        block_total, 1, slot_width
    )
    fill_mask = jnp.repeat(filled.astype(jnp.float32), LATBLK, axis=1).reshape(
        block_total, 1, slot_width
    )
    pre = lax.psum(pre_part.astype(jnp.bfloat16), "layer").astype(jnp.float32) + bias_pick
    codes = (jnp.maximum(pre, 0.0) * fill_mask).astype(jnp.bfloat16)

    def decode_block(pair):
        return jnp.einsum(
            "tk,lkd->tld", pair[0], dec_select(pair[1]), preferred_element_type=jnp.float32
        )

    cover = min(lax.axis_size("lat") * own_rows // TBLK + 2, block_total)
    result = lax.map(decode_block, (codes, local_pick)).reshape(cover * TBLK, layers_here, width)
    cycle_part = lax.psum_scatter(
        result.astype(jnp.bfloat16), "lat", scatter_dimension=0, tiled=True
    )
    summed = lax.psum(cycle_part, "tok").astype(jnp.float32)
    recon = summed + b_dec[None]
    residual = (recon - tokens.astype(jnp.float32)).astype(jnp.bfloat16)

    def back_block(error_block, pick):
        return jnp.einsum(
            "tld,lkd->tk", error_block, dec_select(pick), preferred_element_type=jnp.float32
        )

    grad_part = over_blocks(
        lax.all_gather(residual, "lat", axis=0, tiled=True), back_block
    ).reshape(block_total, TBLK, slot_width)
    onehot = (
        (local_pick[:, :, None] == jnp.arange(device_blocks, dtype=jnp.int32)[None, None, :])
        & filled[:, :, None]
    ).astype(jnp.float32)
    grad = lax.psum(grad_part.astype(jnp.bfloat16), "layer").astype(jnp.float32)
    contrib = jnp.sum(codes.astype(jnp.float32) * grad, axis=1).reshape(block_total, CAP, LATBLK)
    scale_grad = jnp.einsum("bcs,bck->sk", onehot, contrib) / TBLK
    return (residual, scale_grad.reshape(latents_here))


def solution(mesh):
    in_specs = (
        P(("groups", "lat"), "layer", None),
        P("layer", None, ("lat", "tok")),
        P(("lat", "tok")),
        P("layer", ("lat", "tok"), None),
        P("layer", None),
        P("groups", None),
        P("groups"),
    )
    out_specs = (P(("groups", "lat"), "layer", None), P(("groups", "lat", "tok")))
    return jax.shard_map(
        on_device, mesh=mesh, in_specs=in_specs, out_specs=out_specs, check_vma=False
    )
```

profile of v0, /device:TPU:0, one launch (start us, length us, event | category | flops | bytes accessed | tf_op | source)
XLA Modules:
  0.0 292.6 jit_solution(5161841358439407260)
XLA Ops:
  7.2 0.7 all-gather.3.cloned.1.call-update
  8.0 0.8 fusion.26
  8.7 0.2 reduce_window_sum.11
  8.9 0.7 add_select_fusion
  9.6 0.2 convert_reduce_fusion
  9.8 0.1 copy.22
  10.0 0.8 reshape.205
  10.7 0.6 gather_fusion.3
  11.3 0.1 copy.23
  11.6 6.7 %copy.20 = bf16[1,2304,1024]{1,2,0:T(8,128)(2,1)} copy(bf16[1,2304,1024]{2,1,0:T(8,128)(2,1)} %param.16) | data formatting | bytes 9437184 | tf_op args[1]
  18.3 44.5 %all-gather.3.cloned.1.call-done = bf16[512,1,2304]{2,0,1:T(8,128)(2,1)} async-done(((bf16[128,1,2304]{2,0,1:T(8,128)(2,1)}), bf16[512,1,2304]{2,0,1:T(8,128)(2,1)}) %all-gather.3.cloned.1.call-update) | async-done | bytes 2359312 | tf_op jit(solution)/shard_map/all_gather | solution.py:52
  62.8 18.6 %while.30 = (s32[]{:T(128)}, bf16[4,128,192]{1,2,0:T(8,128)(2,1)S(1)}, bf16[4,128,1,2304]{3,1,2,0:T(8,128)(2,1)}, s32[4,3]{1,0:T(4,128)S(1)}, bf16[1,2304,16,64]{1,3,2,0:T(8,128)(2,1)}, /*index=5*/s32[]{:T(128)}) while((s32[]{:T(128)}, bf16[4,128,192]{1,2,0:T(8,128)(2,1)S(1)}, bf16[4,128,1,2304]{3,1,2,0:T(8,128)(2,1)}, s32[4,3]{1,0:T(4,128)S(1)}, ...), condition=%wide.region_3.4_spmd, body=%wide.region_2.3_spmd.sunk | while | flops 113689632 | bytes 5117071 | solution.py:44
  62.9 2.9 %gather_fusion = bf16[3,2304,64]{1,2,0:T(8,128)(2,1)S(1)} fusion(bf16[2304,16,64]{0,2,1:T(8,128)(2,1)} %bitcast.118, s32[1024]{0:T(1024)S(1)} %pad_clamp_fusion.7), kind=kCustom, calls=%fused_computation.clone.1 | custom fusion | bytes 1769484 | tf_op jit(solution)/shard_map/while/body/eval_jaxpr/jit(_take)/gather | solution.py:31
  65.8 0.2 bitcast_select_fusion.6
  66.0 1.5 fusion.44
  67.5 2.9 %gather_fusion = bf16[3,2304,64]{1,2,0:T(8,128)(2,1)S(1)} fusion(bf16[2304,16,64]{0,2,1:T(8,128)(2,1)} %bitcast.118, s32[1024]{0:T(1024)S(1)} %pad_clamp_fusion.7), kind=kCustom, calls=%fused_computation.clone.1 | custom fusion | bytes 1769484 | tf_op jit(solution)/shard_map/while/body/eval_jaxpr/jit(_take)/gather | solution.py:31
  70.5 0.2 bitcast_select_fusion.6
  70.6 1.5 fusion.44
  72.1 2.9 %gather_fusion = bf16[3,2304,64]{1,2,0:T(8,128)(2,1)S(1)} fusion(bf16[2304,16,64]{0,2,1:T(8,128)(2,1)} %bitcast.118, s32[1024]{0:T(1024)S(1)} %pad_clamp_fusion.7), kind=kCustom, calls=%fused_computation.clone.1 | custom fusion | bytes 1769484 | tf_op jit(solution)/shard_map/while/body/eval_jaxpr/jit(_take)/gather | solution.py:31
  75.1 0.2 bitcast_select_fusion.6
  75.3 1.5 fusion.44
  76.8 2.9 %gather_fusion = bf16[3,2304,64]{1,2,0:T(8,128)(2,1)S(1)} fusion(bf16[2304,16,64]{0,2,1:T(8,128)(2,1)} %bitcast.118, s32[1024]{0:T(1024)S(1)} %pad_clamp_fusion.7), kind=kCustom, calls=%fused_computation.clone.1 | custom fusion | bytes 1769484 | tf_op jit(solution)/shard_map/while/body/eval_jaxpr/jit(_take)/gather | solution.py:31
  79.8 0.2 bitcast_select_fusion.6
  79.9 1.5 fusion.44
  81.4 0.7 copy-done.4
  82.2 0.1 copy.25
  82.4 21.0 %all-reduce.4.cloned.1.call-done = bf16[4,128,192]{1,2,0:T(8,128)(2,1)} async-done(((bf16[4,128,192]{1,2,0:T(8,128)(2,1)}), bf16[4,128,192]{1,2,0:T(8,128)(2,1)}) %all-reduce.4.cloned.1.call-update) | async-done | bytes 196624 | tf_op jit(solution)/shard_map/psum | solution.py:61
  103.4 1.2 multiply_convert_fusion
  104.6 14.1 %while.31 = (s32[]{:T(128)}, bf16[4,128,1,2304]{3,1,2,0:T(8,128)(2,1)S(1)}, bf16[4,128,192]{1,2,0:T(8,128)(2,1)S(1)}, s32[4,3]{1,0:T(4,128)S(1)}, bf16[1,16,64,2304]{3,2,1,0:T(8,128)(2,1)}, /*index=5*/s32[]{:T(128)}) while((s32[]{:T(128)}, bf16[4,128,1,2304]{3,1,2,0:T(8,128)(2,1)S(1)}, bf16[4,128,192]{1,2,0:T(8,128)(2,1)S(1)}, ...), condition=%wide.region_7.9_spmd, body=%wide.region_6.8_spmd.sunk | while | flops 113689616 | bytes 5657727 | solution.py:70
  104.7 2.9 %gather_fusion.1 = bf16[3,64,2304]{2,1,0:T(8,128)(2,1)S(1)} fusion(bf16[16,64,2304]{2,1,0:T(8,128)(2,1)} %bitcast.120, s32[1024]{0:T(1024)S(1)} %pad_clamp_fusion.8), kind=kCustom, calls=%fused_computation.1.clone.clone.1 | custom fusion | bytes 1769484 | tf_op jit(solution)/shard_map/while/body/eval_jaxpr/jit(_take)/gather | solution.py:34
  107.6 0.2 bitcast_select_fusion.7
  107.8 0.4 fusion.47
  108.2 2.9 %gather_fusion.1 = bf16[3,64,2304]{2,1,0:T(8,128)(2,1)S(1)} fusion(bf16[16,64,2304]{2,1,0:T(8,128)(2,1)} %bitcast.120, s32[1024]{0:T(1024)S(1)} %pad_clamp_fusion.8), kind=kCustom, calls=%fused_computation.1.clone.clone.1 | custom fusion | bytes 1769484 | tf_op jit(solution)/shard_map/while/body/eval_jaxpr/jit(_take)/gather | solution.py:34
  111.1 0.2 bitcast_select_fusion.7
  111.3 0.4 fusion.47
  111.7 2.9 %gather_fusion.1 = bf16[3,64,2304]{2,1,0:T(8,128)(2,1)S(1)} fusion(bf16[16,64,2304]{2,1,0:T(8,128)(2,1)} %bitcast.120, s32[1024]{0:T(1024)S(1)} %pad_clamp_fusion.8), kind=kCustom, calls=%fused_computation.1.clone.clone.1 | custom fusion | bytes 1769484 | tf_op jit(solution)/shard_map/while/body/eval_jaxpr/jit(_take)/gather | solution.py:34
  114.7 0.2 bitcast_select_fusion.7
  114.8 0.4 fusion.47
  115.2 2.9 %gather_fusion.1 = bf16[3,64,2304]{2,1,0:T(8,128)(2,1)S(1)} fusion(bf16[16,64,2304]{2,1,0:T(8,128)(2,1)} %bitcast.120, s32[1024]{0:T(1024)S(1)} %pad_clamp_fusion.8), kind=kCustom, calls=%fused_computation.1.clone.clone.1 | custom fusion | bytes 1769484 | tf_op jit(solution)/shard_map/while/body/eval_jaxpr/jit(_take)/gather | solution.py:34
  118.2 0.2 bitcast_select_fusion.7
  118.3 0.3 fusion.47
  118.7 1.4 copy-done.1
  120.2 48.1 %reduce-scatter.2.cloned.1.call-done = bf16[128,1,2304]{2,0,1:T(8,128)(2,1)} async-done(((bf16[512,1,2304]{2,0,1:T(8,128)(2,1)}), bf16[128,1,2304]{2,0,1:T(8,128)(2,1)}) %reduce-scatter.2.cloned.1.call-update) | async-done | bytes 589840 | tf_op jit(solution)/shard_map/reduce_scatter | solution.py:71
  168.4 20.5 %all-reduce.6.cloned.1.call-done = bf16[128,1,2304]{2,0,1:T(8,128)(2,1)} async-done(((bf16[128,1,2304]{2,0,1:T(8,128)(2,1)}), bf16[128,1,2304]{2,0,1:T(8,128)(2,1)}) %all-reduce.6.cloned.1.call-update) | async-done | bytes 589840 | tf_op jit(solution)/shard_map/psum | solution.py:74
  188.9 2.1 subtract_convert_fusion
  191.0 51.8 %all-gather.5.cloned.1.call-done = bf16[512,1,2304]{2,0,1:T(8,128)(2,1)} async-done(((bf16[128,1,2304]{2,0,1:T(8,128)(2,1)}), bf16[512,1,2304]{2,0,1:T(8,128)(2,1)}) %all-gather.5.cloned.1.call-update) | async-done | bytes 2359312 | tf_op jit(solution)/shard_map/all_gather | solution.py:84
  242.8 18.5 %while.32 = (s32[]{:T(128)}, bf16[4,128,192]{1,2,0:T(8,128)(2,1)S(1)}, bf16[4,128,1,2304]{3,1,2,0:T(8,128)(2,1)}, s32[4,3]{1,0:T(4,128)S(1)}, bf16[1,16,64,2304]{3,2,1,0:T(8,128)(2,1)}, /*index=5*/s32[]{:T(128)}) while((s32[]{:T(128)}, bf16[4,128,192]{1,2,0:T(8,128)(2,1)S(1)}, bf16[4,128,1,2304]{3,1,2,0:T(8,128)(2,1)}, ...), condition=%wide.region_11.13_spmd, body=%wide.region_10.12_spmd.sunk | while | flops 113689616 | bytes 5117055 | solution.py:44
  242.9 3.0 %gather_fusion.2 = bf16[3,64,2304]{2,1,0:T(8,128)(2,1)S(1)} fusion(bf16[16,64,2304]{2,1,0:T(8,128)(2,1)} %bitcast.121, s32[1024]{0:T(1024)S(1)} %pad_clamp_fusion.9), kind=kCustom, calls=%fused_computation.2.clone.clone.1 | custom fusion | bytes 1769484 | tf_op jit(solution)/shard_map/while/body/eval_jaxpr/jit(_take)/gather | solution.py:34
  245.9 0.2 bitcast_select_fusion.8
  246.0 1.5 fusion.50
  247.6 2.9 %gather_fusion.2 = bf16[3,64,2304]{2,1,0:T(8,128)(2,1)S(1)} fusion(bf16[16,64,2304]{2,1,0:T(8,128)(2,1)} %bitcast.121, s32[1024]{0:T(1024)S(1)} %pad_clamp_fusion.9), kind=kCustom, calls=%fused_computation.2.clone.clone.1 | custom fusion | bytes 1769484 | tf_op jit(solution)/shard_map/while/body/eval_jaxpr/jit(_take)/gather | solution.py:34
  250.5 0.2 bitcast_select_fusion.8
  250.7 1.5 fusion.50
  252.2 2.9 %gather_fusion.2 = bf16[3,64,2304]{2,1,0:T(8,128)(2,1)S(1)} fusion(bf16[16,64,2304]{2,1,0:T(8,128)(2,1)} %bitcast.121, s32[1024]{0:T(1024)S(1)} %pad_clamp_fusion.9), kind=kCustom, calls=%fused_computation.2.clone.clone.1 | custom fusion | bytes 1769484 | tf_op jit(solution)/shard_map/while/body/eval_jaxpr/jit(_take)/gather | solution.py:34
  255.1 0.2 bitcast_select_fusion.8
  255.3 1.5 fusion.50
  256.8 2.9 %gather_fusion.2 = bf16[3,64,2304]{2,1,0:T(8,128)(2,1)S(1)} fusion(bf16[16,64,2304]{2,1,0:T(8,128)(2,1)} %bitcast.121, s32[1024]{0:T(1024)S(1)} %pad_clamp_fusion.9), kind=kCustom, calls=%fused_computation.2.clone.clone.1 | custom fusion | bytes 1769484 | tf_op jit(solution)/shard_map/while/body/eval_jaxpr/jit(_take)/gather | solution.py:34
  259.8 0.2 bitcast_select_fusion.8
  259.9 1.5 fusion.50
  261.4 0.7 copy-done.3
  262.1 21.3 %all-reduce.8.cloned.1.call-done = bf16[4,128,192]{1,2,0:T(8,128)(2,1)} async-done(((bf16[4,128,192]{1,2,0:T(8,128)(2,1)}), bf16[4,128,192]{1,2,0:T(8,128)(2,1)}) %all-reduce.8.cloned.1.call-update) | async-done | bytes 196624 | tf_op jit(solution)/shard_map/psum | solution.py:90
  283.4 1.4 multiply_reduce_fusion
  284.9 0.3 fusion.15
  285.1 0.7 reshape.209
  (63 shorter events, 1.2 us)
Async XLA Ops:
  7.2 55.6 %all-gather.3.cloned.1.call-start = ((), (), s32[]{:S(2)}) async-start(), calls=%async_computation.1 | async-start | bytes 2949120 | tf_op jit(solution)/shard_map/all_gather | solution.py:52
  7.9 95.5 %all-reduce.4.cloned.1.call-start = ((), (), s32[]{:S(2)}) async-start(), calls=%async_computation.2 | async-start | bytes 393216 | tf_op jit(solution)/shard_map/psum | solution.py:61
  81.4 0.7 copy-start.4
  82.1 86.2 %reduce-scatter.2.cloned.1.call-start = ((), (), s32[]{:S(2)}) async-start(), calls=%async_computation.3 | async-start | bytes 2949120 | tf_op jit(solution)/shard_map/reduce_scatter | solution.py:71
  118.7 1.4 copy-start.1
  118.7 49.7 %copy-start.5 = (f32[1,2304]{1,0:T(1,128)S(1)}, f32[1,2304]{1,0:T(1,128)}, u32[]{:S(2)}) copy-start(f32[1,2304]{1,0:T(1,128)} %param.19) | copy-start | bytes 27652
  118.7 70.2 %copy-start = (bf16[128,1,2304]{2,0,1:T(8,128)(2,1)S(1)}, bf16[128,1,2304]{2,0,1:T(8,128)(2,1)}, u32[]{:S(2)}) copy-start(bf16[128,1,2304]{2,0,1:T(8,128)(2,1)} %param.15) | copy-start | bytes 1769476
  120.1 68.8 %all-reduce.6.cloned.1.call-start = ((), (), s32[]{:S(2)}) async-start(), calls=%async_computation.4 | async-start | bytes 1179648 | tf_op jit(solution)/shard_map/psum | solution.py:74
  168.3 74.5 %all-gather.5.cloned.1.call-start = ((), (), s32[]{:S(2)}) async-start(), calls=%async_computation.5 | async-start | bytes 2949120 | tf_op jit(solution)/shard_map/all_gather | solution.py:84
  191.0 92.4 %all-reduce.8.cloned.1.call-start = ((), (), s32[]{:S(2)}) async-start(), calls=%async_computation.6 | async-start | bytes 393216 | tf_op jit(solution)/shard_map/psum | solution.py:90
  242.8 40.6 %copy-start.2 = (bf16[4,128,192]{1,2,0:T(8,128)(2,1)S(1)}, bf16[4,128,192]{1,2,0:T(8,128)(2,1)}, u32[]{:S(2)}) copy-start(bf16[4,128,192]{1,2,0:T(8,128)(2,1)} %all-reduce.4.cloned.1.call-done) | copy-start | bytes 589828
  261.4 0.7 copy-start.3
Sparse Core Ops, SparseCore 0:
  9.6 53.1 all-gather.2
  82.2 21.1 all-reduce.3
  120.2 48.0 reduce-scatter.1
  170.5 18.3 all-reduce.5
  191.1 51.6 all-gather.4
  262.2 21.1 all-reduce.7
where the time goes:
time: 294 us; the launch traced here: 293 us
  waiting for transfers between devices  208 us (71%)
  local copies, waits for them, and re-layouts  47.6 us (16%)
  between operations  14.3 us (5%)
  matrix products  13.5 us (5%)
  other arithmetic  8.67 us (3%)
    all_gather x1, waiting for transfers between devices, on_device(): lax.all_gather(residual, 'lat', axis=0, tiled=True)  51.8 us
    reduce_scatter x1, waiting for transfers between devices, on_device(): lax.psum_scatter(result.astype(jnp.bfloat16), 'lat', scatter_dimension=0,...  48.1 us
    all_gather x1, waiting for transfers between devices, on_device(): lax.all_gather(tokens, 'lat', axis=0, tiled=True)  44.5 us
    gather x8, local copies, waits for them, and re-layouts, dec_select(): jnp.take(dec_blocks, pick, axis=1).reshape(layers_here, slot_width, width)  23.6 us
    psum x1, waiting for transfers between devices, on_device(): grad = lax.psum(grad_part.astype(jnp.bfloat16), 'layer').astype(jnp.float32)  21.3 us
    psum x1, waiting for transfers between devices, on_device(): lax.psum(pre_part.astype(jnp.bfloat16), 'layer').astype(jnp.float32)  21 us
    psum x1, waiting for transfers between devices, on_device(): summed = lax.psum(cycle_part, 'tok').astype(jnp.float32)  20.5 us
    gather x4, local copies, waits for them, and re-layouts, enc_select(): jnp.take(enc_blocks, pick, axis=2).reshape(layers_here, width, slot_width)  11.8 us
  transfers between devices with their start and end apart: 6, of which 6 were waited for; matrix products, arithmetic and copies ran while one was open for 4% of the time, Pallas kernels for 0%

commit v1 on v0

v1 whole, which is shorter than its diff:
```python
import jax
import jax.numpy as jnp
from jax import lax
from jax.sharding import PartitionSpec as P

LATBLK = 64
TBLK = 128
CAP = 3
SLOT = CAP * LATBLK


def swap(value, axis, mask):
    size = lax.axis_size(axis)
    return lax.ppermute(value, axis, [(i, i ^ mask) for i in range(size)])


def masks_of(axis):
    size = lax.axis_size(axis)
    return [1 << i for i in range(size.bit_length() - 1)]


def spread(value):
    have = {0: value}
    for mask in reversed(masks_of("lat")):
        for offset in list(have):
            have[offset ^ mask] = swap(have[offset], "lat", mask)
    return have


def collect(parts):
    held = dict(parts)
    for mask in masks_of("lat"):
        for offset in sorted(held):
            if offset & mask:
                arrived = swap(held.pop(offset).astype(jnp.bfloat16), "lat", mask)
                held[offset ^ mask] = held[offset ^ mask] + arrived.astype(jnp.float32)
    return held[0]


def sum_layers(value):
    for mask in masks_of("layer"):
        total = value.astype(jnp.float32) + swap(value, "layer", mask).astype(jnp.float32)
        value = total.astype(value.dtype)
    return total


def on_device(tokens, w_enc, b_enc, w_dec, b_dec, block_ids, counts):
    own_rows, layers_here, width = tokens.shape
    assert own_rows == TBLK and layers_here == 1
    latents_here = w_enc.shape[2]
    device_blocks = latents_here // LATBLK
    slot_total = block_ids.shape[1]
    half = width // 2
    lat_size = lax.axis_size("lat")
    place = lax.axis_index("lat")
    core = lax.axis_index("tok")
    cycle_place = place * lax.axis_size("tok") + core
    bf16, f32 = jnp.bfloat16, jnp.float32

    order = place ^ jnp.arange(lat_size, dtype=jnp.int32)
    ids = jnp.take(block_ids, order, axis=0)
    live = jnp.arange(slot_total, dtype=jnp.int32)[None, :] < jnp.take(counts, order)[:, None]
    mine = live & (ids // device_blocks == cycle_place)
    position = jnp.cumsum(mine.astype(jnp.int32), axis=1) - 1
    select = mine[:, :, None] & (
        position[:, :, None] == jnp.arange(CAP, dtype=jnp.int32)[None, None, :]
    )
    pick = jnp.sum(select.astype(jnp.int32) * (ids % device_blocks + 1)[:, :, None], axis=1) - 1

    onehot = pick[:, :, None] == jnp.arange(device_blocks, dtype=jnp.int32)[None, None, :]
    column = (
        jnp.where(pick < 0, -latents_here, pick * LATBLK)[:, :, None]
        + jnp.arange(LATBLK, dtype=jnp.int32)[None, None, :]
    ).reshape(1, lat_size * SLOT)
    choose = (jnp.arange(latents_here, dtype=jnp.int32)[:, None] == column).astype(bf16)
    bias_own = jnp.sum(
        jnp.where(onehot[:, :, :, None], b_enc.reshape(1, 1, device_blocks, LATBLK), 0.0), axis=2
    ).reshape(lat_size, SLOT)

    def picked(a, b):
        return jnp.dot(a, b, preferred_element_type=f32).astype(bf16)

    enc_sel = picked(w_enc[0], choose)
    dec_sel = picked(choose.T, w_dec[0])

    def cut(value, axis, which):
        return lax.dynamic_slice_in_dim(value, which * half, half, axis)

    enc_two = (cut(enc_sel, 0, core), swap(cut(enc_sel, 0, 1 - core), "tok", 1))
    dec_two = (cut(dec_sel, 1, core), swap(cut(dec_sel, 1, 1 - core), "tok", 1))
    bias_two = (bias_own, swap(bias_own, "tok", 1))

    def slot(offset):
        return slice(offset * SLOT, (offset + 1) * SLOT)

    own = tokens.reshape(own_rows, width)
    own_half = cut(own, 1, core)
    token_blocks = spread(own_half)

    codes = {}
    parts = {}
    for offset in token_blocks:
        block = token_blocks[offset]
        part = jnp.stack(
            [jnp.dot(block, w[:, slot(offset)], preferred_element_type=f32) for w in enc_two]
        ).astype(bf16)
        other = swap(part, "tok", 1)
        both = (part.astype(f32) + other[::-1].astype(f32)).astype(bf16)
        pre = sum_layers(both) + jnp.stack([b[offset] for b in bias_two])[:, None, :]
        codes[offset] = jnp.maximum(pre, 0.0).astype(bf16)
        parts[offset] = sum(
            jnp.dot(codes[offset][i], dec_two[i][slot(offset)], preferred_element_type=f32)
            for i in range(2)
        )

    recon = collect(parts) + cut(b_dec, 1, core)
    residual_half = (recon - own_half.astype(f32)).astype(bf16)
    residual_other = swap(residual_half, "tok", 1)
    residual = jnp.where(
        core == 0,
        jnp.concatenate([residual_half, residual_other], axis=1),
        jnp.concatenate([residual_other, residual_half], axis=1),
    )

    error_blocks = spread(residual_half)
    contrib = []
    for offset in range(lat_size):
        grad = jnp.stack(
            [
                lax.dot_general(
                    error_blocks[offset],
                    w[slot(offset)],
                    (((1,), (1,)), ((), ())),
                    preferred_element_type=f32,
                )
                for w in dec_two
            ]
        )
        contrib.append(jnp.sum(codes[offset].astype(f32) * grad, axis=1))
    contrib = jnp.stack(contrib, axis=1)
    contrib = sum_layers(contrib[0] + swap(contrib[1], "tok", 1))
    scale_grad = jnp.sum(
        jnp.where(onehot[:, :, :, None], contrib.reshape(lat_size, CAP, 1, LATBLK), 0.0),
        axis=(0, 1),
    ) * (1.0 / TBLK)
    return residual.reshape(tokens.shape), scale_grad.reshape(latents_here)


def solution(mesh):
    in_specs = (
        P(("groups", "lat"), "layer", None),
        P("layer", None, ("lat", "tok")),
        P(("lat", "tok")),
        P("layer", ("lat", "tok"), None),
        P("layer", None),
        P("groups", None),
        P("groups"),
    )
    out_specs = (P(("groups", "lat"), "layer", None), P(("groups", "lat", "tok")))
    return jax.shard_map(
        on_device, mesh=mesh, in_specs=in_specs, out_specs=out_specs, check_vma=False
    )
```

time: 294 us -> 117 us (0.40)
  waiting for transfers between devices: 208 us -> 56 us
  local copies, waits for them, and re-layouts: 47.6 us -> 11.5 us
  matrix products: 13.5 us -> 29.2 us
  starting transfers between devices: 0.24 us -> 15.9 us
  between operations: 14.3 us -> 1.18 us
  other arithmetic: 8.67 us -> 3.15 us
    all_gather x2 -> x0, waiting for transfers between devices: 96.2 us -> none  [the longest x1 51.8 us: on_device(): lax.all_gather(residual, 'lat', axis=0, tiled=True)]
    psum x3 -> x0, waiting for transfers between devices: 62.7 us -> none  [the longest x1 21.3 us: on_device(): grad = lax.psum(grad_part.astype(jnp.bfloat16), 'layer').astype(jnp.float32)]
    ppermute x0 -> x23, waiting for transfers between devices: none -> 56 us  [swap(): return lax.ppermute(value, axis, [(i, i ^ mask) for i in range(size)])]
    reduce_scatter x1 -> x0, waiting for transfers between devices: 48.1 us -> none  [on_device(): lax.psum_scatter(result.astype(jnp.bfloat16), 'lat', scatter_dimension=0,...]
    gather x14 -> x2, local copies, waits for them, and re-layouts: 35.9 us -> 2.54 us  [the longest x1 1.3 us: on_device(): jnp.take(counts, order)[:, None]]
    ppermute x0 -> x23, starting transfers between devices: none -> 15.9 us  [swap(): return lax.ppermute(value, axis, [(i, i ^ mask) for i in range(size)])]
    dot_general x13 -> x26, matrix products: 13.5 us -> 29.2 us  [the longest x2 14.2 us: picked(): return jnp.dot(a, b, preferred_element_type=f32).astype(bf16)]
    unnamed x13 -> x10, local copies, waits for them, and re-layouts: 9.47 us -> 1.81 us
  transfers between devices with their start and end apart: 6 -> 23, of which waited for: 6 -> 11; matrix products, arithmetic and copies ran while one was open for 4% -> 35% of each run, Pallas kernels for 0% -> 0%
where the time goes in v1:
time: 117 us
  waiting for transfers between devices  56 us (48%)
  matrix products  29.2 us (25%)
  starting transfers between devices  15.9 us (14%)
  local copies, waits for them, and re-layouts  11.5 us (10%)
  other arithmetic  3.15 us (3%)
  between operations  1.18 us (1%)
    ppermute x23, waiting for transfers between devices, swap(): return lax.ppermute(value, axis, [(i, i ^ mask) for i in range(size)])  56 us
    ppermute x23, starting transfers between devices, swap(): return lax.ppermute(value, axis, [(i, i ^ mask) for i in range(size)])  15.9 us
    dot_general x2, matrix products, picked(): return jnp.dot(a, b, preferred_element_type=f32).astype(bf16)  14.2 us
    dot_general x8, matrix products, on_device(): jnp.dot(block, w[:, slot(offset)], preferred_element_type=f32)  10.6 us
    dynamic_slice x4, local copies, waits for them, and re-layouts, cut(): return lax.dynamic_slice_in_dim(value, which * half, half, axis)  5.66 us
  transfers between devices with their start and end apart: 23, of which 11 were waited for; matrix products, arithmetic and copies ran while one was open for 35% of the time, Pallas kernels for 0%

profile of v1, /device:TPU:0, one launch (start us, length us, event | category | flops | bytes accessed | tf_op | source)
XLA Modules:
  0.0 116.9 jit_solution(3875926121400734465)
XLA Ops:
  0.7 1.0 copy-done
  1.7 3.1 %collective-permute-start.5 = (bf16[128,1152]{1,0:T(8,128)(2,1)S(1)}, bf16[128,1152]{1,0:T(8,128)(2,1)S(1)}, u32[]{:S(2)}, u32[]{:S(2)}) collective-permute-start(bf16[128,1152]{1,0:T(8,128)(2,1)S(1)} %dynamic-slice_bitcast_fusion.2), channel_id=1, source_target_pairs={{0,4},{4,0},{8,12},{12,8},{1,5},{5,1},{9,13},{13,9},{2,6},{6,2},{1... | collective-permute-start | bytes 884744 | tf_op jit(solution)/shard_map/ppermute | solution.py:14
  4.8 2.6 %collective-permute-start.9 = (bf16[128,1152]{1,0:T(8,128)(2,1)S(1)}, bf16[128,1152]{1,0:T(8,128)(2,1)S(1)}, u32[]{:S(2)}, u32[]{:S(2)}) collective-permute-start(bf16[128,1152]{1,0:T(8,128)(2,1)S(1)} %dynamic-slice_bitcast_fusion.2), channel_id=1, source_target_pairs={{0,8},{4,12},{8,0},{12,4},{1,9},{5,13},{9,1},{13,5},{2,10},{6,14},... | collective-permute-start | bytes 884744 | tf_op jit(solution)/shard_map/ppermute | solution.py:14
  7.4 1.3 %gather_fusion = s32[4]{0:T(128)S(1)} fusion(s32[4]{0:T(128)} %param.13, s32[1024]{0:T(1024)S(1)} %pad_clamp_fusion), kind=kCustom, calls=%fused_computation | custom fusion | bytes 48 | tf_op jit(solution)/shard_map/jit(_take)/gather | solution.py:62
  8.7 1.2 %gather_fusion.1 = s32[4,16]{1,0:T(4,128)S(1)} fusion(s32[4,16]{1,0:T(4,128)} %param.12, s32[1024]{0:T(1024)S(1)} %pad_clamp_fusion), kind=kCustom, calls=%fused_computation.1 | custom fusion | bytes 528 | tf_op jit(solution)/shard_map/jit(_take)/gather | solution.py:61
  10.1 0.2 reduce_window_sum.11
  10.8 7.7 %convolution_convert_fusion = bf16[768,2304]{1,0:T(8,128)(2,1)} fusion(bf16[1,2304,1024]{2,1,0:T(8,128)(2,1)} %param.8, s32[768]{0:T(1024)S(1)} %add.194), kind=kOutput, calls=%fused_computation.2 | convolution fusion | flops 3627220992 | bytes 8260608 | tf_op jit(solution)/shard_map/dot_general | solution.py:81
  18.4 4.1 %dynamic-slice_bitcast_fusion.1 = (bf16[1152,768]{0,1:T(8,128)(2,1)}, bf16[1152,768]{0,1:T(8,128)(2,1)}) fusion(bf16[768,2304]{1,0:T(8,128)(2,1)} %convolution_convert_fusion, s32[]{:T(128)S(6)} %select_n.110, s32[]{:T(128)S(6)} %select_n.118), kind=kLoop, calls=%fused_computation.22 | loop fusion | bytes 7077896 | tf_op jit(solution)/shard_map/dynamic_slice | solution.py:87
  23.0 0.5 collective-permute-start.3
  23.5 6.5 %convolution_convert_fusion.1 = bf16[768,2304]{1,0:T(8,128)(2,1)S(1)} fusion(bf16[1,1024,2304]{2,1,0:T(8,128)(2,1)} %param.10, s32[768]{0:T(1024)S(1)} %add.194), kind=kOutput, calls=%fused_computation.3 | convolution fusion | flops 3626434560 | bytes 8260608 | tf_op jit(solution)/shard_map/dot_general | solution.py:81
  30.0 1.5 %constant_dynamic-slice_fusion = bf16[768,1152]{1,0:T(8,128)(2,1)} fusion(bf16[768,2304]{1,0:T(8,128)(2,1)S(1)} %convolution_convert_fusion.1, s32[]{:T(128)S(6)} %select_n.118), kind=kLoop, calls=%fused_computation.142 | loop fusion | bytes 3538948 | tf_op jit(solution)/shard_map/dynamic_slice | solution.py:87
  31.5 0.7 copy-done.1
  32.3 1.3 %fusion.15 = bf16[1,128,192]{1,2,0:T(8,128)(2,1)S(1)} fusion(bf16[128,1152]{1,0:T(8,128)(2,1)S(1)} %dynamic-slice_bitcast_fusion.2, bf16[1152,768]{0,1:T(8,128)(2,1)} %get-tuple-element.4), kind=kOutput, calls=%fused_computation.41 | convolution fusion | flops 56647680 | bytes 786432 | tf_op jit(solution)/shard_map/dot_general | solution.py:105
  34.0 0.5 collective-permute-start.12
  34.6 1.3 %fusion.19 = bf16[1,128,192]{1,2,0:T(8,128)(2,1)S(1)} fusion(bf16[128,1152]{1,0:T(8,128)(2,1)S(1)} %collective-permute-done.9, bf16[1152,768]{0,1:T(8,128)(2,1)} %get-tuple-element.4), kind=kOutput, calls=%fused_computation.45 | convolution fusion | flops 56647680 | bytes 786432 | tf_op jit(solution)/shard_map/dot_general | solution.py:105
  35.9 1.3 %fusion.17 = bf16[1,128,192]{1,2,0:T(8,128)(2,1)S(1)} fusion(bf16[128,1152]{1,0:T(8,128)(2,1)S(1)} %collective-permute-done.5, bf16[1152,768]{0,1:T(8,128)(2,1)} %get-tuple-element.4), kind=kOutput, calls=%fused_computation.43 | convolution fusion | flops 56647680 | bytes 786432 | tf_op jit(solution)/shard_map/dot_general | solution.py:105
  37.2 6.3 %collective-permute-done.12 = bf16[128,1152]{1,0:T(8,128)(2,1)S(1)} collective-permute-done((bf16[128,1152]{1,0:T(8,128)(2,1)S(1)}, bf16[128,1152]{1,0:T(8,128)(2,1)S(1)}, u32[]{:S(2)}, u32[]{:S(2)}) %collective-permute-start.12) | collective-permute-done | bytes 294944 | tf_op jit(solution)/shard_map/ppermute | solution.py:14
  43.5 1.3 %fusion.21 = bf16[1,128,192]{1,2,0:T(8,128)(2,1)S(1)} fusion(bf16[128,1152]{1,0:T(8,128)(2,1)S(1)} %collective-permute-done.12, bf16[1152,768]{0,1:T(8,128)(2,1)} %get-tuple-element.4), kind=kOutput, calls=%fused_computation.47 | convolution fusion | flops 56647680 | bytes 786432 | tf_op jit(solution)/shard_map/dot_general | solution.py:105
  44.8 1.3 %fusion.18 = bf16[1,128,192]{1,2,0:T(8,128)(2,1)S(1)} fusion(bf16[128,1152]{1,0:T(8,128)(2,1)S(1)} %collective-permute-done.5, bf16[1152,768]{0,1:T(8,128)(2,1)} %collective-permute-done), kind=kOutput, calls=%fused_computation.44 | convolution fusion | flops 56647680 | bytes 786432 | tf_op jit(solution)/shard_map/dot_general | solution.py:105
  46.2 1.3 %fusion.22 = bf16[1,128,192]{1,2,0:T(8,128)(2,1)S(1)} fusion(bf16[128,1152]{1,0:T(8,128)(2,1)S(1)} %collective-permute-done.12, bf16[1152,768]{0,1:T(8,128)(2,1)} %collective-permute-done), kind=kOutput, calls=%fused_computation.48 | convolution fusion | flops 56647680 | bytes 786432 | tf_op jit(solution)/shard_map/dot_general | solution.py:105
  47.5 0.6 collective-permute-start.13
  48.1 1.6 %fusion.20 = bf16[1,128,192]{1,2,0:T(8,128)(2,1)S(1)} fusion(bf16[128,1152]{1,0:T(8,128)(2,1)S(1)} %collective-permute-done.9, bf16[1152,768]{0,1:T(8,128)(2,1)} %collective-permute-done), kind=kOutput, calls=%fused_computation.46 | convolution fusion | flops 56647680 | bytes 786432 | tf_op jit(solution)/shard_map/dot_general | solution.py:105
  49.8 1.3 %fusion.16 = bf16[1,128,192]{1,2,0:T(8,128)(2,1)S(1)} fusion(bf16[128,1152]{1,0:T(8,128)(2,1)S(1)} %dynamic-slice_bitcast_fusion.2, bf16[1152,768]{0,1:T(8,128)(2,1)} %collective-permute-done), kind=kOutput, calls=%fused_computation.42 | convolution fusion | flops 56647680 | bytes 786432 | tf_op jit(solution)/shard_map/dot_general | solution.py:105
  51.1 0.6 collective-permute-start.1
  51.7 1.6 %collective-permute-start.7 = (bf16[2,128,192]{1,2,0:T(8,128)(2,1)S(1)}, bf16[2,128,192]{1,2,0:T(8,128)(2,1)S(1)}, u32[]{:S(2)}, u32[]{:S(2)}) collective-permute-start(bf16[2,128,192]{1,2,0:T(8,128)(2,1)S(1)} %add_convert_fusion.2), channel_id=1, source_target_pairs={{0,2},{2,0},{1,3},{3,1},{4,6},{6,4},{5,7},{7,5},{8,10},{10,8},{9,1... | collective-permute-start | bytes 294920 | tf_op jit(solution)/shard_map/ppermute | solution.py:14
  53.3 0.6 collective-permute-start.14
  53.9 1.6 %collective-permute-start.11 = (bf16[2,128,192]{1,2,0:T(8,128)(2,1)S(1)}, bf16[2,128,192]{1,2,0:T(8,128)(2,1)S(1)}, u32[]{:S(2)}, u32[]{:S(2)}) collective-permute-start(bf16[2,128,192]{1,2,0:T(8,128)(2,1)S(1)} %add_convert_fusion.1), channel_id=1, source_target_pairs={{0,2},{2,0},{1,3},{3,1},{4,6},{6,4},{5,7},{7,5},{8,10},{10,8},{9,1... | collective-permute-start | bytes 294920 | tf_op jit(solution)/shard_map/ppermute | solution.py:14
  55.5 0.6 collective-permute-start.2
  56.1 1.2 collective-permute-done.7
  57.4 0.3 fusion.49
  57.7 0.3 fusion.9
  58.0 0.5 collective-permute-start.8
  58.5 0.9 collective-permute-done.14
  59.5 0.3 fusion.43
  59.8 0.3 fusion.11
  60.0 0.7 collective-permute-start.15
  60.8 0.7 collective-permute-done.11
  61.6 0.3 fusion.46
  61.9 9.8 %collective-permute-done.15 = bf16[128,1152]{1,0:T(8,128)(2,1)S(1)} collective-permute-done((bf16[128,1152]{1,0:T(8,128)(2,1)S(1)}, bf16[128,1152]{1,0:T(8,128)(2,1)S(1)}, u32[]{:S(2)}, u32[]{:S(2)}) %collective-permute-start.15) | collective-permute-done | bytes 294944 | tf_op jit(solution)/shard_map/ppermute | solution.py:14
  71.6 0.3 fusion.10
  71.9 0.4 collective-permute-start.16
  72.5 0.3 fusion.40
  72.7 12.7 %collective-permute-done.16 = bf16[128,1152]{1,0:T(8,128)(2,1)S(1)} collective-permute-done((bf16[128,1152]{1,0:T(8,128)(2,1)S(1)}, bf16[128,1152]{1,0:T(8,128)(2,1)S(1)}, u32[]{:S(2)}, u32[]{:S(2)}) %collective-permute-start.16) | collective-permute-done | bytes 294944 | tf_op jit(solution)/shard_map/ppermute | solution.py:14
  85.5 0.4 fusion.8
  85.9 0.3 convolution_bitcast_fusion.7
  86.2 0.9 collective-permute-start.19
  87.1 0.3 convolution_bitcast_fusion.6
  87.4 0.1 fusion.51
  87.5 11.1 %collective-permute-done.18 = bf16[128,1152]{1,0:T(8,128)(2,1)S(1)} collective-permute-done((bf16[128,1152]{1,0:T(8,128)(2,1)S(1)}, bf16[128,1152]{1,0:T(8,128)(2,1)S(1)}, u32[]{:S(2)}, u32[]{:S(2)}) %collective-permute-start.18) | collective-permute-done | bytes 294944 | tf_op jit(solution)/shard_map/ppermute | solution.py:14
  98.7 0.3 convolution_bitcast_fusion.5
  99.0 0.3 convolution_bitcast_fusion.4
  99.3 3.0 %collective-permute-done.19 = bf16[128,1152]{1,0:T(8,128)(2,1)S(1)} collective-permute-done((bf16[128,1152]{1,0:T(8,128)(2,1)S(1)}, bf16[128,1152]{1,0:T(8,128)(2,1)S(1)}, u32[]{:S(2)}, u32[]{:S(2)}) %collective-permute-start.19) | collective-permute-done | bytes 294944 | tf_op jit(solution)/shard_map/ppermute | solution.py:14
  102.2 0.3 convolution_bitcast_fusion.3
  102.7 0.3 convolution_bitcast_fusion.2
  103.0 0.1 fusion.53
  103.2 7.2 %collective-permute-done.20 = bf16[128,1152]{1,0:T(8,128)(2,1)S(1)} collective-permute-done((bf16[128,1152]{1,0:T(8,128)(2,1)S(1)}, bf16[128,1152]{1,0:T(8,128)(2,1)S(1)}, u32[]{:S(2)}, u32[]{:S(2)}) %collective-permute-start.20) | collective-permute-done | bytes 294944 | tf_op jit(solution)/shard_map/ppermute | solution.py:14
  110.4 0.3 convolution_bitcast_fusion.1
  110.7 0.3 convolution_bitcast_fusion
  111.0 0.1 fusion.54
  111.3 1.1 collective-permute-done.21
  112.4 0.8 collective-permute-start.22
  113.2 1.0 maximum_select_fusion
  114.2 1.9 %collective-permute-done.22 = f32[4,192]{1,0:T(4,128)S(1)} collective-permute-done((f32[4,192]{1,0:T(4,128)S(1)}, f32[4,192]{1,0:T(4,128)S(1)}, u32[]{:S(2)}, u32[]{:S(2)}) %collective-permute-start.22) | collective-permute-done | bytes 3104 | tf_op jit(solution)/shard_map/ppermute | solution.py:14
  116.2 0.7 mul.62
  (80 shorter events, 2.9 us)
Async XLA Ops:
  0.6 1.1 copy-start
  1.7 34.1 %collective-permute-start.5 = (bf16[128,1152]{1,0:T(8,128)(2,1)S(1)}, bf16[128,1152]{1,0:T(8,128)(2,1)S(1)}, u32[]{:S(2)}, u32[]{:S(2)}) collective-permute-start(bf16[128,1152]{1,0:T(8,128)(2,1)S(1)} %dynamic-slice_bitcast_fusion.2), channel_id=1, source_target_pairs={{0,4},{4,0},{8,12},{12,8},{1,5},{5,1},{9,13},{13,9},{2,6},{6,2},{1... | collective-permute-start | bytes 884744 | tf_op jit(solution)/shard_map/ppermute | solution.py:14
  4.8 29.2 %collective-permute-start.9 = (bf16[128,1152]{1,0:T(8,128)(2,1)S(1)}, bf16[128,1152]{1,0:T(8,128)(2,1)S(1)}, u32[]{:S(2)}, u32[]{:S(2)}) collective-permute-start(bf16[128,1152]{1,0:T(8,128)(2,1)S(1)} %dynamic-slice_bitcast_fusion.2), channel_id=1, source_target_pairs={{0,8},{4,12},{8,0},{12,4},{1,9},{5,13},{9,1},{13,5},{2,10},{6,14},... | collective-permute-start | bytes 884744 | tf_op jit(solution)/shard_map/ppermute | solution.py:14
  18.4 4.3 %copy-start.3 = (f32[1024]{0:T(1024)S(1)}, f32[1024]{0:T(1024)}, u32[]{:S(2)}) copy-start(f32[1024]{0:T(1024)} %param.9) | copy-start | bytes 12292
  22.5 22.3 %collective-permute-start = (bf16[1152,768]{0,1:T(8,128)(2,1)}, bf16[1152,768]{0,1:T(8,128)(2,1)}, u32[]{:S(2)}, u32[]{:S(2)}) collective-permute-start(bf16[1152,768]{0,1:T(8,128)(2,1)} %get-tuple-element.5), channel_id=1, source_target_pairs={{0,1},{1,0},{2,3},{3,2},{4,5},{5,4},{6,7},{7,6},{8,9},{9,8},{10,11... | collective-permute-start | bytes 5308424 | tf_op jit(solution)/shard_map/ppermute | solution.py:14
  23.0 11.0 %collective-permute-start.3 = (f32[4,192]{1,0:T(4,128)S(1)}, f32[4,192]{1,0:T(4,128)S(1)}, u32[]{:S(2)}, u32[]{:S(2)}) collective-permute-start(f32[4,192]{1,0:T(4,128)S(1)} %reshape.273), channel_id=1, source_target_pairs={{0,1},{1,0},{2,3},{3,2},{4,5},{5,4},{6,7},{7,6},{8,9},{9,8},{10,11... | collective-permute-start | bytes 9224 | tf_op jit(solution)/shard_map/ppermute | solution.py:14
  30.0 2.3 %copy-start.1 = (bf16[768,2304]{1,0:T(8,128)(2,1)}, bf16[768,2304]{1,0:T(8,128)(2,1)S(1)}, u32[]{:S(2)}) copy-start(bf16[768,2304]{1,0:T(8,128)(2,1)S(1)} %convolution_convert_fusion.1) | copy-start | bytes 10616836
  30.0 3.9 %copy-start.4 = (f32[1,2304]{1,0:T(1,128)S(1)}, f32[1,2304]{1,0:T(1,128)}, u32[]{:S(2)}) copy-start(f32[1,2304]{1,0:T(1,128)} %param.11) | copy-start | bytes 27652
  32.3 25.4 %collective-permute-start.4 = (bf16[768,1152]{1,0:T(8,128)(2,1)}, bf16[768,1152]{1,0:T(8,128)(2,1)S(1)}, u32[]{:S(2)}, u32[]{:S(2)}) collective-permute-start(bf16[768,1152]{1,0:T(8,128)(2,1)} %constant_dynamic-slice_fusion), channel_id=1, source_target_pairs={{0,1},{1,0},{2,3},{3,2},{4,5},{5,4},{6,7},{7,6},{8,9},{9,8},{10,11... | collective-permute-start | bytes 5308424 | tf_op jit(solution)/shard_map/ppermute | solution.py:14
  34.0 9.5 %collective-permute-start.12 = (bf16[128,1152]{1,0:T(8,128)(2,1)S(1)}, bf16[128,1152]{1,0:T(8,128)(2,1)S(1)}, u32[]{:S(2)}, u32[]{:S(2)}) collective-permute-start(bf16[128,1152]{1,0:T(8,128)(2,1)S(1)} %collective-permute-done.9), channel_id=1, source_target_pairs={{0,4},{4,0},{8,12},{12,8},{1,5},{5,1},{9,13},{13,9},{2,6},{6,2},{1... | collective-permute-start | bytes 884744 | tf_op jit(solution)/shard_map/ppermute | solution.py:14
  46.1 5.5 %collective-permute-start.6 = (bf16[2,128,192]{1,2,0:T(8,128)(2,1)S(1)}, bf16[2,128,192]{1,2,0:T(8,128)(2,1)S(1)}, u32[]{:S(2)}, u32[]{:S(2)}) collective-permute-start(bf16[2,128,192]{1,2,0:T(8,128)(2,1)S(1)} %pad_maximum_fusion.1), channel_id=1, source_target_pairs={{0,1},{1,0},{2,3},{3,2},{4,5},{5,4},{6,7},{7,6},{8,9},{9,8},{10,11... | collective-permute-start | bytes 294920 | tf_op jit(solution)/shard_map/ppermute | solution.py:14
  47.5 9.9 %copy-start.2 = (bf16[768,2304]{1,0:T(8,128)(2,1)S(1)}, bf16[768,2304]{1,0:T(8,128)(2,1)}, u32[]{:S(2)}) copy-start(bf16[768,2304]{1,0:T(8,128)(2,1)} %copy-done.1) | copy-start | bytes 10616836
  47.5 5.7 %collective-permute-start.13 = (bf16[2,128,192]{1,2,0:T(8,128)(2,1)S(1)}, bf16[2,128,192]{1,2,0:T(8,128)(2,1)S(1)}, u32[]{:S(2)}, u32[]{:S(2)}) collective-permute-start(bf16[2,128,192]{1,2,0:T(8,128)(2,1)S(1)} %pad_maximum_fusion.3), channel_id=1, source_target_pairs={{0,1},{1,0},{2,3},{3,2},{4,5},{5,4},{6,7},{7,6},{8,9},{9,8},{10,11... | collective-permute-start | bytes 294920 | tf_op jit(solution)/shard_map/ppermute | solution.py:14
  49.7 4.2 %collective-permute-start.10 = (bf16[2,128,192]{1,2,0:T(8,128)(2,1)S(1)}, bf16[2,128,192]{1,2,0:T(8,128)(2,1)S(1)}, u32[]{:S(2)}, u32[]{:S(2)}) collective-permute-start(bf16[2,128,192]{1,2,0:T(8,128)(2,1)S(1)} %pad_maximum_fusion.2), channel_id=1, source_target_pairs={{0,1},{1,0},{2,3},{3,2},{4,5},{5,4},{6,7},{7,6},{8,9},{9,8},{10,11... | collective-permute-start | bytes 294920 | tf_op jit(solution)/shard_map/ppermute | solution.py:14
  51.1 4.4 %collective-permute-start.1 = (bf16[2,128,192]{1,2,0:T(8,128)(2,1)S(1)}, bf16[2,128,192]{1,2,0:T(8,128)(2,1)S(1)}, u32[]{:S(2)}, u32[]{:S(2)}) collective-permute-start(bf16[2,128,192]{1,2,0:T(8,128)(2,1)S(1)} %pad_maximum_fusion), channel_id=1, source_target_pairs={{0,1},{1,0},{2,3},{3,2},{4,5},{5,4},{6,7},{7,6},{8,9},{9,8},{10,11... | collective-permute-start | bytes 294920 | tf_op jit(solution)/shard_map/ppermute | solution.py:14
  51.7 5.6 %collective-permute-start.7 = (bf16[2,128,192]{1,2,0:T(8,128)(2,1)S(1)}, bf16[2,128,192]{1,2,0:T(8,128)(2,1)S(1)}, u32[]{:S(2)}, u32[]{:S(2)}) collective-permute-start(bf16[2,128,192]{1,2,0:T(8,128)(2,1)S(1)} %add_convert_fusion.2), channel_id=1, source_target_pairs={{0,2},{2,0},{1,3},{3,1},{4,6},{6,4},{5,7},{7,5},{8,10},{10,8},{9,1... | collective-permute-start | bytes 294920 | tf_op jit(solution)/shard_map/ppermute | solution.py:14
  53.3 6.1 %collective-permute-start.14 = (bf16[2,128,192]{1,2,0:T(8,128)(2,1)S(1)}, bf16[2,128,192]{1,2,0:T(8,128)(2,1)S(1)}, u32[]{:S(2)}, u32[]{:S(2)}) collective-permute-start(bf16[2,128,192]{1,2,0:T(8,128)(2,1)S(1)} %add_convert_fusion), channel_id=1, source_target_pairs={{0,2},{2,0},{1,3},{3,1},{4,6},{6,4},{5,7},{7,5},{8,10},{10,8},{9,1... | collective-permute-start | bytes 294920 | tf_op jit(solution)/shard_map/ppermute | solution.py:14
  53.9 7.6 %collective-permute-start.11 = (bf16[2,128,192]{1,2,0:T(8,128)(2,1)S(1)}, bf16[2,128,192]{1,2,0:T(8,128)(2,1)S(1)}, u32[]{:S(2)}, u32[]{:S(2)}) collective-permute-start(bf16[2,128,192]{1,2,0:T(8,128)(2,1)S(1)} %add_convert_fusion.1), channel_id=1, source_target_pairs={{0,2},{2,0},{1,3},{3,1},{4,6},{6,4},{5,7},{7,5},{8,10},{10,8},{9,1... | collective-permute-start | bytes 294920 | tf_op jit(solution)/shard_map/ppermute | solution.py:14
  55.5 16.8 %collective-permute-start.2 = (bf16[2,128,192]{1,2,0:T(8,128)(2,1)S(1)}, bf16[2,128,192]{1,2,0:T(8,128)(2,1)S(1)}, u32[]{:S(2)}, u32[]{:S(2)}) collective-permute-start(bf16[2,128,192]{1,2,0:T(8,128)(2,1)S(1)} %add_convert_fusion.3), channel_id=1, source_target_pairs={{0,2},{2,0},{1,3},{3,1},{4,6},{6,4},{5,7},{7,5},{8,10},{10,8},{9,1... | collective-permute-start | bytes 294920 | tf_op jit(solution)/shard_map/ppermute | solution.py:14
  58.0 14.8 %collective-permute-start.8 = (bf16[128,1152]{1,0:T(8,128)(2,1)S(1)}, bf16[128,1152]{1,0:T(8,128)(2,1)S(1)}, u32[]{:S(2)}, u32[]{:S(2)}) collective-permute-start(bf16[128,1152]{1,0:T(8,128)(2,1)S(1)} %fusion.9), channel_id=1, source_target_pairs={{0,4},{4,0},{8,12},{12,8},{1,5},{5,1},{9,13},{13,9},{2,6},{6,2},{1... | collective-permute-start | bytes 884744 | tf_op jit(solution)/shard_map/ppermute | solution.py:14
  60.0 11.6 %collective-permute-start.15 = (bf16[128,1152]{1,0:T(8,128)(2,1)S(1)}, bf16[128,1152]{1,0:T(8,128)(2,1)S(1)}, u32[]{:S(2)}, u32[]{:S(2)}) collective-permute-start(bf16[128,1152]{1,0:T(8,128)(2,1)S(1)} %fusion.11), channel_id=1, source_target_pairs={{0,4},{4,0},{8,12},{12,8},{1,5},{5,1},{9,13},{13,9},{2,6},{6,2},{1... | collective-permute-start | bytes 884744 | tf_op jit(solution)/shard_map/ppermute | solution.py:14
  71.9 13.5 %collective-permute-start.16 = (bf16[128,1152]{1,0:T(8,128)(2,1)S(1)}, bf16[128,1152]{1,0:T(8,128)(2,1)S(1)}, u32[]{:S(2)}, u32[]{:S(2)}) collective-permute-start(bf16[128,1152]{1,0:T(8,128)(2,1)S(1)} %fusion.10), channel_id=1, source_target_pairs={{0,8},{4,12},{8,0},{12,4},{1,9},{5,13},{9,1},{13,5},{2,10},{6,14},... | collective-permute-start | bytes 884744 | tf_op jit(solution)/shard_map/ppermute | solution.py:14
  85.8 12.8 %collective-permute-start.18 = (bf16[128,1152]{1,0:T(8,128)(2,1)S(1)}, bf16[128,1152]{1,0:T(8,128)(2,1)S(1)}, u32[]{:S(2)}, u32[]{:S(2)}) collective-permute-start(bf16[128,1152]{1,0:T(8,128)(2,1)S(1)} %fusion.8), channel_id=1, source_target_pairs={{0,4},{4,0},{8,12},{12,8},{1,5},{5,1},{9,13},{13,9},{2,6},{6,2},{1... | collective-permute-start | bytes 884744 | tf_op jit(solution)/shard_map/ppermute | solution.py:14
  86.2 16.0 %collective-permute-start.19 = (bf16[128,1152]{1,0:T(8,128)(2,1)S(1)}, bf16[128,1152]{1,0:T(8,128)(2,1)S(1)}, u32[]{:S(2)}, u32[]{:S(2)}) collective-permute-start(bf16[128,1152]{1,0:T(8,128)(2,1)S(1)} %fusion.8), channel_id=1, source_target_pairs={{0,8},{4,12},{8,0},{12,4},{1,9},{5,13},{9,1},{13,5},{2,10},{6,14},... | collective-permute-start | bytes 884744 | tf_op jit(solution)/shard_map/ppermute | solution.py:14
  87.1 26.1 %collective-permute-start.17 = (bf16[128,1152]{1,0:T(8,128)(2,1)S(1)}, bf16[128,1152]{1,0:T(8,128)(2,1)S(1)}, u32[]{:S(2)}, u32[]{:S(2)}) collective-permute-start(bf16[128,1152]{1,0:T(8,128)(2,1)S(1)} %fusion.8), channel_id=1, source_target_pairs={{0,1},{1,0},{2,3},{3,2},{4,5},{5,4},{6,7},{7,6},{8,9},{9,8},{10,11... | collective-permute-start | bytes 884744 | tf_op jit(solution)/shard_map/ppermute | solution.py:14
  102.5 7.9 %collective-permute-start.20 = (bf16[128,1152]{1,0:T(8,128)(2,1)S(1)}, bf16[128,1152]{1,0:T(8,128)(2,1)S(1)}, u32[]{:S(2)}, u32[]{:S(2)}) collective-permute-start(bf16[128,1152]{1,0:T(8,128)(2,1)S(1)} %collective-permute-done.19), channel_id=1, source_target_pairs={{0,4},{4,0},{8,12},{12,8},{1,5},{5,1},{9,13},{13,9},{2,6},{6,2},{1... | collective-permute-start | bytes 884744 | tf_op jit(solution)/shard_map/ppermute | solution.py:14
  111.2 1.2 %collective-permute-start.21 = (f32[4,192]{1,0:T(4,128)S(1)}, f32[4,192]{1,0:T(4,128)S(1)}, u32[]{:S(2)}, u32[]{:S(2)}) collective-permute-start(f32[4,192]{1,0:T(4,128)S(1)} %slice_bitcast_fusion.16), channel_id=1, source_target_pairs={{0,1},{1,0},{2,3},{3,2},{4,5},{5,4},{6,7},{7,6},{8,9},{9,8},{10,11... | collective-permute-start | bytes 9224 | tf_op jit(solution)/shard_map/ppermute | solution.py:14
  112.4 3.6 %collective-permute-start.22 = (f32[4,192]{1,0:T(4,128)S(1)}, f32[4,192]{1,0:T(4,128)S(1)}, u32[]{:S(2)}, u32[]{:S(2)}) collective-permute-start(f32[4,192]{1,0:T(4,128)S(1)} %fusion.56), channel_id=1, source_target_pairs={{0,2},{2,0},{1,3},{3,1},{4,6},{6,4},{5,7},{7,5},{8,10},{10,8},{9,1... | collective-permute-start | bytes 9224 | tf_op jit(solution)/shard_map/ppermute | solution.py:14

commit v2 on v1

v2 whole, which is shorter than its diff:
```python
import jax
import jax.numpy as jnp
from jax import lax
from jax.experimental import pallas as pl
from jax.experimental.pallas import tpu as pltpu
from jax.sharding import PartitionSpec as P

LATBLK = 64
TBLK = 128
CAP = 3
SLOT = CAP * LATBLK


def swap(value, axis, mask):
    size = lax.axis_size(axis)
    return lax.ppermute(value, axis, [(i, i ^ mask) for i in range(size)])


def masks_of(axis):
    size = lax.axis_size(axis)
    return [1 << i for i in range(size.bit_length() - 1)]


def spread(value):
    have = {0: value}
    for mask in reversed(masks_of("lat")):
        for offset in list(have):
            have[offset ^ mask] = swap(have[offset], "lat", mask)
    return have


def collect(parts):
    held = dict(parts)
    for mask in masks_of("lat"):
        for offset in sorted(held):
            if offset & mask:
                arrived = swap(held.pop(offset).astype(jnp.bfloat16), "lat", mask)
                held[offset ^ mask] = held[offset ^ mask] + arrived.astype(jnp.float32)
    return held[0]


def sum_layers(value):
    for mask in masks_of("layer"):
        total = value.astype(jnp.float32) + swap(value, "layer", mask).astype(jnp.float32)
        value = total.astype(value.dtype)
    return total


def selected(w_enc, w_dec, pick, half_at):
    width, latents = w_enc.shape
    half = width // 2
    blocks = pick.shape[0] // CAP

    def body(pick_ref, half_ref, *refs):
        enc_refs, dec_refs, out_ref = refs[:CAP], refs[CAP : 2 * CAP], refs[2 * CAP]
        step = pl.program_id(0)
        row = lax.broadcasted_iota(jnp.int32, (LATBLK, 2 * LATBLK), 0)
        lane = lax.broadcasted_iota(jnp.int32, (LATBLK, 2 * LATBLK), 1)
        for s in range(CAP):
            odd = lax.rem(pick_ref[step * CAP + s], 2)
            choose = (lane == row + odd * LATBLK).astype(jnp.bfloat16)
            rows = slice(s * LATBLK, (s + 1) * LATBLK)
            out_ref[0, rows, :] = lax.dot_general(
                choose, enc_refs[s][...], (((1,), (1,)), ((), ())),
                preferred_element_type=jnp.float32,
            ).astype(jnp.bfloat16)
            out_ref[1, rows, :] = dec_refs[s][...]

    def enc_spec(s):
        return pl.BlockSpec(
            (half, 2 * LATBLK), lambda i, p, h: (h[0], lax.div(p[i * CAP + s], 2))
        )

    def dec_spec(s):
        return pl.BlockSpec((LATBLK, half), lambda i, p, h: (p[i * CAP + s], h[0]))

    return pl.pallas_call(
        body,
        grid_spec=pltpu.PrefetchScalarGridSpec(
            num_scalar_prefetch=2,
            grid=(blocks,),
            in_specs=[enc_spec(s) for s in range(CAP)] + [dec_spec(s) for s in range(CAP)],
            out_specs=pl.BlockSpec((2, SLOT, half), lambda i, p, h: (0, i, 0)),
        ),
        out_shape=jax.ShapeDtypeStruct((2, blocks * SLOT, half), jnp.bfloat16),
        compiler_params=pltpu.CompilerParams(vmem_limit_bytes=24 * 1024 * 1024),
        cost_estimate=pl.CostEstimate(
            flops=blocks * CAP * 2 * LATBLK * 2 * LATBLK * half,
            bytes_accessed=blocks * SLOT * half * 10,
            transcendentals=0,
        ),
    )(pick, half_at, *([w_enc] * CAP), *([w_dec] * CAP))


ROW_PARTS = 1


def on_device(tokens, w_enc, b_enc, w_dec, b_dec, block_ids, counts):
    own_rows, layers_here, width = tokens.shape
    assert own_rows == TBLK and layers_here == 1
    latents_here = w_enc.shape[2]
    device_blocks = latents_here // LATBLK
    slot_total = block_ids.shape[1]
    half = width // 2
    lat_size = lax.axis_size("lat")
    place = lax.axis_index("lat")
    core = lax.axis_index("tok")
    cycle_place = place * lax.axis_size("tok") + core
    bf16, f32 = jnp.bfloat16, jnp.float32

    def cut(value, axis, which):
        return lax.dynamic_slice_in_dim(value, which * half, half, axis)

    own_half = cut(tokens.reshape(own_rows, width), 1, core)
    rows = own_rows // ROW_PARTS
    own_parts = [own_half[r * rows : (r + 1) * rows] for r in range(ROW_PARTS)]
    token_blocks = [spread(part) for part in own_parts]

    order = place ^ jnp.arange(lat_size, dtype=jnp.int32)
    owner = order[:, None] == jnp.arange(lat_size, dtype=jnp.int32)[None, :]
    ids = jnp.sum(jnp.where(owner[:, :, None], block_ids[None], 0), axis=1)
    live_count = jnp.sum(jnp.where(owner, counts[None], 0), axis=1)
    live = jnp.arange(slot_total, dtype=jnp.int32)[None, :] < live_count[:, None]
    mine = live & (ids // device_blocks == cycle_place)
    position = jnp.cumsum(mine.astype(jnp.int32), axis=1) - 1
    select = mine[:, :, None] & (
        position[:, :, None] == jnp.arange(CAP, dtype=jnp.int32)[None, None, :]
    )
    pick = jnp.sum(select.astype(jnp.int32) * (ids % device_blocks + 1)[:, :, None], axis=1) - 1
    onehot = pick[:, :, None] == jnp.arange(device_blocks, dtype=jnp.int32)[None, None, :]
    bias_pick = jnp.sum(
        jnp.where(onehot[:, :, :, None], b_enc.reshape(1, 1, device_blocks, LATBLK), 0.0), axis=2
    )
    bias_own = jnp.where(pick[:, :, None] < 0, -jnp.inf, bias_pick).reshape(lat_size, SLOT)

    pick_flat = jnp.maximum(pick, 0).reshape(lat_size * CAP)
    sent = selected(w_enc[0], w_dec[0], pick_flat, jnp.full((1,), 1 - core, jnp.int32))
    held = selected(w_enc[0], w_dec[0], pick_flat, jnp.full((1,), core, jnp.int32))
    weights = (held, swap(sent, "tok", 1))
    bias_two = jnp.stack([bias_own, swap(bias_own, "tok", 1)])

    def slot(offset):
        return slice(offset * SLOT, (offset + 1) * SLOT)

    def times_rows(block, w):
        return lax.dot_general(
            block, w, (((1,), (1,)), ((), ())), preferred_element_type=f32
        )

    def forward(r):
        codes, parts = {}, {}
        for group in (range(lat_size - 1), range(lat_size - 1, lat_size)):
            part = jnp.stack(
                [
                    jnp.stack([times_rows(token_blocks[r][o], w[0, slot(o)]) for o in group])
                    for w in weights
                ]
            ).astype(bf16)
            other = swap(part, "tok", 1)
            both = (part.astype(f32) + other[::-1].astype(f32)).astype(bf16)
            pre = sum_layers(both) + bias_two[:, group.start : group.stop, None, :]
            code = jnp.maximum(pre, 0.0).astype(bf16)
            for at, o in enumerate(group):
                codes[o] = code[:, at]
                parts[o] = sum(
                    jnp.dot(code[i, at], weights[i][1, slot(o)], preferred_element_type=f32)
                    for i in range(2)
                )
        return codes, parts

    bias_dec = cut(b_dec, 1, core)
    codes, halves = [], []
    for r in range(ROW_PARTS):
        code, parts = forward(r)
        codes.append(code)
        recon = collect(parts) + bias_dec
        halves.append((recon - own_parts[r].astype(f32)).astype(bf16))

    contrib = 0.0
    for r in range(ROW_PARTS):
        error_blocks = spread(halves[r])
        contrib = contrib + jnp.stack(
            [
                jnp.stack(
                    [
                        jnp.sum(
                            codes[r][o][i].astype(f32)
                            * times_rows(error_blocks[o], weights[i][1, slot(o)]),
                            axis=0,
                        )
                        for o in range(lat_size)
                    ]
                )
                for i in range(2)
            ]
        )
    contrib = sum_layers(contrib[0] + swap(contrib[1], "tok", 1))
    scale_grad = jnp.sum(
        jnp.where(onehot[:, :, :, None], contrib.reshape(lat_size, CAP, 1, LATBLK), 0.0),
        axis=(0, 1),
    ) * (1.0 / TBLK)

    residual_half = jnp.concatenate(halves, axis=0)
    residual_other = swap(residual_half, "tok", 1)
    residual = jnp.where(
        core == 0,
        jnp.concatenate([residual_half, residual_other], axis=1),
        jnp.concatenate([residual_other, residual_half], axis=1),
    )
    return residual.reshape(tokens.shape), scale_grad.reshape(latents_here)


def solution(mesh):
    in_specs = (
        P(("groups", "lat"), "layer", None),
        P("layer", None, ("lat", "tok")),
        P(("lat", "tok")),
        P("layer", ("lat", "tok"), None),
        P("layer", None),
        P("groups", None),
        P("groups"),
    )
    out_specs = (P(("groups", "lat"), "layer", None), P(("groups", "lat", "tok")))
    return jax.shard_map(
        on_device, mesh=mesh, in_specs=in_specs, out_specs=out_specs, check_vma=False
    )
```

time: 117 us -> 117 us (level); the launches traced: 117 us -> 115 us
  waiting for transfers between devices: 56 us -> 38.6 us
  Pallas kernels: 0 us -> 8.81 us
  starting transfers between devices: 15.9 us -> 19.5 us
  matrix products: 29.2 us -> 30.7 us
    ppermute x23 -> x18, waiting for transfers between devices: 56 us -> 38.6 us  [swap(): return lax.ppermute(value, axis, [(i, i ^ mask) for i in range(size)])]
    unnamed x10 -> x17, local copies, waits for them, and re-layouts: 1.81 us -> 11.1 us
    pallas_call x0 -> x2, Pallas kernels: none -> 8.81 us  [selected(): pl.pallas_call(body, grid_spec=pltpu.PrefetchScalarGridSpec(num_scalar_pr...]
    dynamic_slice x4 -> x2, local copies, waits for them, and re-layouts: 5.66 us -> 0.05 us  [cut(): return lax.dynamic_slice_in_dim(value, which * half, half, axis)]
    ppermute x23 -> x18, starting transfers between devices: 15.9 us -> 19.5 us  [swap(): return lax.ppermute(value, axis, [(i, i ^ mask) for i in range(size)])]
    gather x2 -> x0, local copies, waits for them, and re-layouts: 2.54 us -> none  [the longest x1 1.3 us: on_device(): jnp.take(counts, order)[:, None]]
    dot_general x26 -> x24, matrix products: 29.2 us -> 30.7 us  [the longest x16 20.4 us: times_rows(): lax.dot_general(block, w, (((1,), (1,)), ((), ())), preferred_element_typ...]
  transfers between devices with their start and end apart: 23 -> 18, of which waited for: 11 -> 10; matrix products, arithmetic and copies ran while one was open for 35% -> 25% of each run, Pallas kernels for 0% -> 3%
where the time goes in v2:
time: 117 us; the launch traced here: 115 us
  waiting for transfers between devices  38.6 us (33%)
  matrix products  30.7 us (26%)
  starting transfers between devices  19.5 us (17%)
  local copies, waits for them, and re-layouts  12.5 us (11%)
  Pallas kernels  8.81 us (8%)
  other arithmetic  4.08 us (3%)
    ppermute x18, waiting for transfers between devices, swap(): return lax.ppermute(value, axis, [(i, i ^ mask) for i in range(size)])  38.6 us
    dot_general x16, matrix products, times_rows(): lax.dot_general(block, w, (((1,), (1,)), ((), ())), preferred_element_typ...  20.4 us
    ppermute x18, starting transfers between devices, swap(): return lax.ppermute(value, axis, [(i, i ^ mask) for i in range(size)])  19.5 us
    unnamed x17, local copies, waits for them, and re-layouts  11.1 us
    dot_general x8, matrix products, forward(): jnp.dot(code[i, at], weights[i][1, slot(o)], preferred_element_type=f32)  10.3 us
    pallas_call x2, Pallas kernels, selected(): pl.pallas_call(body, grid_spec=pltpu.PrefetchScalarGridSpec(num_scalar_pr...  8.81 us
  transfers between devices with their start and end apart: 18, of which 10 were waited for; matrix products, arithmetic and copies ran while one was open for 25% of the time, Pallas kernels for 3%

profile of v2, /device:TPU:0, one launch (start us, length us, event | category | flops | bytes accessed | tf_op | source)
XLA Modules:
  0.0 115.2 jit_solution(17794871693368206709)
XLA Ops:
  0.7 0.8 select_reduce_fusion.2
  1.6 0.8 select_reduce_fusion.4
  2.5 0.2 reduce_window_sum.11
  2.7 0.1 select_reduce_fusion.3
  3.0 2.3 %copy-done.1 = bf16[1,2304,1024]{2,1,0:T(8,128)(2,1)S(1)} copy-done((bf16[1,2304,1024]{2,1,0:T(8,128)(2,1)S(1)}, bf16[1,2304,1024]{2,1,0:T(8,128)(2,1)}, u32[]{:S(2)}) %copy-start.1) | copy-done | bytes 4718616
  5.4 2.3 %copy-done.3 = bf16[1,1024,2304]{2,1,0:T(8,128)(2,1)S(1)} copy-done((bf16[1,1024,2304]{2,1,0:T(8,128)(2,1)S(1)}, bf16[1,1024,2304]{2,1,0:T(8,128)(2,1)}, u32[]{:S(2)}) %copy-start.3) | copy-done | bytes 4718616
  7.7 4.9 %shard_map.87 = bf16[2,768,1152]{2,1,0:T(8,128)(2,1)} custom-call(s32[12]{0:T(128)S(1)} %max.20.pick_ref, s32[1]{0:T(128)} %bitcast.11.half_ref, bf16[2304,1024]{1,0:T(8,128)(2,1)S(1)} %bitcast.152, bf16[2304,1024]{1,0:T(8,128)(2,1)S(1)} %bitcast.153, bf16[2304,1024]{1,0:T(8,128)(2,1)S(1)} %bitcast.154, bf16[1024,2304]{1,0:T(8,128)(2,1)S(1)} %bitcast.158, ...), custom_call_target="tpu_custom_call" | custom-call | flops 226492416 | bytes 8847360 | tf_op jit(solution)/shard_map/pallas_call | solution.py:77
  12.6 4.1 %collective-permute-start.1 = (bf16[128,1152]{1,0:T(8,128)(2,1)S(1)}, bf16[128,1152]{1,0:T(8,128)(2,1)S(1)}, u32[]{:S(2)}, u32[]{:S(2)}) collective-permute-start(bf16[128,1152]{1,0:T(8,128)(2,1)S(1)} %dynamic-slice_bitcast_fusion), channel_id=1, source_target_pairs={{0,8},{4,12},{8,0},{12,4},{1,9},{5,13},{9,1},{13,5},{2,10},{6,14},... | collective-permute-start | bytes 884744 | tf_op jit(solution)/shard_map/ppermute | solution.py:16
  16.7 1.6 %collective-permute-start = (bf16[128,1152]{1,0:T(8,128)(2,1)S(1)}, bf16[128,1152]{1,0:T(8,128)(2,1)S(1)}, u32[]{:S(2)}, u32[]{:S(2)}) collective-permute-start(bf16[128,1152]{1,0:T(8,128)(2,1)S(1)} %dynamic-slice_bitcast_fusion), channel_id=1, source_target_pairs={{0,4},{4,0},{8,12},{12,8},{1,5},{5,1},{9,13},{13,9},{2,6},{6,2},{1... | collective-permute-start | bytes 884744 | tf_op jit(solution)/shard_map/ppermute | solution.py:16
  18.4 0.1 copy.10
  18.6 0.1 select_reduce_fusion.1
  18.9 2.3 %copy-done.2 = bf16[1,2304,1024]{2,1,0:T(8,128)(2,1)S(1)} copy-done((bf16[1,2304,1024]{2,1,0:T(8,128)(2,1)S(1)}, bf16[1,2304,1024]{2,1,0:T(8,128)(2,1)}, u32[]{:S(2)}) %copy-start.2) | copy-done | bytes 4718616
  21.3 2.3 %copy-done.4 = bf16[1,1024,2304]{2,1,0:T(8,128)(2,1)S(1)} copy-done((bf16[1,1024,2304]{2,1,0:T(8,128)(2,1)S(1)}, bf16[1,1024,2304]{2,1,0:T(8,128)(2,1)}, u32[]{:S(2)}) %copy-start.4) | copy-done | bytes 4718616
  23.6 4.0 %shard_map.86 = bf16[2,768,1152]{2,1,0:T(8,128)(2,1)S(1)} custom-call(s32[12]{0:T(128)S(1)} %max.20.pick_ref, s32[1]{0:T(128)} %bitcast.1.half_ref, bf16[2304,1024]{1,0:T(8,128)(2,1)S(1)} %bitcast.155, bf16[2304,1024]{1,0:T(8,128)(2,1)S(1)} %bitcast.156, bf16[2304,1024]{1,0:T(8,128)(2,1)S(1)} %bitcast.157, bf16[1024,2304]{1,0:T(8,128)(2,1)S(1)} %bitcast.161, ...), custom_call_target="tpu_custom_call" | custom-call | flops 226492416 | bytes 8847360 | tf_op jit(solution)/shard_map/pallas_call | solution.py:77
  27.6 1.7 %copy-done.5 = bf16[2,768,1152]{2,1,0:T(8,128)(2,1)} copy-done((bf16[2,768,1152]{2,1,0:T(8,128)(2,1)}, bf16[2,768,1152]{2,1,0:T(8,128)(2,1)S(1)}, u32[]{:S(2)}) %copy-start.5) | copy-done | bytes 3538968
  29.3 0.3 fusion.17
  29.7 1.1 collective-permute-done.1
  30.8 0.6 collective-permute-start.7
  31.4 1.3 %fusion.19 = bf16[1,128,192]{1,2,0:T(8,128)(2,1)S(1)} fusion(bf16[128,1152]{1,0:T(8,128)(2,1)S(1)} %collective-permute-done.1, bf16[2,768,1152]{2,1,0:T(8,128)(2,1)} %copy-done.5), kind=kOutput, calls=%fused_computation.39 | convolution fusion | flops 56647680 | bytes 786432 | tf_op jit(solution)/shard_map/dot_general | solution.py:146
  32.8 1.3 %fusion.18 = bf16[1,128,192]{1,2,0:T(8,128)(2,1)S(1)} fusion(bf16[128,1152]{1,0:T(8,128)(2,1)S(1)} %collective-permute-done, bf16[2,768,1152]{2,1,0:T(8,128)(2,1)} %copy-done.5), kind=kOutput, calls=%fused_computation.38 | convolution fusion | flops 56647680 | bytes 786432 | tf_op jit(solution)/shard_map/dot_general | solution.py:146
  34.1 5.5 %collective-permute-done.7 = bf16[128,1152]{1,0:T(8,128)(2,1)S(1)} collective-permute-done((bf16[128,1152]{1,0:T(8,128)(2,1)S(1)}, bf16[128,1152]{1,0:T(8,128)(2,1)S(1)}, u32[]{:S(2)}, u32[]{:S(2)}) %collective-permute-start.7) | collective-permute-done | bytes 294944 | tf_op jit(solution)/shard_map/ppermute | solution.py:16
  39.6 1.3 %fusion.23 = bf16[1,1,128,192]{2,3,1,0:T(8,128)(2,1)S(1)} fusion(bf16[128,1152]{1,0:T(8,128)(2,1)S(1)} %collective-permute-done.7, bf16[2,768,1152]{2,1,0:T(8,128)(2,1)} %copy-done.5), kind=kOutput, calls=%fused_computation.43 | convolution fusion | flops 56647680 | bytes 786432 | tf_op jit(solution)/shard_map/dot_general | solution.py:146
  40.9 1.3 %fusion.24 = bf16[1,1,128,192]{2,3,1,0:T(8,128)(2,1)S(1)} fusion(bf16[128,1152]{1,0:T(8,128)(2,1)S(1)} %collective-permute-done.7, bf16[2,768,1152]{2,1,0:T(8,128)(2,1)} %collective-permute-done.2), kind=kOutput, calls=%fused_computation.44 | convolution fusion | flops 56647680 | bytes 786432 | tf_op jit(solution)/shard_map/dot_general | solution.py:146
  42.3 1.3 %fusion.22 = bf16[1,128,192]{1,2,0:T(8,128)(2,1)S(1)} fusion(bf16[128,1152]{1,0:T(8,128)(2,1)S(1)} %collective-permute-done.1, bf16[2,768,1152]{2,1,0:T(8,128)(2,1)} %collective-permute-done.2), kind=kOutput, calls=%fused_computation.42 | convolution fusion | flops 56647680 | bytes 786432 | tf_op jit(solution)/shard_map/dot_general | solution.py:146
  43.6 1.3 %fusion.21 = bf16[1,128,192]{1,2,0:T(8,128)(2,1)S(1)} fusion(bf16[128,1152]{1,0:T(8,128)(2,1)S(1)} %collective-permute-done, bf16[2,768,1152]{2,1,0:T(8,128)(2,1)} %collective-permute-done.2), kind=kOutput, calls=%fused_computation.41 | convolution fusion | flops 56647680 | bytes 786432 | tf_op jit(solution)/shard_map/dot_general | solution.py:146
  44.9 1.3 %fusion.20 = bf16[1,128,192]{1,2,0:T(8,128)(2,1)S(1)} fusion(bf16[128,1152]{1,0:T(8,128)(2,1)S(1)} %dynamic-slice_bitcast_fusion, bf16[2,768,1152]{2,1,0:T(8,128)(2,1)} %collective-permute-done.2), kind=kOutput, calls=%fused_computation.40 | convolution fusion | flops 56647680 | bytes 786432 | tf_op jit(solution)/shard_map/dot_general | solution.py:146
  46.2 0.6 collective-permute-start.3
  46.8 1.4 %collective-permute-start.9 = (bf16[2,1,128,192]{2,3,1,0:T(8,128)(2,1)S(1)}, bf16[2,1,128,192]{2,3,1,0:T(8,128)(2,1)S(1)}, u32[]{:S(2)}, u32[]{:S(2)}) collective-permute-start(bf16[2,1,128,192]{2,3,1,0:T(8,128)(2,1)S(1)} %add_convert_fusion.1), channel_id=1, source_target_pairs={{0,2},{2,0},{1,3},{3,1},{4,6},{6,4},{5,7},{7,5},{8,10},{10,8},{9,1... | collective-permute-start | bytes 294920 | tf_op jit(solution)/shard_map/ppermute | solution.py:16
  48.3 3.4 %collective-permute-done.9 = bf16[2,1,128,192]{2,3,1,0:T(8,128)(2,1)S(1)} collective-permute-done((bf16[2,1,128,192]{2,3,1,0:T(8,128)(2,1)S(1)}, bf16[2,1,128,192]{2,3,1,0:T(8,128)(2,1)S(1)}, u32[]{:S(2)}, u32[]{:S(2)}) %collective-permute-start.9) | collective-permute-done | bytes 98336 | tf_op jit(solution)/shard_map/ppermute | solution.py:16
  51.6 0.1 maximum_convert_fusion.1
  51.9 1.4 %collective-permute-start.4 = (bf16[2,3,128,192]{2,3,1,0:T(8,128)(2,1)S(1)}, bf16[2,3,128,192]{2,3,1,0:T(8,128)(2,1)S(1)}, u32[]{:S(2)}, u32[]{:S(2)}) collective-permute-start(bf16[2,3,128,192]{2,3,1,0:T(8,128)(2,1)S(1)} %add_convert_fusion), channel_id=1, source_target_pairs={{0,2},{2,0},{1,3},{3,1},{4,6},{6,4},{5,7},{7,5},{8,10},{10,8},{9,1... | collective-permute-start | bytes 884744 | tf_op jit(solution)/shard_map/ppermute | solution.py:16
  53.3 1.3 %fusion.28 = f32[128,1152]{1,0:T(8,128)S(1)} fusion(bf16[2,768,1152]{2,1,0:T(8,128)(2,1)} %copy-done.5, bf16[2,1,128,192]{2,3,1,0:T(8,128)(2,1)S(1)} %maximum_convert_fusion.1), kind=kOutput, calls=%fused_computation.67 | convolution fusion | flops 56623104 | bytes 1081344 | tf_op jit(solution)/shard_map/dot_general | solution.py:166
  54.5 1.3 %fusion.8 = bf16[128,1152]{1,0:T(8,128)(2,1)S(1)} fusion(f32[128,1152]{1,0:T(8,128)S(1)} %fusion.28, bf16[2,768,1152]{2,1,0:T(8,128)(2,1)} %collective-permute-done.2, bf16[2,1,128,192]{2,3,1,0:T(8,128)(2,1)S(1)} %maximum_convert_fusion.1), kind=kOutput, calls=%fused_computation.12 | convolution fusion | flops 56918016 | bytes 1376256 | tf_op jit(solution)/shard_map/dot_general | solution.py:166
  55.8 1.0 collective-permute-start.10
  56.9 3.1 %collective-permute-done.4 = bf16[2,3,128,192]{2,3,1,0:T(8,128)(2,1)S(1)} collective-permute-done((bf16[2,3,128,192]{2,3,1,0:T(8,128)(2,1)S(1)}, bf16[2,3,128,192]{2,3,1,0:T(8,128)(2,1)S(1)}, u32[]{:S(2)}, u32[]{:S(2)}) %collective-permute-start.4) | collective-permute-done | bytes 294944 | tf_op jit(solution)/shard_map/ppermute | solution.py:16
  60.0 0.2 maximum_convert_fusion
  60.2 1.3 %fusion.27 = f32[128,1152]{1,0:T(8,128)S(1)} fusion(bf16[2,768,1152]{2,1,0:T(8,128)(2,1)} %copy-done.5, bf16[2,3,128,192]{2,3,1,0:T(8,128)(2,1)S(1)} %maximum_convert_fusion), kind=kOutput, calls=%fused_computation.66 | convolution fusion | flops 56623104 | bytes 1081344 | tf_op jit(solution)/shard_map/dot_general | solution.py:166
  61.5 1.3 %fusion.26 = f32[128,1152]{1,0:T(8,128)S(1)} fusion(bf16[2,768,1152]{2,1,0:T(8,128)(2,1)} %copy-done.5, bf16[2,3,128,192]{2,3,1,0:T(8,128)(2,1)S(1)} %maximum_convert_fusion), kind=kOutput, calls=%fused_computation.65 | convolution fusion | flops 56623104 | bytes 1081344 | tf_op jit(solution)/shard_map/dot_general | solution.py:166
  62.8 0.9 collective-permute-done.10
  63.7 1.3 %fusion.7 = bf16[128,1152]{1,0:T(8,128)(2,1)S(1)} fusion(f32[128,1152]{1,0:T(8,128)S(1)} %fusion.27, bf16[128,1152]{1,0:T(8,128)(2,1)S(1)} %collective-permute-done.10, bf16[2,768,1152]{2,1,0:T(8,128)(2,1)} %collective-permute-done.2, bf16[2,3,128,192]{2,3,1,0:T(8,128)(2,1)S(1)} %maximum_convert_fusion), kind=kOutput, calls=%fused_computation.11 | convolution fusion | flops 57212928 | bytes 1671168 | tf_op jit(solution)/shard_map/dot_general | solution.py:166
  65.0 2.7 %collective-permute-start.11 = (bf16[128,1152]{1,0:T(8,128)(2,1)S(1)}, bf16[128,1152]{1,0:T(8,128)(2,1)S(1)}, u32[]{:S(2)}, u32[]{:S(2)}) collective-permute-start(bf16[128,1152]{1,0:T(8,128)(2,1)S(1)} %fusion.7), channel_id=1, source_target_pairs={{0,8},{4,12},{8,0},{12,4},{1,9},{5,13},{9,1},{13,5},{2,10},{6,14},... | collective-permute-start | bytes 884744 | tf_op jit(solution)/shard_map/ppermute | solution.py:16
  67.7 1.3 %fusion.6 = bf16[128,1152]{1,0:T(8,128)(2,1)S(1)} fusion(f32[128,1152]{1,0:T(8,128)S(1)} %fusion.26, bf16[2,768,1152]{2,1,0:T(8,128)(2,1)} %collective-permute-done.2, bf16[2,3,128,192]{2,3,1,0:T(8,128)(2,1)S(1)} %maximum_convert_fusion), kind=kOutput, calls=%fused_computation.10 | convolution fusion | flops 56918016 | bytes 1376256 | tf_op jit(solution)/shard_map/dot_general | solution.py:166
  69.0 1.8 %collective-permute-start.6 = (bf16[128,1152]{1,0:T(8,128)(2,1)S(1)}, bf16[128,1152]{1,0:T(8,128)(2,1)S(1)}, u32[]{:S(2)}, u32[]{:S(2)}) collective-permute-start(bf16[128,1152]{1,0:T(8,128)(2,1)S(1)} %fusion.6), channel_id=1, source_target_pairs={{0,4},{4,0},{8,12},{12,8},{1,5},{5,1},{9,13},{13,9},{2,6},{6,2},{1... | collective-permute-start | bytes 884744 | tf_op jit(solution)/shard_map/ppermute | solution.py:16
  70.8 1.3 %fusion.25 = f32[128,1152]{1,0:T(8,128)S(1)} fusion(bf16[2,768,1152]{2,1,0:T(8,128)(2,1)} %copy-done.5, bf16[2,3,128,192]{2,3,1,0:T(8,128)(2,1)S(1)} %maximum_convert_fusion), kind=kOutput, calls=%fused_computation.64 | convolution fusion | flops 56623104 | bytes 1081344 | tf_op jit(solution)/shard_map/dot_general | solution.py:166
  72.1 7.2 %collective-permute-done.11 = bf16[128,1152]{1,0:T(8,128)(2,1)S(1)} collective-permute-done((bf16[128,1152]{1,0:T(8,128)(2,1)S(1)}, bf16[128,1152]{1,0:T(8,128)(2,1)S(1)}, u32[]{:S(2)}, u32[]{:S(2)}) %collective-permute-start.11) | collective-permute-done | bytes 294944 | tf_op jit(solution)/shard_map/ppermute | solution.py:16
  79.3 1.4 %collective-permute-done.6 = bf16[128,1152]{1,0:T(8,128)(2,1)S(1)} collective-permute-done((bf16[128,1152]{1,0:T(8,128)(2,1)S(1)}, bf16[128,1152]{1,0:T(8,128)(2,1)S(1)}, u32[]{:S(2)}, u32[]{:S(2)}) %collective-permute-start.6) | collective-permute-done | bytes 294944 | tf_op jit(solution)/shard_map/ppermute | solution.py:16
  80.7 1.4 %fusion.5 = bf16[128,1152]{1,0:T(8,128)(2,1)S(1)} fusion(f32[128,1152]{1,0:T(8,128)S(1)} %fusion.25, bf16[128,1152]{1,0:T(8,128)(2,1)S(1)} %dynamic-slice_bitcast_fusion, bf16[128,1152]{1,0:T(8,128)(2,1)S(1)} %collective-permute-done.11, bf16[128,1152]{1,0:T(8,128)(2,1)S(1)} %collective-permute-done.6, bf16[2,768,1152]{2,1,0:T(8,128)(2,1)} %collective-permute-done.2, ...), kind=kOutput, calls=%fused_computation.9 | convolution fusion | flops 57950208 | bytes 2269184 | tf_op jit(solution)/shard_map/dot_general | solution.py:166
  82.2 0.9 collective-permute-start.14
  83.0 2.4 %collective-permute-start.13 = (bf16[128,1152]{1,0:T(8,128)(2,1)S(1)}, bf16[128,1152]{1,0:T(8,128)(2,1)S(1)}, u32[]{:S(2)}, u32[]{:S(2)}) collective-permute-start(bf16[128,1152]{1,0:T(8,128)(2,1)S(1)} %fusion.5), channel_id=1, source_target_pairs={{0,4},{4,0},{8,12},{12,8},{1,5},{5,1},{9,13},{13,9},{2,6},{6,2},{1... | collective-permute-start | bytes 884744 | tf_op jit(solution)/shard_map/ppermute | solution.py:16
  85.5 1.4 %fusion.9 = f32[192]{0:T(256)S(1)} fusion(bf16[128,1152]{1,0:T(8,128)(2,1)S(1)} %fusion.5, bf16[2,768,1152]{2,1,0:T(8,128)(2,1)} %copy-done.5, bf16[2,3,128,192]{2,3,1,0:T(8,128)(2,1)S(1)} %maximum_convert_fusion), kind=kOutput, calls=%fused_computation.29 | convolution fusion | flops 56696640 | bytes 787200 | tf_op jit(solution)/shard_map/dot_general | solution.py:146
  86.9 1.4 %fusion.13 = f32[192]{0:T(256)S(1)} fusion(bf16[128,1152]{1,0:T(8,128)(2,1)S(1)} %fusion.5, bf16[2,768,1152]{2,1,0:T(8,128)(2,1)} %collective-permute-done.2, bf16[2,3,128,192]{2,3,1,0:T(8,128)(2,1)S(1)} %maximum_convert_fusion), kind=kOutput, calls=%fused_computation.33 | convolution fusion | flops 56696640 | bytes 787200 | tf_op jit(solution)/shard_map/dot_general | solution.py:146
  88.2 10.7 %collective-permute-done.14 = bf16[128,1152]{1,0:T(8,128)(2,1)S(1)} collective-permute-done((bf16[128,1152]{1,0:T(8,128)(2,1)S(1)}, bf16[128,1152]{1,0:T(8,128)(2,1)S(1)}, u32[]{:S(2)}, u32[]{:S(2)}) %collective-permute-start.14) | collective-permute-done | bytes 294944 | tf_op jit(solution)/shard_map/ppermute | solution.py:16
  98.9 1.4 %fusion.15 = f32[192]{0:T(256)S(1)} fusion(bf16[128,1152]{1,0:T(8,128)(2,1)S(1)} %collective-permute-done.14, bf16[2,768,1152]{2,1,0:T(8,128)(2,1)} %collective-permute-done.2, bf16[2,3,128,192]{2,3,1,0:T(8,128)(2,1)S(1)} %maximum_convert_fusion), kind=kOutput, calls=%fused_computation.35 | convolution fusion | flops 56696640 | bytes 787200 | tf_op jit(solution)/shard_map/dot_general | solution.py:146
  100.3 1.4 %fusion.11 = f32[192]{0:T(256)S(1)} fusion(bf16[128,1152]{1,0:T(8,128)(2,1)S(1)} %collective-permute-done.14, bf16[2,768,1152]{2,1,0:T(8,128)(2,1)} %copy-done.5, bf16[2,3,128,192]{2,3,1,0:T(8,128)(2,1)S(1)} %maximum_convert_fusion), kind=kOutput, calls=%fused_computation.31 | convolution fusion | flops 56696640 | bytes 787200 | tf_op jit(solution)/shard_map/dot_general | solution.py:146
  101.7 1.4 %fusion.14 = f32[192]{0:T(256)S(1)} fusion(bf16[128,1152]{1,0:T(8,128)(2,1)S(1)} %collective-permute-done.13, bf16[2,768,1152]{2,1,0:T(8,128)(2,1)} %collective-permute-done.2, bf16[2,3,128,192]{2,3,1,0:T(8,128)(2,1)S(1)} %maximum_convert_fusion), kind=kOutput, calls=%fused_computation.34 | convolution fusion | flops 56696640 | bytes 787200 | tf_op jit(solution)/shard_map/dot_general | solution.py:146
  103.1 1.4 %fusion.10 = f32[192]{0:T(256)S(1)} fusion(bf16[128,1152]{1,0:T(8,128)(2,1)S(1)} %collective-permute-done.13, bf16[2,768,1152]{2,1,0:T(8,128)(2,1)} %copy-done.5, bf16[2,3,128,192]{2,3,1,0:T(8,128)(2,1)S(1)} %maximum_convert_fusion), kind=kOutput, calls=%fused_computation.30 | convolution fusion | flops 56696640 | bytes 787200 | tf_op jit(solution)/shard_map/dot_general | solution.py:146
  104.5 3.3 %collective-permute-done.15 = bf16[128,1152]{1,0:T(8,128)(2,1)S(1)} collective-permute-done((bf16[128,1152]{1,0:T(8,128)(2,1)S(1)}, bf16[128,1152]{1,0:T(8,128)(2,1)S(1)}, u32[]{:S(2)}, u32[]{:S(2)}) %collective-permute-start.15) | collective-permute-done | bytes 294944 | tf_op jit(solution)/shard_map/ppermute | solution.py:16
  107.8 1.4 %fusion.16 = f32[192]{0:T(256)S(1)} fusion(bf16[128,1152]{1,0:T(8,128)(2,1)S(1)} %collective-permute-done.15, bf16[2,768,1152]{2,1,0:T(8,128)(2,1)} %collective-permute-done.2, bf16[2,1,128,192]{2,3,1,0:T(8,128)(2,1)S(1)} %maximum_convert_fusion.1), kind=kOutput, calls=%fused_computation.36 | convolution fusion | flops 56696640 | bytes 787200 | tf_op jit(solution)/shard_map/dot_general | solution.py:146
  109.3 1.4 %fusion.12 = f32[192]{0:T(256)S(1)} fusion(bf16[128,1152]{1,0:T(8,128)(2,1)S(1)} %collective-permute-done.15, bf16[2,768,1152]{2,1,0:T(8,128)(2,1)} %copy-done.5, bf16[2,1,128,192]{2,3,1,0:T(8,128)(2,1)S(1)} %maximum_convert_fusion.1), kind=kOutput, calls=%fused_computation.32 | convolution fusion | flops 56696640 | bytes 787200 | tf_op jit(solution)/shard_map/dot_general | solution.py:146
  110.7 0.7 collective-permute-start.17
  111.4 1.0 maximum_select_fusion
  112.4 2.0 %collective-permute-done.17 = f32[4,192]{1,0:T(4,128)S(1)} collective-permute-done((f32[4,192]{1,0:T(4,128)S(1)}, f32[4,192]{1,0:T(4,128)S(1)}, u32[]{:S(2)}, u32[]{:S(2)}) %collective-permute-start.17) | collective-permute-done | bytes 3104 | tf_op jit(solution)/shard_map/ppermute | solution.py:16
  114.5 0.1 select_reduce_fusion
  114.6 0.7 mul.63
  (56 shorter events, 1.5 us)
Async XLA Ops:
  0.6 11.9 %copy-start = (bf16[128,1,2304]{2,0,1:T(8,128)(2,1)S(1)}, bf16[128,1,2304]{2,0,1:T(8,128)(2,1)}, u32[]{:S(2)}) copy-start(bf16[128,1,2304]{2,0,1:T(8,128)(2,1)} %param.7) | copy-start | bytes 1769476
  3.0 2.3 %copy-start.1 = (bf16[1,2304,1024]{2,1,0:T(8,128)(2,1)S(1)}, bf16[1,2304,1024]{2,1,0:T(8,128)(2,1)}, u32[]{:S(2)}) copy-start(bf16[1,2304,1024]{2,1,0:T(8,128)(2,1)} %param.8) | copy-start | bytes 14155780
  5.4 2.3 %copy-start.3 = (bf16[1,1024,2304]{2,1,0:T(8,128)(2,1)S(1)}, bf16[1,1024,2304]{2,1,0:T(8,128)(2,1)}, u32[]{:S(2)}) copy-start(bf16[1,1024,2304]{2,1,0:T(8,128)(2,1)} %param.10) | copy-start | bytes 14155780
  7.7 10.6 %copy-start.6 = (f32[1024]{0:T(1024)S(1)}, f32[1024]{0:T(1024)}, u32[]{:S(2)}) copy-start(f32[1024]{0:T(1024)} %param.9) | copy-start | bytes 12292
  12.6 28.3 %collective-permute-start.2 = (bf16[2,768,1152]{2,1,0:T(8,128)(2,1)}, bf16[2,768,1152]{2,1,0:T(8,128)(2,1)}, u32[]{:S(2)}, u32[]{:S(2)}) collective-permute-start(bf16[2,768,1152]{2,1,0:T(8,128)(2,1)} %shard_map.87), channel_id=1, source_target_pairs={{0,1},{1,0},{2,3},{3,2},{4,5},{5,4},{6,7},{7,6},{8,9},{9,8},{10,11... | collective-permute-start | bytes 10616840 | tf_op jit(solution)/shard_map/ppermute | solution.py:16
  12.6 18.2 %collective-permute-start.1 = (bf16[128,1152]{1,0:T(8,128)(2,1)S(1)}, bf16[128,1152]{1,0:T(8,128)(2,1)S(1)}, u32[]{:S(2)}, u32[]{:S(2)}) collective-permute-start(bf16[128,1152]{1,0:T(8,128)(2,1)S(1)} %dynamic-slice_bitcast_fusion), channel_id=1, source_target_pairs={{0,8},{4,12},{8,0},{12,4},{1,9},{5,13},{9,1},{13,5},{2,10},{6,14},... | collective-permute-start | bytes 884744 | tf_op jit(solution)/shard_map/ppermute | solution.py:16
  16.7 16.0 %collective-permute-start = (bf16[128,1152]{1,0:T(8,128)(2,1)S(1)}, bf16[128,1152]{1,0:T(8,128)(2,1)S(1)}, u32[]{:S(2)}, u32[]{:S(2)}) collective-permute-start(bf16[128,1152]{1,0:T(8,128)(2,1)S(1)} %dynamic-slice_bitcast_fusion), channel_id=1, source_target_pairs={{0,4},{4,0},{8,12},{12,8},{1,5},{5,1},{9,13},{13,9},{2,6},{6,2},{1... | collective-permute-start | bytes 884744 | tf_op jit(solution)/shard_map/ppermute | solution.py:16
  18.9 10.8 %collective-permute-start.5 = (f32[4,192]{1,0:T(4,128)S(1)}, f32[4,192]{1,0:T(4,128)S(1)}, u32[]{:S(2)}, u32[]{:S(2)}) collective-permute-start(f32[4,192]{1,0:T(4,128)S(1)} %select_n.86), channel_id=1, source_target_pairs={{0,1},{1,0},{2,3},{3,2},{4,5},{5,4},{6,7},{7,6},{8,9},{9,8},{10,11... | collective-permute-start | bytes 9224 | tf_op jit(solution)/shard_map/ppermute | solution.py:16
  18.9 2.3 %copy-start.2 = (bf16[1,2304,1024]{2,1,0:T(8,128)(2,1)S(1)}, bf16[1,2304,1024]{2,1,0:T(8,128)(2,1)}, u32[]{:S(2)}) copy-start(bf16[1,2304,1024]{2,1,0:T(8,128)(2,1)} %param.8) | copy-start | bytes 14155780
  21.3 2.3 %copy-start.4 = (bf16[1,1024,2304]{2,1,0:T(8,128)(2,1)S(1)}, bf16[1,1024,2304]{2,1,0:T(8,128)(2,1)}, u32[]{:S(2)}) copy-start(bf16[1,1024,2304]{2,1,0:T(8,128)(2,1)} %param.10) | copy-start | bytes 14155780
  27.6 1.8 %copy-start.5 = (bf16[2,768,1152]{2,1,0:T(8,128)(2,1)}, bf16[2,768,1152]{2,1,0:T(8,128)(2,1)S(1)}, u32[]{:S(2)}) copy-start(bf16[2,768,1152]{2,1,0:T(8,128)(2,1)S(1)} %shard_map.86) | copy-start | bytes 10616836
  30.8 8.8 %collective-permute-start.7 = (bf16[128,1152]{1,0:T(8,128)(2,1)S(1)}, bf16[128,1152]{1,0:T(8,128)(2,1)S(1)}, u32[]{:S(2)}, u32[]{:S(2)}) collective-permute-start(bf16[128,1152]{1,0:T(8,128)(2,1)S(1)} %collective-permute-done.1), channel_id=1, source_target_pairs={{0,4},{4,0},{8,12},{12,8},{1,5},{5,1},{9,13},{13,9},{2,6},{6,2},{1... | collective-permute-start | bytes 884744 | tf_op jit(solution)/shard_map/ppermute | solution.py:16
  42.2 4.6 %collective-permute-start.8 = (bf16[2,1,128,192]{2,3,1,0:T(8,128)(2,1)S(1)}, bf16[2,1,128,192]{2,3,1,0:T(8,128)(2,1)S(1)}, u32[]{:S(2)}, u32[]{:S(2)}) collective-permute-start(bf16[2,1,128,192]{2,3,1,0:T(8,128)(2,1)S(1)} %pad_maximum_fusion.1), channel_id=1, source_target_pairs={{0,1},{1,0},{2,3},{3,2},{4,5},{5,4},{6,7},{7,6},{8,9},{9,8},{10,11... | collective-permute-start | bytes 294920 | tf_op jit(solution)/shard_map/ppermute | solution.py:16
  46.2 5.5 %collective-permute-start.3 = (bf16[2,3,128,192]{2,3,1,0:T(8,128)(2,1)S(1)}, bf16[2,3,128,192]{2,3,1,0:T(8,128)(2,1)S(1)}, u32[]{:S(2)}, u32[]{:S(2)}) collective-permute-start(bf16[2,3,128,192]{2,3,1,0:T(8,128)(2,1)S(1)} %pad_maximum_fusion), channel_id=1, source_target_pairs={{0,1},{1,0},{2,3},{3,2},{4,5},{5,4},{6,7},{7,6},{8,9},{9,8},{10,11... | collective-permute-start | bytes 884744 | tf_op jit(solution)/shard_map/ppermute | solution.py:16
  46.8 4.8 %collective-permute-start.9 = (bf16[2,1,128,192]{2,3,1,0:T(8,128)(2,1)S(1)}, bf16[2,1,128,192]{2,3,1,0:T(8,128)(2,1)S(1)}, u32[]{:S(2)}, u32[]{:S(2)}) collective-permute-start(bf16[2,1,128,192]{2,3,1,0:T(8,128)(2,1)S(1)} %add_convert_fusion.1), channel_id=1, source_target_pairs={{0,2},{2,0},{1,3},{3,1},{4,6},{6,4},{5,7},{7,5},{8,10},{10,8},{9,1... | collective-permute-start | bytes 294920 | tf_op jit(solution)/shard_map/ppermute | solution.py:16
  51.9 8.2 %collective-permute-start.4 = (bf16[2,3,128,192]{2,3,1,0:T(8,128)(2,1)S(1)}, bf16[2,3,128,192]{2,3,1,0:T(8,128)(2,1)S(1)}, u32[]{:S(2)}, u32[]{:S(2)}) collective-permute-start(bf16[2,3,128,192]{2,3,1,0:T(8,128)(2,1)S(1)} %add_convert_fusion), channel_id=1, source_target_pairs={{0,2},{2,0},{1,3},{3,1},{4,6},{6,4},{5,7},{7,5},{8,10},{10,8},{9,1... | collective-permute-start | bytes 884744 | tf_op jit(solution)/shard_map/ppermute | solution.py:16
  55.8 15.0 %copy-start.7 = (f32[1,2304]{1,0:T(1,128)S(1)}, f32[1,2304]{1,0:T(1,128)}, u32[]{:S(2)}) copy-start(f32[1,2304]{1,0:T(1,128)} %param.11) | copy-start | bytes 27652
  55.8 7.9 %collective-permute-start.10 = (bf16[128,1152]{1,0:T(8,128)(2,1)S(1)}, bf16[128,1152]{1,0:T(8,128)(2,1)S(1)}, u32[]{:S(2)}, u32[]{:S(2)}) collective-permute-start(bf16[128,1152]{1,0:T(8,128)(2,1)S(1)} %fusion.8), channel_id=1, source_target_pairs={{0,4},{4,0},{8,12},{12,8},{1,5},{5,1},{9,13},{13,9},{2,6},{6,2},{1... | collective-permute-start | bytes 884744 | tf_op jit(solution)/shard_map/ppermute | solution.py:16
  65.0 14.3 %collective-permute-start.11 = (bf16[128,1152]{1,0:T(8,128)(2,1)S(1)}, bf16[128,1152]{1,0:T(8,128)(2,1)S(1)}, u32[]{:S(2)}, u32[]{:S(2)}) collective-permute-start(bf16[128,1152]{1,0:T(8,128)(2,1)S(1)} %fusion.7), channel_id=1, source_target_pairs={{0,8},{4,12},{8,0},{12,4},{1,9},{5,13},{9,1},{13,5},{2,10},{6,14},... | collective-permute-start | bytes 884744 | tf_op jit(solution)/shard_map/ppermute | solution.py:16
  69.0 11.8 %collective-permute-start.6 = (bf16[128,1152]{1,0:T(8,128)(2,1)S(1)}, bf16[128,1152]{1,0:T(8,128)(2,1)S(1)}, u32[]{:S(2)}, u32[]{:S(2)}) collective-permute-start(bf16[128,1152]{1,0:T(8,128)(2,1)S(1)} %fusion.6), channel_id=1, source_target_pairs={{0,4},{4,0},{8,12},{12,8},{1,5},{5,1},{9,13},{13,9},{2,6},{6,2},{1... | collective-permute-start | bytes 884744 | tf_op jit(solution)/shard_map/ppermute | solution.py:16
  82.1 29.4 %collective-permute-start.12 = (bf16[128,1152]{1,0:T(8,128)(2,1)S(1)}, bf16[128,1152]{1,0:T(8,128)(2,1)S(1)}, u32[]{:S(2)}, u32[]{:S(2)}) collective-permute-start(bf16[128,1152]{1,0:T(8,128)(2,1)S(1)} %fusion.5), channel_id=1, source_target_pairs={{0,1},{1,0},{2,3},{3,2},{4,5},{5,4},{6,7},{7,6},{8,9},{9,8},{10,11... | collective-permute-start | bytes 884744 | tf_op jit(solution)/shard_map/ppermute | solution.py:16
  82.2 16.8 %collective-permute-start.14 = (bf16[128,1152]{1,0:T(8,128)(2,1)S(1)}, bf16[128,1152]{1,0:T(8,128)(2,1)S(1)}, u32[]{:S(2)}, u32[]{:S(2)}) collective-permute-start(bf16[128,1152]{1,0:T(8,128)(2,1)S(1)} %fusion.5), channel_id=1, source_target_pairs={{0,8},{4,12},{8,0},{12,4},{1,9},{5,13},{9,1},{13,5},{2,10},{6,14},... | collective-permute-start | bytes 884744 | tf_op jit(solution)/shard_map/ppermute | solution.py:16
  83.0 18.7 %collective-permute-start.13 = (bf16[128,1152]{1,0:T(8,128)(2,1)S(1)}, bf16[128,1152]{1,0:T(8,128)(2,1)S(1)}, u32[]{:S(2)}, u32[]{:S(2)}) collective-permute-start(bf16[128,1152]{1,0:T(8,128)(2,1)S(1)} %fusion.5), channel_id=1, source_target_pairs={{0,4},{4,0},{8,12},{12,8},{1,5},{5,1},{9,13},{13,9},{2,6},{6,2},{1... | collective-permute-start | bytes 884744 | tf_op jit(solution)/shard_map/ppermute | solution.py:16
  98.9 8.9 %collective-permute-start.15 = (bf16[128,1152]{1,0:T(8,128)(2,1)S(1)}, bf16[128,1152]{1,0:T(8,128)(2,1)S(1)}, u32[]{:S(2)}, u32[]{:S(2)}) collective-permute-start(bf16[128,1152]{1,0:T(8,128)(2,1)S(1)} %collective-permute-done.14), channel_id=1, source_target_pairs={{0,4},{4,0},{8,12},{12,8},{1,5},{5,1},{9,13},{13,9},{2,6},{6,2},{1... | collective-permute-start | bytes 884744 | tf_op jit(solution)/shard_map/ppermute | solution.py:16
  109.2 1.5 %collective-permute-start.16 = (f32[4,192]{1,0:T(4,128)S(1)}, f32[4,192]{1,0:T(4,128)S(1)}, u32[]{:S(2)}, u32[]{:S(2)}) collective-permute-start(f32[4,192]{1,0:T(4,128)S(1)} %pad_maximum_fusion.2), channel_id=1, source_target_pairs={{0,1},{1,0},{2,3},{3,2},{4,5},{5,4},{6,7},{7,6},{8,9},{9,8},{10,11... | collective-permute-start | bytes 9224 | tf_op jit(solution)/shard_map/ppermute | solution.py:16
  110.7 3.7 %collective-permute-start.17 = (f32[4,192]{1,0:T(4,128)S(1)}, f32[4,192]{1,0:T(4,128)S(1)}, u32[]{:S(2)}, u32[]{:S(2)}) collective-permute-start(f32[4,192]{1,0:T(4,128)S(1)} %maximum_add_fusion), channel_id=1, source_target_pairs={{0,2},{2,0},{1,3},{3,1},{4,6},{6,4},{5,7},{7,5},{8,10},{10,8},{9,1... | collective-permute-start | bytes 9224 | tf_op jit(solution)/shard_map/ppermute | solution.py:16

commit v3 on v1

v3 whole, which is shorter than its diff:
```python
import jax
import jax.numpy as jnp
from jax import lax
from jax.experimental import pallas as pl
from jax.experimental.pallas import tpu as pltpu
from jax.sharding import PartitionSpec as P

LATBLK = 64
TBLK = 128
CAP = 3
SLOT = CAP * LATBLK
ROW_PARTS = 2
PARAMS = pltpu.CompilerParams(vmem_limit_bytes=16 * 1024 * 1024)
SMALL = pl.CostEstimate(flops=0, bytes_accessed=0, transcendentals=0)


def swap(value, axis, mask):
    size = lax.axis_size(axis)
    return lax.ppermute(value, axis, [(i, i ^ mask) for i in range(size)])


def masks_of(axis):
    size = lax.axis_size(axis)
    return [1 << i for i in range(size.bit_length() - 1)]


def spread(value):
    have = {0: value}
    for mask in reversed(masks_of("lat")):
        for offset in list(have):
            have[offset ^ mask] = swap(have[offset], "lat", mask)
    return have


def sum_layers(value):
    for mask in masks_of("layer"):
        total = value.astype(jnp.float32) + swap(value, "layer", mask).astype(jnp.float32)
        value = total.astype(value.dtype)
    return total


def in_hbm(value):
    return pltpu.with_memory_space_constraint(value, pltpu.HBM)


def in_vmem(value):
    return pltpu.with_memory_space_constraint(value, pltpu.VMEM)


def half_of(tokens, core):
    rows, width = tokens.shape
    half = width // 2

    def body(core_ref, token_ref, out_ref):
        out_ref[...] = token_ref[...]

    return pl.pallas_call(
        body,
        grid_spec=pltpu.PrefetchScalarGridSpec(
            num_scalar_prefetch=1,
            grid=(1,),
            in_specs=[pl.BlockSpec((rows, half), lambda i, c: (0, c[0]))],
            out_specs=pl.BlockSpec((rows, half), lambda i, c: (0, 0)),
        ),
        out_shape=jax.ShapeDtypeStruct((rows, half), tokens.dtype),
        compiler_params=PARAMS,
        cost_estimate=SMALL,
    )(core, in_hbm(tokens))


def plan(block_ids, counts, places, bias):
    block_total, slot_total = block_ids.shape
    latents = bias.shape[0]
    device_blocks = latents // LATBLK
    wide = 2 * LATBLK

    def body(ids_ref, counts_ref, places_ref, bias_ref, own_ref, other_ref, out_ref):
        place, core = places_ref[0], places_ref[1]
        pick_refs = (own_ref, other_ref)
        for offset in range(block_total):
            block = place ^ offset
            for pick_ref in pick_refs:
                for s in range(CAP):
                    pick_ref[offset * CAP + s] = -1

            def step(slot, found):
                chosen = ids_ref[block, slot]
                shard = lax.div(chosen, device_blocks)
                local = lax.rem(chosen, device_blocks)
                live = slot < counts_ref[block]
                new = []
                for i, pick_ref in enumerate(pick_refs):
                    mine = live & (shard == place * 2 + (core ^ i))
                    at = offset * CAP + jnp.minimum(found[i], CAP - 1)

                    @pl.when(mine)
                    def _():
                        pick_ref[at] = local

                    new.append(found[i] + mine.astype(jnp.int32))
                return tuple(new)

            lax.fori_loop(0, slot_total, step, (jnp.int32(0), jnp.int32(0)))
        for offset in range(block_total):
            for s in range(CAP):
                chosen = own_ref[offset * CAP + s]
                at = jnp.maximum(chosen, 0)
                pair = bias_ref[pl.ds(lax.div(at, 2), 1), :]
                row = jnp.where(lax.rem(at, 2) == 1, pair[:, LATBLK:], pair[:, :LATBLK])
                out_ref[offset : offset + 1, s * LATBLK : (s + 1) * LATBLK] = jnp.where(
                    chosen < 0, -jnp.inf, row
                )

    smem = pl.BlockSpec(memory_space=pltpu.SMEM)
    picks = jax.ShapeDtypeStruct((block_total * CAP,), jnp.int32)
    return pl.pallas_call(
        body,
        grid=(1,),
        in_specs=[smem] * 3 + [whole((latents // wide, wide))],
        out_specs=[smem, smem, whole((block_total, SLOT))],
        out_shape=[picks, picks, jax.ShapeDtypeStruct((block_total, SLOT), jnp.float32)],
        compiler_params=PARAMS,
        cost_estimate=SMALL,
    )(in_hbm(block_ids), in_hbm(counts), places, in_hbm(bias.reshape(latents // wide, wide)))


def encoder_slots(w_enc, pick, core):
    half = w_enc.shape[0] // 2
    blocks = pick.shape[0] // CAP

    def body(pick_ref, core_ref, *refs):
        step = pl.program_id(0)
        for s in range(CAP):
            odd = lax.rem(jnp.maximum(pick_ref[step * CAP + s], 0), 2)
            wide = refs[s][...]
            left, right = wide[:, :LATBLK], wide[:, LATBLK:]
            refs[CAP][:, s * LATBLK : (s + 1) * LATBLK] = jnp.where(odd == 1, right, left)

    def spec(s):
        return pl.BlockSpec(
            (half, 2 * LATBLK),
            lambda i, p, c: (c[0], lax.div(jnp.maximum(p[i * CAP + s], 0), 2)),
        )

    return pl.pallas_call(
        body,
        grid_spec=pltpu.PrefetchScalarGridSpec(
            num_scalar_prefetch=2,
            grid=(blocks,),
            in_specs=[spec(s) for s in range(CAP)],
            out_specs=pl.BlockSpec((None, half, SLOT), lambda i, p, c: (i, 0, 0)),
        ),
        out_shape=jax.ShapeDtypeStruct((blocks, half, SLOT), jnp.bfloat16),
        compiler_params=PARAMS,
        cost_estimate=SMALL,
    )(pick, core, *([in_hbm(w_enc)] * CAP))


def decoder_slots(w_dec, pick, core):
    half = w_dec.shape[1] // 2
    blocks = pick.shape[0] // CAP

    def body(pick_ref, core_ref, *refs):
        for s in range(CAP):
            refs[CAP][s * LATBLK : (s + 1) * LATBLK, :] = refs[s][...]

    def spec(s):
        return pl.BlockSpec(
            (LATBLK, half), lambda i, p, c: (jnp.maximum(p[i * CAP + s], 0), c[0])
        )

    return pl.pallas_call(
        body,
        grid_spec=pltpu.PrefetchScalarGridSpec(
            num_scalar_prefetch=2,
            grid=(blocks,),
            in_specs=[spec(s) for s in range(CAP)],
            out_specs=pl.BlockSpec((None, SLOT, half), lambda i, p, c: (i, 0, 0)),
        ),
        out_shape=jax.ShapeDtypeStruct((blocks, SLOT, half), jnp.bfloat16),
        compiler_params=PARAMS,
        cost_estimate=SMALL,
    )(pick, core, *([in_hbm(w_dec)] * CAP))


def whole(shape):
    return pl.BlockSpec(shape, lambda i, *_: (0,) * len(shape))


def slot_specs(weights, offsets):
    return [
        pl.BlockSpec((None, *w.shape[1:]), lambda i, *_, o=o: (o, 0, 0))
        for o in offsets
        for w in weights
    ]


def slots(weights, offsets):
    return [w for _ in offsets for w in weights]


def across(a, b):
    return lax.dot_general(a, b, (((1,), (1,)), ((), ())), preferred_element_type=jnp.float32)


def encode(blocks, weights, offsets, core):
    count = len(blocks)
    rows, half = blocks[0].shape

    def body(core_ref, *refs):
        out_ref = refs[-1]
        first = core_ref[0] == 0
        for at in range(count):
            own, other = [
                jnp.dot(
                    refs[at][...], refs[count + 2 * at + i][...],
                    preferred_element_type=jnp.float32,
                ).astype(jnp.bfloat16)
                for i in range(2)
            ]
            out_ref[at, :, :SLOT] = jnp.where(first, own, other)
            out_ref[at, :, SLOT:] = jnp.where(first, other, own)

    return pl.pallas_call(
        body,
        grid_spec=pltpu.PrefetchScalarGridSpec(
            num_scalar_prefetch=1,
            grid=(1,),
            in_specs=[whole((rows, half))] * count + slot_specs(weights, offsets),
            out_specs=whole((count, rows, 2 * SLOT)),
        ),
        out_shape=jax.ShapeDtypeStruct((count, rows, 2 * SLOT), jnp.bfloat16),
        compiler_params=PARAMS,
        cost_estimate=SMALL,
    )(core, *[in_vmem(block) for block in blocks], *slots(weights, offsets))


def own_and_other(value, core_ref):
    low, high = value[:, :SLOT], value[:, SLOT:]
    first = core_ref[0] == 0
    return jnp.where(first, low, high), jnp.where(first, high, low)


def decode(pre, biases, weights, offsets, splits, core):
    count, rows, _ = pre.shape
    half = weights[0].shape[2]

    def body(core_ref, *refs):
        pre_ref, bias_refs, weight_refs = refs[0], refs[1:3], refs[3 : 3 + 2 * count]
        code_ref, part_refs = refs[3 + 2 * count], refs[4 + 2 * count :]
        for at, offset in enumerate(offsets):
            total = None
            for i, one in enumerate(own_and_other(pre_ref[at], core_ref)):
                code = jnp.maximum(one + bias_refs[i][offset : offset + 1, :], 0.0)
                code = code.astype(jnp.bfloat16)
                code_ref[at, :, i * SLOT : (i + 1) * SLOT] = code
                term = jnp.dot(
                    code, weight_refs[2 * at + i][...], preferred_element_type=jnp.float32
                )
                total = term if total is None else total + term
            step = rows // splits[at]
            for r in range(splits[at]):
                part_ref = part_refs[sum(splits[:at]) + r]
                part_ref[...] = total[r * step : (r + 1) * step].astype(part_ref.dtype)

    shapes = [
        jax.ShapeDtypeStruct((rows // split, half), jnp.bfloat16 if offset else jnp.float32)
        for offset, split in zip(offsets, splits)
        for _ in range(split)
    ]
    code, *parts = pl.pallas_call(
        body,
        grid_spec=pltpu.PrefetchScalarGridSpec(
            num_scalar_prefetch=1,
            grid=(1,),
            in_specs=[whole(pre.shape)]
            + [whole(bias.shape) for bias in biases]
            + slot_specs(weights, offsets),
            out_specs=[whole(pre.shape)] + [whole(shape.shape) for shape in shapes],
        ),
        out_shape=[jax.ShapeDtypeStruct(pre.shape, jnp.bfloat16)] + shapes,
        compiler_params=PARAMS,
        cost_estimate=SMALL,
    )(core, pre, *biases, *slots(weights, offsets))
    by_offset = {}
    for offset, split in zip(offsets, splits):
        by_offset[offset], parts = parts[:split], parts[split:]
    return code, by_offset


def remainder(part, arrived, bias, tokens, core, r, rows):
    half = part.shape[1]

    def body(core_ref, part_ref, bias_ref, token_ref, *refs):
        total = part_ref[...]
        for arrived_ref in refs[:-1]:
            total = total + arrived_ref[...].astype(jnp.float32)
        total = total + bias_ref[...]
        refs[-1][...] = (total - token_ref[...].astype(jnp.float32)).astype(jnp.bfloat16)

    def at_part(value):
        return pl.BlockSpec((rows, half), lambda i, c: (r if value.shape[0] > rows else 0, 0))

    return pl.pallas_call(
        body,
        grid_spec=pltpu.PrefetchScalarGridSpec(
            num_scalar_prefetch=1,
            grid=(1,),
            in_specs=[
                at_part(part),
                pl.BlockSpec((1, half), lambda i, c: (0, c[0])),
                at_part(tokens),
            ]
            + [at_part(value) for value in arrived],
            out_specs=pl.BlockSpec((rows, half), lambda i, c: (0, 0)),
        ),
        out_shape=jax.ShapeDtypeStruct((rows, half), jnp.bfloat16),
        compiler_params=PARAMS,
        cost_estimate=SMALL,
    )(core, part, bias, tokens, *arrived)


def gradient(error, codes, at, first, weights, offset):
    rows, half = error.shape

    def body(error_ref, code_ref, own_ref, other_ref, out_ref):
        for i, weight_ref in enumerate((own_ref, other_ref)):
            code = code_ref[:, i * SLOT : (i + 1) * SLOT].astype(jnp.float32)
            grad = across(error_ref[...], weight_ref[...])
            out_ref[i : i + 1, :] = jnp.sum(code * grad, axis=0, keepdims=True)

    return pl.pallas_call(
        body,
        grid=(1,),
        in_specs=[
            whole((rows, half)),
            pl.BlockSpec((None, rows, 2 * SLOT), lambda i: (at, first, 0)),
        ]
        + slot_specs(weights, [offset]),
        out_specs=whole((2, SLOT)),
        out_shape=jax.ShapeDtypeStruct((2, SLOT), jnp.float32),
        compiler_params=PARAMS,
        cost_estimate=SMALL,
    )(error, codes, *slots(weights, [offset]))


def gathered(terms):
    blocks = len(terms)
    flat = [term for block in terms for term in block]
    ends = [sum(len(block) for block in terms[: i + 1]) for i in range(blocks)]

    def body(*refs):
        for o in range(blocks):
            total = None
            for ref in refs[ends[o] - len(terms[o]) : ends[o]]:
                total = ref[...] if total is None else total + ref[...]
            for i in range(2):
                refs[len(flat) + i][o : o + 1, :] = total[i : i + 1, :]

    shape = jax.ShapeDtypeStruct((blocks, SLOT), jnp.float32)
    return pl.pallas_call(
        body,
        grid=(1,),
        in_specs=[whole((2, SLOT))] * len(flat),
        out_specs=[whole(shape.shape)] * 2,
        out_shape=[shape, shape],
        compiler_params=PARAMS,
        cost_estimate=SMALL,
    )(*flat)


def by_latent(total, pick, latents):
    wide = 2 * LATBLK
    blocks = total.shape[0]

    def body(pick_ref, total_ref, out_ref):
        out_ref[...] = jnp.zeros(out_ref.shape, jnp.float32)
        lane = lax.broadcasted_iota(jnp.int32, (1, wide), 1)
        for o in range(blocks):
            for s in range(CAP):
                chosen = pick_ref[o * CAP + s]
                at = jnp.maximum(chosen, 0)
                value = total_ref[o : o + 1, s * LATBLK : (s + 1) * LATBLK] * (1.0 / TBLK)
                here = (lane // LATBLK == lax.rem(at, 2)) & (chosen >= 0)
                row = pl.ds(lax.div(at, 2), 1)
                pair = jnp.concatenate([value, value], axis=1)
                out_ref[row, :] = out_ref[row, :] + jnp.where(here, pair, 0.0)

    return pl.pallas_call(
        body,
        grid_spec=pltpu.PrefetchScalarGridSpec(
            num_scalar_prefetch=1,
            grid=(1,),
            in_specs=[whole(total.shape)],
            out_specs=whole((latents // wide, wide)),
        ),
        out_shape=jax.ShapeDtypeStruct((latents // wide, wide), jnp.float32),
        compiler_params=PARAMS,
        cost_estimate=SMALL,
    )(pick, total).reshape(latents)


def side_by_side(own, other, core):
    parts = len(own)
    rows, half = own[0].shape

    def body(core_ref, *refs):
        out_ref = refs[-1]
        first = core_ref[0] == 0
        for r in range(parts):
            here, there = refs[r][...], refs[parts + r][...]
            at = slice(r * rows, (r + 1) * rows)
            out_ref[at, :half] = jnp.where(first, here, there)
            out_ref[at, half:] = jnp.where(first, there, here)

    return pl.pallas_call(
        body,
        grid_spec=pltpu.PrefetchScalarGridSpec(
            num_scalar_prefetch=1,
            grid=(1,),
            in_specs=[whole((rows, half))] * (2 * parts),
            out_specs=whole((parts * rows, 2 * half)),
        ),
        out_shape=jax.ShapeDtypeStruct((parts * rows, 2 * half), own[0].dtype),
        compiler_params=PARAMS,
        cost_estimate=SMALL,
    )(core, *own, *other)


def on_device(tokens, w_enc, b_enc, w_dec, b_dec, block_ids, counts):
    own_rows, layers_here, width = tokens.shape
    assert own_rows == TBLK and layers_here == 1
    latents_here = w_enc.shape[2]
    device_blocks = latents_here // LATBLK
    half = width // 2
    lat_size = lax.axis_size("lat")
    place = lax.axis_index("lat")
    core = lax.axis_index("tok")
    bf16, f32 = jnp.bfloat16, jnp.float32

    odds = list(range(1, lat_size, 2))
    evens = list(range(2, lat_size, 2))
    core_at = jnp.full((1,), core, jnp.int32)
    own_half = half_of(tokens.reshape(own_rows, width), core_at)
    near_tokens = swap(own_half, "lat", 1)

    own_pick, other_pick, bias_own = plan(
        block_ids, counts, jnp.stack([place, core]).astype(jnp.int32), b_enc
    )
    enc_own = encoder_slots(w_enc[0], own_pick, core_at)
    enc_swapped, near_tokens = lax.optimization_barrier((swap(w_enc, "tok", 1), near_tokens))
    enc_two = [enc_own, encoder_slots(enc_swapped[0], other_pick, core_at)]
    token_blocks = {0: own_half, 1: near_tokens}
    for mask in reversed(masks_of("lat")):
        if mask > 1:
            for offset in [o for o in token_blocks if o % 2 == 0]:
                token_blocks[offset ^ mask] = swap(token_blocks[offset], "lat", mask)
    even_tokens, enc_two = lax.optimization_barrier(
        ([token_blocks[o] for o in evens], enc_two)
    )
    for offset, value in zip(evens, even_tokens):
        token_blocks[offset] = value
        token_blocks[offset ^ 1] = swap(value, "lat", 1)
    biases = (bias_own, swap(bias_own, "tok", 1))

    def encoded(offsets):
        return encode([token_blocks[o] for o in offsets], enc_two, offsets, core_at)

    def forward(term, offsets, split):
        other = swap(term, "tok", 1)
        both = (term.astype(f32) + other.astype(f32)).astype(bf16)
        pre = sum_layers(both)
        code, parts = decode(
            pre, biases, dec_two, offsets, [split] * len(offsets), core_at
        )
        return {o: (code, at) for at, o in enumerate(offsets)}, parts

    dec_two = [
        decoder_slots(w_dec[0], own_pick, core_at),
        decoder_slots(swap(w_dec, "tok", 1)[0], other_pick, core_at),
    ]
    codes, parts = {}, {}
    for offsets, split in ((evens, 1), ([0, 1], 1), (odds[1:], ROW_PARTS)):
        code, part = forward(encoded(offsets), offsets, split)
        codes.update(code)
        parts.update(part)

    arrived = {
        o: [swap(part, "lat", o) for part in parts[o]] for o in [*evens, *odds]
    }
    halves = [
        remainder(
            parts[0][0],
            [value[r if len(value) > 1 else 0] for value in arrived.values()],
            b_dec,
            own_half,
            core_at,
            r,
            own_rows // ROW_PARTS,
        )
        for r in range(ROW_PARTS)
    ]

    terms = [[] for _ in range(lat_size)]
    for r in range(ROW_PARTS):
        for o, error in spread(halves[r]).items():
            terms[o].append(gradient(error, *codes[o], r, dec_two, o))
    own_sum, other_sum = gathered(terms)
    scale_grad = by_latent(
        sum_layers(own_sum + swap(other_sum, "tok", 1)), own_pick, latents_here
    )
    residual = side_by_side(halves, [swap(half, "tok", 1) for half in halves], core_at)
    return residual.reshape(tokens.shape), scale_grad


def solution(mesh):
    in_specs = (
        P(("groups", "lat"), "layer", None),
        P("layer", None, ("lat", "tok")),
        P(("lat", "tok")),
        P("layer", ("lat", "tok"), None),
        P("layer", None),
        P("groups", None),
        P("groups"),
    )
    out_specs = (P(("groups", "lat"), "layer", None), P(("groups", "lat", "tok")))
    return jax.shard_map(
        on_device, mesh=mesh, in_specs=in_specs, out_specs=out_specs, check_vma=False
    )
```

time: 117 us -> 96.7 us (0.83)
  Pallas kernels: 0 us -> 30.3 us
  matrix products: 29.2 us -> 0 us
  waiting for transfers between devices: 56 us -> 32.6 us
  starting transfers between devices: 15.9 us -> 31.8 us
  local copies, waits for them, and re-layouts: 11.5 us -> 0.01 us
  other arithmetic: 3.15 us -> 0.28 us
    pallas_call x0 -> x25, Pallas kernels: none -> 30.3 us  [the longest x2 11 us: encoder_slots(): pl.pallas_call(body, grid_spec=pltpu.PrefetchScalarGridSpec(num_scalar_pr...]
    dot_general x26 -> x0, matrix products: 29.2 us -> none  [the longest x2 14.2 us: picked(): return jnp.dot(a, b, preferred_element_type=f32).astype(bf16)]
    ppermute x23 -> x26, waiting for transfers between devices: 56 us -> 32.6 us  [swap(): return lax.ppermute(value, axis, [(i, i ^ mask) for i in range(size)])]
    ppermute x23 -> x26, starting transfers between devices: 15.9 us -> 31.8 us  [swap(): return lax.ppermute(value, axis, [(i, i ^ mask) for i in range(size)])]
    dynamic_slice x4 -> x0, local copies, waits for them, and re-layouts: 5.66 us -> none  [cut(): return lax.dynamic_slice_in_dim(value, which * half, half, axis)]
    gather x2 -> x0, local copies, waits for them, and re-layouts: 2.54 us -> none  [the longest x1 1.3 us: on_device(): jnp.take(counts, order)[:, None]]
    unnamed x10 -> x2, local copies, waits for them, and re-layouts: 1.81 us -> 0.01 us
  transfers between devices with their start and end apart: 23 -> 26, of which waited for: 11 -> 14; matrix products, arithmetic and copies ran while one was open for 35% -> 0% of each run, Pallas kernels for 0% -> 30%
where the time goes in v3:
time: 96.7 us; the launch traced here: 95.8 us
  waiting for transfers between devices  32.6 us (34%)
  starting transfers between devices  31.8 us (33%)
  Pallas kernels  30.3 us (31%)
    ppermute x26, waiting for transfers between devices, swap(): return lax.ppermute(value, axis, [(i, i ^ mask) for i in range(size)])  32.6 us
    ppermute x26, starting transfers between devices, swap(): return lax.ppermute(value, axis, [(i, i ^ mask) for i in range(size)])  31.8 us
    pallas_call x2, Pallas kernels, encoder_slots(): pl.pallas_call(body, grid_spec=pltpu.PrefetchScalarGridSpec(num_scalar_pr...  11 us
    pallas_call x2, Pallas kernels, decoder_slots(): pl.pallas_call(body, grid_spec=pltpu.PrefetchScalarGridSpec(num_scalar_pr...  6.01 us
    pallas_call x8, Pallas kernels, gradient(): pl.pallas_call(body, grid=(1,), in_specs=[whole((rows, half)), pl.BlockSp...  4.66 us
    pallas_call x1, Pallas kernels, plan(): pl.pallas_call(body, grid=(1,), in_specs=[smem] * 3 + [whole((latents //...  2.26 us
  transfers between devices with their start and end apart: 26, of which 14 were waited for; matrix products, arithmetic and copies ran while one was open for 0% of the time, Pallas kernels for 30%

profile of v3, /device:TPU:0, one launch (start us, length us, event | category | flops | bytes accessed | tf_op | source)
XLA Modules:
  0.0 95.8 jit_solution(13537680647276809334)
XLA Ops:
  0.6 0.5 collective-permute-start
  1.1 0.1 collective-permute-start.6
  1.2 1.0 %shard_map.86.refs_0_.token_ref = bf16[128,1152]{1,0:T(8,128)(2,1)S(1)} custom-call(s32[1]{0:T(128)} %bitcast.core_ref, bf16[128,2304]{1,0:T(8,128)(2,1)} %bitcast.16), custom_call_target="tpu_custom_call" | custom-call | tf_op jit(solution)/shard_map/pallas_call | solution.py:57
  2.2 3.1 %collective-permute-start.1 = (bf16[128,1152]{1,0:T(8,128)(2,1)S(1)}, bf16[128,1152]{1,0:T(8,128)(2,1)S(1)}, u32[]{:S(2)}, u32[]{:S(2)}) collective-permute-start(bf16[128,1152]{1,0:T(8,128)(2,1)S(1)} %shard_map.86.refs_0_.token_ref), channel_id=1, source_target_pairs={{0,4},{4,0},{8,12},{12,8},{1,5},{5,1},{9,13},{13,9},{2,6},{6,2},{1... | collective-permute-start | bytes 884744 | tf_op jit(solution)/shard_map/ppermute | solution.py:19
  5.3 2.6 %collective-permute-start.2 = (bf16[128,1152]{1,0:T(8,128)(2,1)S(1)}, bf16[128,1152]{1,0:T(8,128)(2,1)S(1)}, u32[]{:S(2)}, u32[]{:S(2)}) collective-permute-start(bf16[128,1152]{1,0:T(8,128)(2,1)S(1)} %shard_map.86.refs_0_.token_ref), channel_id=1, source_target_pairs={{0,8},{4,12},{8,0},{12,4},{1,9},{5,13},{9,1},{13,5},{2,10},{6,14},... | collective-permute-start | bytes 884744 | tf_op jit(solution)/shard_map/ppermute | solution.py:19
  7.9 0.1 pad_add_fusion.places_ref
  7.9 2.3 %shard_map.87 = (s32[12]{0:T(128)S(1)}, s32[12]{0:T(128)S(1)}, f32[4,192]{1,0:T(4,128)S(1)}) custom-call(s32[4,16]{1,0:T(4,128)} %ids_ref.1, s32[4]{0:T(128)} %counts_ref.1, s32[2]{0:T(128)S(1)} %pad_add_fusion.places_ref, f32[8,128]{1,0:T(8,128)} %bitcast.18), custom_call_target="tpu_custom_call" | custom-call | tf_op jit(solution)/shard_map/pallas_call | solution.py:116
  10.2 5.5 %shard_map.88.refs_2_.refs_4_.refs_1_ = bf16[4,1152,192]{2,1,0:T(8,128)(2,1)S(1)} custom-call(s32[12]{0:T(128)S(1)} %get-tuple-element.21.pick_ref, s32[1]{0:T(128)} %bitcast.core_ref, bf16[2304,1024]{1,0:T(8,128)(2,1)} %bitcast.10, bf16[2304,1024]{1,0:T(8,128)(2,1)} %bitcast.11, bf16[2304,1024]{1,0:T(8,128)(2,1)} %bitcast.12), custom_call_target="tpu_custom_call" | custom-call | tf_op jit(solution)/shard_map/pallas_call | solution.py:145
  15.7 3.1 %collective-permute-done.1.refs_1_ = bf16[128,1152]{1,0:T(8,128)(2,1)S(1)} collective-permute-done((bf16[128,1152]{1,0:T(8,128)(2,1)S(1)}, bf16[128,1152]{1,0:T(8,128)(2,1)S(1)}, u32[]{:S(2)}, u32[]{:S(2)}) %collective-permute-start.1) | collective-permute-done | bytes 294944 | tf_op jit(solution)/shard_map/ppermute | solution.py:19
  18.7 5.6 %shard_map.89.refs_3_.refs_5_.refs_2_ = bf16[4,1152,192]{2,1,0:T(8,128)(2,1)S(1)} custom-call(s32[12]{0:T(128)S(1)} %get-tuple-element.22.pick_ref, s32[1]{0:T(128)} %bitcast.core_ref, bf16[2304,1024]{1,0:T(8,128)(2,1)} %bitcast.5.refs_0_.refs_1_.refs_2_, bf16[2304,1024]{1,0:T(8,128)(2,1)} %bitcast.5.refs_0_.refs_1_.refs_2_, ...), custom_call_target="tpu_custom_call" | custom-call | tf_op jit(solution)/shard_map/pallas_call | solution.py:145
  24.3 0.4 shard_map.94
  24.8 0.1 collective-permute-start.7
  24.8 0.5 collective-permute-start.5
  25.3 3.0 %shard_map.91.refs_3_.refs_5_.own_ref = bf16[4,192,1152]{2,1,0:T(8,128)(2,1)S(1)} custom-call(s32[12]{0:T(128)S(1)} %get-tuple-element.21.pick_ref, s32[1]{0:T(128)} %bitcast.core_ref, bf16[1024,2304]{1,0:T(8,128)(2,1)} %bitcast.13, bf16[1024,2304]{1,0:T(8,128)(2,1)} %bitcast.14, bf16[1024,2304]{1,0:T(8,128)(2,1)} %bitcast.15), custom_call_target="tpu_custom_call" | custom-call | tf_op jit(solution)/shard_map/pallas_call | solution.py:172
  28.4 0.1 collective-permute-start.11
  28.4 0.6 shard_map.90
  29.0 0.1 collective-permute-start.3
  29.1 3.0 %shard_map.92.refs_4_.refs_6_.other_ref = bf16[4,192,1152]{2,1,0:T(8,128)(2,1)S(1)} custom-call(s32[12]{0:T(128)S(1)} %get-tuple-element.22.pick_ref, s32[1]{0:T(128)} %bitcast.core_ref, bf16[1024,2304]{1,0:T(8,128)(2,1)} %bitcast.7.refs_0_.refs_1_.refs_2_, bf16[1024,2304]{1,0:T(8,128)(2,1)} %bitcast.7.refs_0_.refs_1_.refs_2_, ...), custom_call_target="tpu_custom_call" | custom-call | tf_op jit(solution)/shard_map/pallas_call | solution.py:172
  32.2 1.7 %collective-permute-start.8 = (bf16[1,128,384]{2,1,0:T(8,128)(2,1)S(1)}, bf16[1,128,384]{2,1,0:T(8,128)(2,1)S(1)}, u32[]{:S(2)}, u32[]{:S(2)}) collective-permute-start(bf16[1,128,384]{2,1,0:T(8,128)(2,1)S(1)} %add_convert_fusion.2), channel_id=1, source_target_pairs={{0,2},{2,0},{1,3},{3,1},{4,6},{6,4},{5,7},{7,5},{8,10},{10,8},{9,1... | collective-permute-start | bytes 294920 | tf_op jit(solution)/shard_map/ppermute | solution.py:19
  33.9 0.1 add_convert_fusion
  34.0 0.4 collective-permute-start.4
  34.4 3.0 %collective-permute-done.11.refs_0_ = bf16[128,1152]{1,0:T(8,128)(2,1)S(1)} collective-permute-done((bf16[128,1152]{1,0:T(8,128)(2,1)S(1)}, bf16[128,1152]{1,0:T(8,128)(2,1)S(1)}, u32[]{:S(2)}, u32[]{:S(2)}) %collective-permute-start.11) | collective-permute-done | bytes 294944 | tf_op jit(solution)/shard_map/ppermute | solution.py:19
  37.4 0.4 shard_map.96
  37.8 0.1 collective-permute-start.12
  37.9 0.5 shard_map.95
  38.4 2.9 %collective-permute-start.9 = (bf16[128,1152]{1,0:T(8,128)(2,1)S(1)}, bf16[128,1152]{1,0:T(8,128)(2,1)S(1)}, u32[]{:S(2)}, u32[]{:S(2)}) collective-permute-start(bf16[128,1152]{1,0:T(8,128)(2,1)S(1)} %get-tuple-element.29), channel_id=1, source_target_pairs={{0,8},{4,12},{8,0},{12,4},{1,9},{5,13},{9,1},{13,5},{2,10},{6,14},... | collective-permute-start | bytes 884744 | tf_op jit(solution)/shard_map/ppermute | solution.py:19
  41.3 1.6 %collective-permute-start.13 = (bf16[1,128,384]{2,1,0:T(8,128)(2,1)S(1)}, bf16[1,128,384]{2,1,0:T(8,128)(2,1)S(1)}, u32[]{:S(2)}, u32[]{:S(2)}) collective-permute-start(bf16[1,128,384]{2,1,0:T(8,128)(2,1)S(1)} %add_convert_fusion.1), channel_id=1, source_target_pairs={{0,2},{2,0},{1,3},{3,1},{4,6},{6,4},{5,7},{7,5},{8,10},{10,8},{9,1... | collective-permute-start | bytes 294920 | tf_op jit(solution)/shard_map/ppermute | solution.py:19
  42.9 0.0 copy-start
  42.9 0.6 shard_map.93
  43.6 0.1 collective-permute-start.10
  43.7 2.3 %collective-permute-done.13 = bf16[1,128,384]{2,1,0:T(8,128)(2,1)S(1)} collective-permute-done((bf16[1,128,384]{2,1,0:T(8,128)(2,1)S(1)}, bf16[1,128,384]{2,1,0:T(8,128)(2,1)S(1)}, u32[]{:S(2)}, u32[]{:S(2)}) %collective-permute-start.13) | collective-permute-done | bytes 98336 | tf_op jit(solution)/shard_map/ppermute | solution.py:19
  46.0 0.5 shard_map.97
  46.5 1.0 %collective-permute-start.14 = (bf16[64,1152]{1,0:T(8,128)(2,1)S(1)}, bf16[64,1152]{1,0:T(8,128)(2,1)S(1)}, u32[]{:S(2)}, u32[]{:S(2)}) collective-permute-start(bf16[64,1152]{1,0:T(8,128)(2,1)S(1)} %get-tuple-element.31), channel_id=1, source_target_pairs={{0,12},{4,8},{8,4},{12,0},{1,13},{5,9},{9,5},{13,1},{2,14},{6,10},... | collective-permute-start | bytes 442376 | tf_op jit(solution)/shard_map/ppermute | solution.py:19
  47.5 2.9 %collective-permute-start.15 = (bf16[64,1152]{1,0:T(8,128)(2,1)S(1)}, bf16[64,1152]{1,0:T(8,128)(2,1)S(1)}, u32[]{:S(2)}, u32[]{:S(2)}) collective-permute-start(bf16[64,1152]{1,0:T(8,128)(2,1)S(1)} %get-tuple-element.32), channel_id=1, source_target_pairs={{0,12},{4,8},{8,4},{12,0},{1,13},{5,9},{9,5},{13,1},{2,14},{6,10},... | collective-permute-start | bytes 442376 | tf_op jit(solution)/shard_map/ppermute | solution.py:19
  50.4 5.4 %collective-permute-done.9.refs_0_ = bf16[128,1152]{1,0:T(8,128)(2,1)S(1)} collective-permute-done((bf16[128,1152]{1,0:T(8,128)(2,1)S(1)}, bf16[128,1152]{1,0:T(8,128)(2,1)S(1)}, u32[]{:S(2)}, u32[]{:S(2)}) %collective-permute-start.9) | collective-permute-done | bytes 294944 | tf_op jit(solution)/shard_map/ppermute | solution.py:19
  55.7 3.3 %collective-permute-done.14.refs_2_ = bf16[64,1152]{1,0:T(8,128)(2,1)S(1)} collective-permute-done((bf16[64,1152]{1,0:T(8,128)(2,1)S(1)}, bf16[64,1152]{1,0:T(8,128)(2,1)S(1)}, u32[]{:S(2)}, u32[]{:S(2)}) %collective-permute-start.14) | collective-permute-done | bytes 147488 | tf_op jit(solution)/shard_map/ppermute | solution.py:19
  59.0 4.5 %collective-permute-done.10.refs_1_ = bf16[128,1152]{1,0:T(8,128)(2,1)S(1)} collective-permute-done((bf16[128,1152]{1,0:T(8,128)(2,1)S(1)}, bf16[128,1152]{1,0:T(8,128)(2,1)S(1)}, u32[]{:S(2)}, u32[]{:S(2)}) %collective-permute-start.10) | collective-permute-done | bytes 294944 | tf_op jit(solution)/shard_map/ppermute | solution.py:19
  63.5 0.1 shard_map.98.refs_0_.error_ref
  63.6 2.1 %collective-permute-start.20 = (bf16[64,1152]{1,0:T(8,128)(2,1)S(1)}, bf16[64,1152]{1,0:T(8,128)(2,1)S(1)}, u32[]{:S(2)}, u32[]{:S(2)}) collective-permute-start(bf16[64,1152]{1,0:T(8,128)(2,1)S(1)} %shard_map.98.refs_0_.error_ref), channel_id=1, source_target_pairs={{0,8},{4,12},{8,0},{12,4},{1,9},{5,13},{9,1},{13,5},{2,10},{6,14},... | collective-permute-start | bytes 442376 | tf_op jit(solution)/shard_map/ppermute | solution.py:19
  65.7 0.1 shard_map.99.refs_1_.error_ref
  65.8 7.8 %collective-permute-start.21 = (bf16[64,1152]{1,0:T(8,128)(2,1)S(1)}, bf16[64,1152]{1,0:T(8,128)(2,1)S(1)}, u32[]{:S(2)}, u32[]{:S(2)}) collective-permute-start(bf16[64,1152]{1,0:T(8,128)(2,1)S(1)} %shard_map.99.refs_1_.error_ref), channel_id=1, source_target_pairs={{0,8},{4,12},{8,0},{12,4},{1,9},{5,13},{9,1},{13,5},{2,10},{6,14},... | collective-permute-start | bytes 442376 | tf_op jit(solution)/shard_map/ppermute | solution.py:19
  73.6 0.1 collective-permute-start.18
  73.7 1.9 %collective-permute-start.19 = (bf16[64,1152]{1,0:T(8,128)(2,1)S(1)}, bf16[64,1152]{1,0:T(8,128)(2,1)S(1)}, u32[]{:S(2)}, u32[]{:S(2)}) collective-permute-start(bf16[64,1152]{1,0:T(8,128)(2,1)S(1)} %shard_map.99.refs_1_.error_ref), channel_id=1, source_target_pairs={{0,4},{4,0},{8,12},{12,8},{1,5},{5,1},{9,13},{13,9},{2,6},{6,2},{1... | collective-permute-start | bytes 442376 | tf_op jit(solution)/shard_map/ppermute | solution.py:19
  75.6 0.6 collective-permute-done.20.error_ref
  76.1 4.2 %collective-permute-done.21.error_ref = bf16[64,1152]{1,0:T(8,128)(2,1)S(1)} collective-permute-done((bf16[64,1152]{1,0:T(8,128)(2,1)S(1)}, bf16[64,1152]{1,0:T(8,128)(2,1)S(1)}, u32[]{:S(2)}, u32[]{:S(2)}) %collective-permute-start.21) | collective-permute-done | bytes 147488 | tf_op jit(solution)/shard_map/ppermute | solution.py:19
  80.4 0.7 collective-permute-start.23
  81.1 1.1 %collective-permute-done.18.error_ref = bf16[64,1152]{1,0:T(8,128)(2,1)S(1)} collective-permute-done((bf16[64,1152]{1,0:T(8,128)(2,1)S(1)}, bf16[64,1152]{1,0:T(8,128)(2,1)S(1)}, u32[]{:S(2)}, u32[]{:S(2)}) %collective-permute-start.18) | collective-permute-done | bytes 147488 | tf_op jit(solution)/shard_map/ppermute | solution.py:19
  82.1 0.6 shard_map.101.refs_0_
  82.7 0.6 shard_map.102.refs_1_
  83.3 0.6 shard_map.105.refs_4_
  83.9 0.6 shard_map.106.refs_5_
  84.5 0.6 shard_map.103.refs_2_
  85.1 0.2 collective-permute-done.19.error_ref
  85.3 0.6 shard_map.104.refs_3_
  85.9 1.6 %collective-permute-done.22.error_ref = bf16[64,1152]{1,0:T(8,128)(2,1)S(1)} collective-permute-done((bf16[64,1152]{1,0:T(8,128)(2,1)S(1)}, bf16[64,1152]{1,0:T(8,128)(2,1)S(1)}, u32[]{:S(2)}, u32[]{:S(2)}) %collective-permute-start.22) | collective-permute-done | bytes 147488 | tf_op jit(solution)/shard_map/ppermute | solution.py:19
  87.5 0.6 shard_map.107.refs_6_
  88.1 1.0 %collective-permute-done.23.error_ref = bf16[64,1152]{1,0:T(8,128)(2,1)S(1)} collective-permute-done((bf16[64,1152]{1,0:T(8,128)(2,1)S(1)}, bf16[64,1152]{1,0:T(8,128)(2,1)S(1)}, u32[]{:S(2)}, u32[]{:S(2)}) %collective-permute-start.23) | collective-permute-done | bytes 147488 | tf_op jit(solution)/shard_map/ppermute | solution.py:19
  89.1 0.6 shard_map.108.refs_7_
  89.7 0.1 collective-permute-start.24
  89.7 1.2 %collective-permute-done.24 = f32[4,192]{1,0:T(4,128)S(1)} collective-permute-done((f32[4,192]{1,0:T(4,128)S(1)}, f32[4,192]{1,0:T(4,128)S(1)}, u32[]{:S(2)}, u32[]{:S(2)}) %collective-permute-start.24) | collective-permute-done | bytes 3104 | tf_op jit(solution)/shard_map/ppermute | solution.py:19
  90.9 1.5 %collective-permute-start.25 = (f32[4,192]{1,0:T(4,128)S(1)}, f32[4,192]{1,0:T(4,128)S(1)}, u32[]{:S(2)}, u32[]{:S(2)}) collective-permute-start(f32[4,192]{1,0:T(4,128)S(1)} %add.30), channel_id=1, source_target_pairs={{0,2},{2,0},{1,3},{3,1},{4,6},{6,4},{5,7},{7,5},{8,10},{10,8},{9,1... | collective-permute-start | bytes 9224 | tf_op jit(solution)/shard_map/ppermute | solution.py:19
  92.4 0.9 shard_map.100
  93.3 1.2 %collective-permute-done.25 = f32[4,192]{1,0:T(4,128)S(1)} collective-permute-done((f32[4,192]{1,0:T(4,128)S(1)}, f32[4,192]{1,0:T(4,128)S(1)}, u32[]{:S(2)}, u32[]{:S(2)}) %collective-permute-start.25) | collective-permute-done | bytes 3104 | tf_op jit(solution)/shard_map/ppermute | solution.py:19
  94.5 1.2 %shard_map.110 = f32[8,128]{1,0:T(8,128)} custom-call(s32[12]{0:T(128)S(1)} %get-tuple-element.21.pick_ref, f32[4,192]{1,0:T(4,128)S(1)} %add.31.total_ref), custom_call_target="tpu_custom_call" | custom-call | tf_op jit(solution)/shard_map/pallas_call | solution.py:389
  (24 shorter events, 0.2 us)
Async XLA Ops:
  0.6 18.1 %collective-permute-start = (bf16[1,2304,1024]{2,1,0:T(8,128)(2,1)}, bf16[1,2304,1024]{2,1,0:T(8,128)(2,1)}, u32[]{:S(2)}, u32[]{:S(2)}) collective-permute-start(bf16[1,2304,1024]{2,1,0:T(8,128)(2,1)} %param.8), channel_id=1, source_target_pairs={{0,1},{1,0},{2,3},{3,2},{4,5},{5,4},{6,7},{7,6},{8,9},{9,8},{10,11... | collective-permute-start | bytes 14155784 | tf_op jit(solution)/shard_map/ppermute | solution.py:19
  1.1 28.0 %collective-permute-start.6 = (bf16[1,1024,2304]{2,1,0:T(8,128)(2,1)}, bf16[1,1024,2304]{2,1,0:T(8,128)(2,1)}, u32[]{:S(2)}, u32[]{:S(2)}) collective-permute-start(bf16[1,1024,2304]{2,1,0:T(8,128)(2,1)} %param.10), channel_id=1, source_target_pairs={{0,1},{1,0},{2,3},{3,2},{4,5},{5,4},{6,7},{7,6},{8,9},{9,8},{10,11... | collective-permute-start | bytes 14155784 | tf_op jit(solution)/shard_map/ppermute | solution.py:19
  2.2 16.5 %collective-permute-start.1 = (bf16[128,1152]{1,0:T(8,128)(2,1)S(1)}, bf16[128,1152]{1,0:T(8,128)(2,1)S(1)}, u32[]{:S(2)}, u32[]{:S(2)}) collective-permute-start(bf16[128,1152]{1,0:T(8,128)(2,1)S(1)} %shard_map.86.refs_0_.token_ref), channel_id=1, source_target_pairs={{0,4},{4,0},{8,12},{12,8},{1,5},{5,1},{9,13},{13,9},{2,6},{6,2},{1... | collective-permute-start | bytes 884744 | tf_op jit(solution)/shard_map/ppermute | solution.py:19
  5.3 19.1 %collective-permute-start.2 = (bf16[128,1152]{1,0:T(8,128)(2,1)S(1)}, bf16[128,1152]{1,0:T(8,128)(2,1)S(1)}, u32[]{:S(2)}, u32[]{:S(2)}) collective-permute-start(bf16[128,1152]{1,0:T(8,128)(2,1)S(1)} %shard_map.86.refs_0_.token_ref), channel_id=1, source_target_pairs={{0,8},{4,12},{8,0},{12,4},{1,9},{5,13},{9,1},{13,5},{2,10},{6,14},... | collective-permute-start | bytes 884744 | tf_op jit(solution)/shard_map/ppermute | solution.py:19
  24.8 7.4 %collective-permute-start.7 = (bf16[1,128,384]{2,1,0:T(8,128)(2,1)S(1)}, bf16[1,128,384]{2,1,0:T(8,128)(2,1)S(1)}, u32[]{:S(2)}, u32[]{:S(2)}) collective-permute-start(bf16[1,128,384]{2,1,0:T(8,128)(2,1)S(1)} %shard_map.94), channel_id=1, source_target_pairs={{0,1},{1,0},{2,3},{3,2},{4,5},{5,4},{6,7},{7,6},{8,9},{9,8},{10,11... | collective-permute-start | bytes 294920 | tf_op jit(solution)/shard_map/ppermute | solution.py:19
  24.8 13.1 %collective-permute-start.5 = (f32[4,192]{1,0:T(4,128)S(1)}, f32[4,192]{1,0:T(4,128)S(1)}, u32[]{:S(2)}, u32[]{:S(2)}) collective-permute-start(f32[4,192]{1,0:T(4,128)S(1)} %get-tuple-element.26.refs_1_), channel_id=1, source_target_pairs={{0,1},{1,0},{2,3},{3,2},{4,5},{5,4},{6,7},{7,6},{8,9},{9,8},{10,11... | collective-permute-start | bytes 9224 | tf_op jit(solution)/shard_map/ppermute | solution.py:19
  28.4 9.0 %collective-permute-start.11 = (bf16[128,1152]{1,0:T(8,128)(2,1)S(1)}, bf16[128,1152]{1,0:T(8,128)(2,1)S(1)}, u32[]{:S(2)}, u32[]{:S(2)}) collective-permute-start(bf16[128,1152]{1,0:T(8,128)(2,1)S(1)} %collective-permute-done.2.refs_0_), channel_id=1, source_target_pairs={{0,4},{4,0},{8,12},{12,8},{1,5},{5,1},{9,13},{13,9},{2,6},{6,2},{1... | collective-permute-start | bytes 884744 | tf_op jit(solution)/shard_map/ppermute | solution.py:19
  29.0 4.9 %collective-permute-start.3 = (bf16[2,128,384]{2,1,0:T(8,128)(2,1)S(1)}, bf16[2,128,384]{2,1,0:T(8,128)(2,1)S(1)}, u32[]{:S(2)}, u32[]{:S(2)}) collective-permute-start(bf16[2,128,384]{2,1,0:T(8,128)(2,1)S(1)} %shard_map.90), channel_id=1, source_target_pairs={{0,1},{1,0},{2,3},{3,2},{4,5},{5,4},{6,7},{7,6},{8,9},{9,8},{10,11... | collective-permute-start | bytes 589832 | tf_op jit(solution)/shard_map/ppermute | solution.py:19
  32.2 5.7 %collective-permute-start.8 = (bf16[1,128,384]{2,1,0:T(8,128)(2,1)S(1)}, bf16[1,128,384]{2,1,0:T(8,128)(2,1)S(1)}, u32[]{:S(2)}, u32[]{:S(2)}) collective-permute-start(bf16[1,128,384]{2,1,0:T(8,128)(2,1)S(1)} %add_convert_fusion.2), channel_id=1, source_target_pairs={{0,2},{2,0},{1,3},{3,1},{4,6},{6,4},{5,7},{7,5},{8,10},{10,8},{9,1... | collective-permute-start | bytes 294920 | tf_op jit(solution)/shard_map/ppermute | solution.py:19
  34.0 8.9 %collective-permute-start.4 = (bf16[2,128,384]{2,1,0:T(8,128)(2,1)S(1)}, bf16[2,128,384]{2,1,0:T(8,128)(2,1)S(1)}, u32[]{:S(2)}, u32[]{:S(2)}) collective-permute-start(bf16[2,128,384]{2,1,0:T(8,128)(2,1)S(1)} %add_convert_fusion), channel_id=1, source_target_pairs={{0,2},{2,0},{1,3},{3,1},{4,6},{6,4},{5,7},{7,5},{8,10},{10,8},{9,1... | collective-permute-start | bytes 589832 | tf_op jit(solution)/shard_map/ppermute | solution.py:19
  37.8 3.5 %collective-permute-start.12 = (bf16[1,128,384]{2,1,0:T(8,128)(2,1)S(1)}, bf16[1,128,384]{2,1,0:T(8,128)(2,1)S(1)}, u32[]{:S(2)}, u32[]{:S(2)}) collective-permute-start(bf16[1,128,384]{2,1,0:T(8,128)(2,1)S(1)} %shard_map.96), channel_id=1, source_target_pairs={{0,1},{1,0},{2,3},{3,2},{4,5},{5,4},{6,7},{7,6},{8,9},{9,8},{10,11... | collective-permute-start | bytes 294920 | tf_op jit(solution)/shard_map/ppermute | solution.py:19
  38.4 17.3 %collective-permute-start.9 = (bf16[128,1152]{1,0:T(8,128)(2,1)S(1)}, bf16[128,1152]{1,0:T(8,128)(2,1)S(1)}, u32[]{:S(2)}, u32[]{:S(2)}) collective-permute-start(bf16[128,1152]{1,0:T(8,128)(2,1)S(1)} %get-tuple-element.29), channel_id=1, source_target_pairs={{0,8},{4,12},{8,0},{12,4},{1,9},{5,13},{9,1},{13,5},{2,10},{6,14},... | collective-permute-start | bytes 884744 | tf_op jit(solution)/shard_map/ppermute | solution.py:19
  41.3 4.7 %collective-permute-start.13 = (bf16[1,128,384]{2,1,0:T(8,128)(2,1)S(1)}, bf16[1,128,384]{2,1,0:T(8,128)(2,1)S(1)}, u32[]{:S(2)}, u32[]{:S(2)}) collective-permute-start(bf16[1,128,384]{2,1,0:T(8,128)(2,1)S(1)} %add_convert_fusion.1), channel_id=1, source_target_pairs={{0,2},{2,0},{1,3},{3,1},{4,6},{6,4},{5,7},{7,5},{8,10},{10,8},{9,1... | collective-permute-start | bytes 294920 | tf_op jit(solution)/shard_map/ppermute | solution.py:19
  42.9 20.6 %copy-start = (f32[1,2304]{1,0:T(1,128)S(1)}, f32[1,2304]{1,0:T(1,128)}, u32[]{:S(2)}) copy-start(f32[1,2304]{1,0:T(1,128)} %bias_ref.3) | copy-start | bytes 27652
  43.6 19.9 %collective-permute-start.10 = (bf16[128,1152]{1,0:T(8,128)(2,1)S(1)}, bf16[128,1152]{1,0:T(8,128)(2,1)S(1)}, u32[]{:S(2)}, u32[]{:S(2)}) collective-permute-start(bf16[128,1152]{1,0:T(8,128)(2,1)S(1)} %get-tuple-element.30), channel_id=1, source_target_pairs={{0,4},{4,0},{8,12},{12,8},{1,5},{5,1},{9,13},{13,9},{2,6},{6,2},{1... | collective-permute-start | bytes 884744 | tf_op jit(solution)/shard_map/ppermute | solution.py:19
  46.5 12.5 %collective-permute-start.14 = (bf16[64,1152]{1,0:T(8,128)(2,1)S(1)}, bf16[64,1152]{1,0:T(8,128)(2,1)S(1)}, u32[]{:S(2)}, u32[]{:S(2)}) collective-permute-start(bf16[64,1152]{1,0:T(8,128)(2,1)S(1)} %get-tuple-element.31), channel_id=1, source_target_pairs={{0,12},{4,8},{8,4},{12,0},{1,13},{5,9},{9,5},{13,1},{2,14},{6,10},... | collective-permute-start | bytes 442376 | tf_op jit(solution)/shard_map/ppermute | solution.py:19
  47.5 18.2 %collective-permute-start.15 = (bf16[64,1152]{1,0:T(8,128)(2,1)S(1)}, bf16[64,1152]{1,0:T(8,128)(2,1)S(1)}, u32[]{:S(2)}, u32[]{:S(2)}) collective-permute-start(bf16[64,1152]{1,0:T(8,128)(2,1)S(1)} %get-tuple-element.32), channel_id=1, source_target_pairs={{0,12},{4,8},{8,4},{12,0},{1,13},{5,9},{9,5},{13,1},{2,14},{6,10},... | collective-permute-start | bytes 442376 | tf_op jit(solution)/shard_map/ppermute | solution.py:19
  63.6 12.5 %collective-permute-start.20 = (bf16[64,1152]{1,0:T(8,128)(2,1)S(1)}, bf16[64,1152]{1,0:T(8,128)(2,1)S(1)}, u32[]{:S(2)}, u32[]{:S(2)}) collective-permute-start(bf16[64,1152]{1,0:T(8,128)(2,1)S(1)} %shard_map.98.refs_0_.error_ref), channel_id=1, source_target_pairs={{0,8},{4,12},{8,0},{12,4},{1,9},{5,13},{9,1},{13,5},{2,10},{6,14},... | collective-permute-start | bytes 442376 | tf_op jit(solution)/shard_map/ppermute | solution.py:19
  65.8 14.6 %collective-permute-start.21 = (bf16[64,1152]{1,0:T(8,128)(2,1)S(1)}, bf16[64,1152]{1,0:T(8,128)(2,1)S(1)}, u32[]{:S(2)}, u32[]{:S(2)}) collective-permute-start(bf16[64,1152]{1,0:T(8,128)(2,1)S(1)} %shard_map.99.refs_1_.error_ref), channel_id=1, source_target_pairs={{0,8},{4,12},{8,0},{12,4},{1,9},{5,13},{9,1},{13,5},{2,10},{6,14},... | collective-permute-start | bytes 442376 | tf_op jit(solution)/shard_map/ppermute | solution.py:19
  73.6 8.6 %collective-permute-start.18 = (bf16[64,1152]{1,0:T(8,128)(2,1)S(1)}, bf16[64,1152]{1,0:T(8,128)(2,1)S(1)}, u32[]{:S(2)}, u32[]{:S(2)}) collective-permute-start(bf16[64,1152]{1,0:T(8,128)(2,1)S(1)} %shard_map.98.refs_0_.error_ref), channel_id=1, source_target_pairs={{0,4},{4,0},{8,12},{12,8},{1,5},{5,1},{9,13},{13,9},{2,6},{6,2},{1... | collective-permute-start | bytes 442376 | tf_op jit(solution)/shard_map/ppermute | solution.py:19
  73.7 11.6 %collective-permute-start.19 = (bf16[64,1152]{1,0:T(8,128)(2,1)S(1)}, bf16[64,1152]{1,0:T(8,128)(2,1)S(1)}, u32[]{:S(2)}, u32[]{:S(2)}) collective-permute-start(bf16[64,1152]{1,0:T(8,128)(2,1)S(1)} %shard_map.99.refs_1_.error_ref), channel_id=1, source_target_pairs={{0,4},{4,0},{8,12},{12,8},{1,5},{5,1},{9,13},{13,9},{2,6},{6,2},{1... | collective-permute-start | bytes 442376 | tf_op jit(solution)/shard_map/ppermute | solution.py:19
  76.1 11.4 %collective-permute-start.22 = (bf16[64,1152]{1,0:T(8,128)(2,1)S(1)}, bf16[64,1152]{1,0:T(8,128)(2,1)S(1)}, u32[]{:S(2)}, u32[]{:S(2)}) collective-permute-start(bf16[64,1152]{1,0:T(8,128)(2,1)S(1)} %collective-permute-done.20.error_ref), channel_id=1, source_target_pairs={{0,4},{4,0},{8,12},{12,8},{1,5},{5,1},{9,13},{13,9},{2,6},{6,2},{1... | collective-permute-start | bytes 442376 | tf_op jit(solution)/shard_map/ppermute | solution.py:19
  80.4 8.7 %collective-permute-start.23 = (bf16[64,1152]{1,0:T(8,128)(2,1)S(1)}, bf16[64,1152]{1,0:T(8,128)(2,1)S(1)}, u32[]{:S(2)}, u32[]{:S(2)}) collective-permute-start(bf16[64,1152]{1,0:T(8,128)(2,1)S(1)} %collective-permute-done.21.error_ref), channel_id=1, source_target_pairs={{0,4},{4,0},{8,12},{12,8},{1,5},{5,1},{9,13},{13,9},{2,6},{6,2},{1... | collective-permute-start | bytes 442376 | tf_op jit(solution)/shard_map/ppermute | solution.py:19
  81.1 11.3 %collective-permute-start.16 = (bf16[64,1152]{1,0:T(8,128)(2,1)S(1)}, bf16[64,1152]{1,0:T(8,128)(2,1)S(1)}, u32[]{:S(2)}, u32[]{:S(2)}) collective-permute-start(bf16[64,1152]{1,0:T(8,128)(2,1)S(1)} %shard_map.98.refs_0_.error_ref), channel_id=1, source_target_pairs={{0,1},{1,0},{2,3},{3,2},{4,5},{5,4},{6,7},{7,6},{8,9},{9,8},{10,11... | collective-permute-start | bytes 442376 | tf_op jit(solution)/shard_map/ppermute | solution.py:19
  82.1 10.3 %collective-permute-start.17 = (bf16[64,1152]{1,0:T(8,128)(2,1)S(1)}, bf16[64,1152]{1,0:T(8,128)(2,1)S(1)}, u32[]{:S(2)}, u32[]{:S(2)}) collective-permute-start(bf16[64,1152]{1,0:T(8,128)(2,1)S(1)} %shard_map.99.refs_1_.error_ref), channel_id=1, source_target_pairs={{0,1},{1,0},{2,3},{3,2},{4,5},{5,4},{6,7},{7,6},{8,9},{9,8},{10,11... | collective-permute-start | bytes 442376 | tf_op jit(solution)/shard_map/ppermute | solution.py:19
  89.7 1.2 %collective-permute-start.24 = (f32[4,192]{1,0:T(4,128)S(1)}, f32[4,192]{1,0:T(4,128)S(1)}, u32[]{:S(2)}, u32[]{:S(2)}) collective-permute-start(f32[4,192]{1,0:T(4,128)S(1)} %get-tuple-element.37), channel_id=1, source_target_pairs={{0,1},{1,0},{2,3},{3,2},{4,5},{5,4},{6,7},{7,6},{8,9},{9,8},{10,11... | collective-permute-start | bytes 9224 | tf_op jit(solution)/shard_map/ppermute | solution.py:19
  90.9 3.6 %collective-permute-start.25 = (f32[4,192]{1,0:T(4,128)S(1)}, f32[4,192]{1,0:T(4,128)S(1)}, u32[]{:S(2)}, u32[]{:S(2)}) collective-permute-start(f32[4,192]{1,0:T(4,128)S(1)} %add.30), channel_id=1, source_target_pairs={{0,2},{2,0},{1,3},{3,1},{4,6},{6,4},{5,7},{7,5},{8,10},{10,8},{9,1... | collective-permute-start | bytes 9224 | tf_op jit(solution)/shard_map/ppermute | solution.py:19

commit v4 on v3

--- a/solution.py
+++ b/solution.py
@@ -19,17 +19,15 @@
     return lax.ppermute(value, axis, [(i, i ^ mask) for i in range(size)])
 
 
+def swap_both(value, mask):
+    size = lax.axis_size("layer")
+    pairs = [(2 * i + c, 2 * (i ^ mask) + 1 - c) for i in range(size) for c in range(2)]
+    return lax.ppermute(value, ("layer", "tok"), pairs)
+
+
 def masks_of(axis):
     size = lax.axis_size(axis)
     return [1 << i for i in range(size.bit_length() - 1)]
-
-
-def spread(value):
-    have = {0: value}
-    for mask in reversed(masks_of("lat")):
-        for offset in list(have):
-            have[offset ^ mask] = swap(have[offset], "lat", mask)
-    return have
 
 
 def sum_layers(value):
@@ -73,6 +71,8 @@
     latents = bias.shape[0]
     device_blocks = latents // LATBLK
     wide = 2 * LATBLK
+    shift = device_blocks.bit_length() - 1
+    assert device_blocks == 1 << shift
 
     def body(ids_ref, counts_ref, places_ref, bias_ref, own_ref, other_ref, out_ref):
         place, core = places_ref[0], places_ref[1]
@@ -85,8 +85,8 @@
 
             def step(slot, found):
                 chosen = ids_ref[block, slot]
-                shard = lax.div(chosen, device_blocks)
-                local = lax.rem(chosen, device_blocks)
+                shard = lax.shift_right_logical(chosen, shift)
+                local = chosen & (device_blocks - 1)
                 live = slot < counts_ref[block]
                 new = []
                 for i, pick_ref in enumerate(pick_refs):
@@ -100,7 +100,7 @@
                     new.append(found[i] + mine.astype(jnp.int32))
                 return tuple(new)
 
-            lax.fori_loop(0, slot_total, step, (jnp.int32(0), jnp.int32(0)))
+            lax.fori_loop(0, slot_total, step, (jnp.int32(0), jnp.int32(0)), unroll=8)
         for offset in range(block_total):
             for s in range(CAP):
                 chosen = own_ref[offset * CAP + s]
@@ -130,11 +130,19 @@
 
     def body(pick_ref, core_ref, *refs):
         step = pl.program_id(0)
+        placed = []
         for s in range(CAP):
             odd = lax.rem(jnp.maximum(pick_ref[step * CAP + s], 0), 2)
             wide = refs[s][...]
-            left, right = wide[:, :LATBLK], wide[:, LATBLK:]
-            refs[CAP][:, s * LATBLK : (s + 1) * LATBLK] = jnp.where(odd == 1, right, left)
+            turned = jnp.concatenate([wide[:, LATBLK:], wide[:, :LATBLK]], axis=1)
+            placed.append(jnp.where(odd == s % 2, wide, turned))
+        low = lax.broadcasted_iota(jnp.int32, placed[0].shape, 1) < LATBLK
+        for s in range(0, CAP - 1, 2):
+            refs[CAP][:, s * LATBLK : (s + 2) * LATBLK] = jnp.where(
+                low, placed[s], placed[s + 1]
+            )
+        if CAP % 2:
+            refs[CAP][:, (CAP - 1) * LATBLK :] = placed[-1][:, :LATBLK]
 
     def spec(s):
         return pl.BlockSpec(
@@ -264,7 +272,7 @@
                 part_ref[...] = total[r * step : (r + 1) * step].astype(part_ref.dtype)
 
     shapes = [
-        jax.ShapeDtypeStruct((rows // split, half), jnp.bfloat16 if offset else jnp.float32)
+        jax.ShapeDtypeStruct((rows // split, half), jnp.bfloat16 if offset % 2 else jnp.float32)
         for offset, split in zip(offsets, splits)
         for _ in range(split)
     ]
@@ -286,6 +294,22 @@
     for offset, split in zip(offsets, splits):
         by_offset[offset], parts = parts[:split], parts[split:]
     return code, by_offset
+
+
+def added(part, arrived):
+    def body(part_ref, arrived_ref, out_ref):
+        total = part_ref[...].astype(jnp.float32) + arrived_ref[...].astype(jnp.float32)
+        out_ref[...] = total.astype(jnp.bfloat16)
+
+    return pl.pallas_call(
+        body,
+        grid=(1,),
+        in_specs=[whole(part.shape)] * 2,
+        out_specs=whole(part.shape),
+        out_shape=jax.ShapeDtypeStruct(part.shape, jnp.bfloat16),
+        compiler_params=PARAMS,
+        cost_estimate=SMALL,
+    )(part, arrived)
 
 
 def remainder(part, arrived, bias, tokens, core, r, rows):
@@ -447,68 +471,102 @@
     own_pick, other_pick, bias_own = plan(
         block_ids, counts, jnp.stack([place, core]).astype(jnp.int32), b_enc
     )
-    enc_own = encoder_slots(w_enc[0], own_pick, core_at)
-    enc_swapped, near_tokens = lax.optimization_barrier((swap(w_enc, "tok", 1), near_tokens))
-    enc_two = [enc_own, encoder_slots(enc_swapped[0], other_pick, core_at)]
-    token_blocks = {0: own_half, 1: near_tokens}
+    enc_two = [
+        encoder_slots(w_enc[0], own_pick, core_at),
+        encoder_slots(swap(w_enc, "tok", 1)[0], other_pick, core_at),
+    ]
+    dec_own = decoder_slots(w_dec[0], own_pick, core_at)
+    biases = (bias_own, swap(bias_own, "tok", 1))
+    token_blocks = {0: own_half, 1: swap(own_half, "lat", 1)}
     for mask in reversed(masks_of("lat")):
         if mask > 1:
             for offset in [o for o in token_blocks if o % 2 == 0]:
                 token_blocks[offset ^ mask] = swap(token_blocks[offset], "lat", mask)
-    even_tokens, enc_two = lax.optimization_barrier(
-        ([token_blocks[o] for o in evens], enc_two)
+    even_tokens, enc_two, dec_own, biases = lax.optimization_barrier(
+        ([token_blocks[o] for o in evens], enc_two, dec_own, biases)
     )
     for offset, value in zip(evens, even_tokens):
         token_blocks[offset] = value
         token_blocks[offset ^ 1] = swap(value, "lat", 1)
-    biases = (bias_own, swap(bias_own, "tok", 1))
 
     def encoded(offsets):
         return encode([token_blocks[o] for o in offsets], enc_two, offsets, core_at)
 
-    def forward(term, offsets, split):
-        other = swap(term, "tok", 1)
-        both = (term.astype(f32) + other.astype(f32)).astype(bf16)
-        pre = sum_layers(both)
-        code, parts = decode(
-            pre, biases, dec_two, offsets, [split] * len(offsets), core_at
+    def both_cores(term, other):
+        return (term.astype(f32) + other.astype(f32)).astype(bf16)
+
+    def summed(term, other):
+        return sum_layers(both_cores(term, other))
+
+    def forward(pre, offsets, splits):
+        return decode(pre, biases, dec_two, offsets, splits, core_at)
+
+    first, far = [*evens, 1], odds[1:]
+    own_term, first_term = encoded([0]), encoded(first)
+    first_other = swap(first_term, "tok", 1)
+    w_dec_other, first_other = lax.optimization_barrier((swap(w_dec, "tok", 1), first_other))
+    dec_two = [dec_own, decoder_slots(w_dec_other[0], other_pick, core_at)]
+    far_tokens, dec_two = lax.optimization_barrier(([token_blocks[o] for o in far], dec_two))
+    token_blocks.update(zip(far, far_tokens))
+    first_code, first_parts = forward(
+        summed(first_term, first_other), first, [ROW_PARTS] * len(evens) + [1]
+    )
+    far_term = encoded(far)
+    far_sum = summed(far_term, swap(far_term, "tok", 1))
+    far_code, far_parts = forward(far_sum, far, [ROW_PARTS] * len(far))
+
+    far_sums = [{o - 1: swap(far_parts[o][r], "lat", 1) for o in far} for r in range(ROW_PARTS)]
+    own_both = both_cores(own_term, swap(own_term, "tok", 1))
+    own_both, near_part, far_sums[0] = lax.optimization_barrier(
+        (own_both, first_parts[1][0], far_sums[0])
+    )
+    near_sum = swap(near_part, "lat", 1)
+    own_code, own_parts = forward(sum_layers(own_both), [0], [1])
+    codes = {
+        o: (code, at)
+        for code, offsets in ((first_code, first), (far_code, far), (own_code, [0]))
+        for at, o in enumerate(offsets)
+    }
+    halves = []
+    for r in range(ROW_PARTS):
+        arrived = [near_sum]
+        held = {o: added(first_parts[o][r], far_sums[r][o]) for o in evens}
+        for mask in masks_of("lat")[1:]:
+            for o in sorted(held):
+                if o & mask:
+                    value = swap(held.pop(o), "lat", mask)
+                    if o == mask:
+                        arrived.append(value)
+                    else:
+                        held[o ^ mask] = added(held[o ^ mask], value)
+        halves.append(
+            remainder(
+                own_parts[0][0], arrived, b_dec, own_half, core_at, r, own_rows // ROW_PARTS
+            )
         )
-        return {o: (code, at) for at, o in enumerate(offsets)}, parts
-
-    dec_two = [
-        decoder_slots(w_dec[0], own_pick, core_at),
-        decoder_slots(swap(w_dec, "tok", 1)[0], other_pick, core_at),
-    ]
-    codes, parts = {}, {}
-    for offsets, split in ((evens, 1), ([0, 1], 1), (odds[1:], ROW_PARTS)):
-        code, part = forward(encoded(offsets), offsets, split)
-        codes.update(code)
-        parts.update(part)
-
-    arrived = {
-        o: [swap(part, "lat", o) for part in parts[o]] for o in [*evens, *odds]
-    }
-    halves = [
-        remainder(
-            parts[0][0],
-            [value[r if len(value) > 1 else 0] for value in arrived.values()],
-            b_dec,
-            own_half,
-            core_at,
-            r,
-            own_rows // ROW_PARTS,
-        )
-        for r in range(ROW_PARTS)
-    ]
 
     terms = [[] for _ in range(lat_size)]
+    before = None
     for r in range(ROW_PARTS):
-        for o, error in spread(halves[r]).items():
+        errors = {0: halves[r]}
+        for mask in reversed(masks_of("lat")):
+            sources = dict(errors)
+            if mask == 1:
+                errors[1] = swap(sources.pop(0), "lat", 1)
+                last = max(sources)
+                sources[last], errors[1], before = lax.optimization_barrier(
+                    (sources[last], errors[1], before)
+                )
+            for o, error in sources.items():
+                errors[o ^ mask] = swap(error, "lat", mask)
+        before = errors[lat_size - 1]
+        for o, error in errors.items():
             terms[o].append(gradient(error, *codes[o], r, dec_two, o))
     own_sum, other_sum = gathered(terms)
-    scale_grad = by_latent(
-        sum_layers(own_sum + swap(other_sum, "tok", 1)), own_pick, latents_here
-    )
+    total = own_sum + swap(other_sum, "tok", 1)
+    for mask in range(1, lax.axis_size("layer")):
+        total = total + swap(own_sum, "layer", mask) + swap_both(other_sum, mask)
+    scale_grad = by_latent(total, own_pick, latents_here)
     residual = side_by_side(halves, [swap(half, "tok", 1) for half in halves], core_at)
     return residual.reshape(tokens.shape), scale_grad
 

time: 96.7 us -> 88 us (0.910)
  starting transfers between devices: 31.8 us -> 23.2 us
  waiting for transfers between devices: 32.6 us -> 36 us
  Pallas kernels: 30.3 us -> 27.3 us
    ppermute x26 -> x27, starting transfers between devices: 31.8 us -> 23.2 us  [swap(): return lax.ppermute(value, axis, [(i, i ^ mask) for i in range(size)])]
    pallas_call x2, Pallas kernels: 11 us -> 8.24 us  [encoder_slots(): pl.pallas_call(body, grid_spec=pltpu.PrefetchScalarGridSpec(num_scalar_pr...]
    ppermute x26 -> x27, waiting for transfers between devices: 32.6 us -> 35.1 us  [swap(): return lax.ppermute(value, axis, [(i, i ^ mask) for i in range(size)])]
  transfers between devices with their start and end apart: 26 -> 28, of which waited for: 14 -> 16; matrix products, arithmetic and copies ran while one was open for 0% -> 0% of each run, Pallas kernels for 30% -> 30%
where the time goes in v4:
time: 88 us; the launch traced here: 87.6 us
  waiting for transfers between devices  36 us (41%)
  Pallas kernels  27.3 us (31%)
  starting transfers between devices  23.2 us (26%)
    ppermute x27, waiting for transfers between devices, swap(): return lax.ppermute(value, axis, [(i, i ^ mask) for i in range(size)])  35.1 us
    ppermute x27, starting transfers between devices, swap(): return lax.ppermute(value, axis, [(i, i ^ mask) for i in range(size)])  23.2 us
    pallas_call x2, Pallas kernels, encoder_slots(): pl.pallas_call(body, grid_spec=pltpu.PrefetchScalarGridSpec(num_scalar_pr...  8.24 us
    pallas_call x2, Pallas kernels, decoder_slots(): pl.pallas_call(body, grid_spec=pltpu.PrefetchScalarGridSpec(num_scalar_pr...  6.09 us
    pallas_call x8, Pallas kernels, gradient(): pl.pallas_call(body, grid=(1,), in_specs=[whole((rows, half)), pl.BlockSp...  4.69 us
    pallas_call x1, Pallas kernels, plan(): pl.pallas_call(body, grid=(1,), in_specs=[smem] * 3 + [whole((latents //...  1.96 us
  transfers between devices with their start and end apart: 28, of which 16 were waited for; matrix products, arithmetic and copies ran while one was open for 0% of the time, Pallas kernels for 30%

profile of v4, /device:TPU:0, one launch (start us, length us, event | category | flops | bytes accessed | tf_op | source)
XLA Modules:
  0.0 87.6 jit_solution(18293513277820724169)
XLA Ops:
  0.6 0.5 collective-permute-start.1
  1.1 0.1 collective-permute-start.5
  1.2 1.0 %shard_map.86.refs_0_.token_ref = bf16[128,1152]{1,0:T(8,128)(2,1)S(1)} custom-call(s32[1]{0:T(128)} %bitcast.core_ref, bf16[128,2304]{1,0:T(8,128)(2,1)} %bitcast.16), custom_call_target="tpu_custom_call" | custom-call | tf_op jit(solution)/shard_map/pallas_call | solution.py:55
  2.2 4.1 %collective-permute-start = (bf16[128,1152]{1,0:T(8,128)(2,1)S(1)}, bf16[128,1152]{1,0:T(8,128)(2,1)S(1)}, u32[]{:S(2)}, u32[]{:S(2)}) collective-permute-start(bf16[128,1152]{1,0:T(8,128)(2,1)S(1)} %shard_map.86.refs_0_.token_ref), channel_id=1, source_target_pairs={{0,8},{4,12},{8,0},{12,4},{1,9},{5,13},{9,1},{13,5},{2,10},{6,14},... | collective-permute-start | bytes 884744 | tf_op jit(solution)/shard_map/ppermute | solution.py:19
  6.3 1.6 %collective-permute-start.4 = (bf16[128,1152]{1,0:T(8,128)(2,1)S(1)}, bf16[128,1152]{1,0:T(8,128)(2,1)S(1)}, u32[]{:S(2)}, u32[]{:S(2)}) collective-permute-start(bf16[128,1152]{1,0:T(8,128)(2,1)S(1)} %shard_map.86.refs_0_.token_ref), channel_id=1, source_target_pairs={{0,4},{4,0},{8,12},{12,8},{1,5},{5,1},{9,13},{13,9},{2,6},{6,2},{1... | collective-permute-start | bytes 884744 | tf_op jit(solution)/shard_map/ppermute | solution.py:19
  7.9 0.1 pad_add_fusion.places_ref
  7.9 2.0 %shard_map.87 = (s32[12]{0:T(128)S(1)}, s32[12]{0:T(128)S(1)}, f32[4,192]{1,0:T(4,128)S(1)}) custom-call(s32[4,16]{1,0:T(4,128)} %ids_ref.1, s32[4]{0:T(128)} %counts_ref.1, s32[2]{0:T(128)S(1)} %pad_add_fusion.places_ref, f32[8,128]{1,0:T(8,128)} %bitcast.18), custom_call_target="tpu_custom_call" | custom-call | tf_op jit(solution)/shard_map/pallas_call | solution.py:116
  9.9 0.1 collective-permute-start.2
  10.0 3.1 %shard_map.90.refs_3_.refs_5_.own_ref = bf16[4,192,1152]{2,1,0:T(8,128)(2,1)S(1)} custom-call(s32[12]{0:T(128)S(1)} %get-tuple-element.34.pick_ref, s32[1]{0:T(128)} %bitcast.core_ref, bf16[1024,2304]{1,0:T(8,128)(2,1)} %bitcast.13, bf16[1024,2304]{1,0:T(8,128)(2,1)} %bitcast.14, bf16[1024,2304]{1,0:T(8,128)(2,1)} %bitcast.15), custom_call_target="tpu_custom_call" | custom-call | tf_op jit(solution)/shard_map/pallas_call | solution.py:180
  13.1 4.1 %shard_map.88.refs_1_.refs_2_.refs_4_ = bf16[4,1152,192]{2,1,0:T(8,128)(2,1)S(1)} custom-call(s32[12]{0:T(128)S(1)} %get-tuple-element.34.pick_ref, s32[1]{0:T(128)} %bitcast.core_ref, bf16[2304,1024]{1,0:T(8,128)(2,1)} %bitcast.10, bf16[2304,1024]{1,0:T(8,128)(2,1)} %bitcast.11, bf16[2304,1024]{1,0:T(8,128)(2,1)} %bitcast.12), custom_call_target="tpu_custom_call" | custom-call | tf_op jit(solution)/shard_map/pallas_call | solution.py:153
  17.2 4.1 %shard_map.89.refs_2_.refs_3_.refs_5_ = bf16[4,1152,192]{2,1,0:T(8,128)(2,1)S(1)} custom-call(s32[12]{0:T(128)S(1)} %get-tuple-element.35.pick_ref, s32[1]{0:T(128)} %bitcast.core_ref, bf16[2304,1024]{1,0:T(8,128)(2,1)} %bitcast.5.refs_0_.refs_1_.refs_2_, bf16[2304,1024]{1,0:T(8,128)(2,1)} %bitcast.5.refs_0_.refs_1_.refs_2_, ...), custom_call_target="tpu_custom_call" | custom-call | tf_op jit(solution)/shard_map/pallas_call | solution.py:153
  21.3 0.1 collective-permute-start.8
  21.4 0.6 shard_map.92
  22.0 0.5 collective-permute-start.6
  22.5 0.4 shard_map.91
  22.9 0.1 collective-permute-start.3
  23.1 0.5 collective-permute-done.6
  23.6 3.0 %shard_map.93.refs_4_.refs_6_.other_ref = bf16[4,192,1152]{2,1,0:T(8,128)(2,1)S(1)} custom-call(s32[12]{0:T(128)S(1)} %get-tuple-element.35.pick_ref, s32[1]{0:T(128)} %bitcast.core_ref, bf16[1024,2304]{1,0:T(8,128)(2,1)} %bitcast.7.refs_0_.refs_1_.refs_2_, bf16[1024,2304]{1,0:T(8,128)(2,1)} %bitcast.7.refs_0_.refs_1_.refs_2_, ...), custom_call_target="tpu_custom_call" | custom-call | tf_op jit(solution)/shard_map/pallas_call | solution.py:180
  26.6 4.1 %collective-permute-done.8.refs_0_ = bf16[128,1152]{1,0:T(8,128)(2,1)S(1)} collective-permute-done((bf16[128,1152]{1,0:T(8,128)(2,1)S(1)}, bf16[128,1152]{1,0:T(8,128)(2,1)S(1)}, u32[]{:S(2)}, u32[]{:S(2)}) %collective-permute-start.8) | collective-permute-done | bytes 294944 | tf_op jit(solution)/shard_map/ppermute | solution.py:19
  30.8 0.4 shard_map.95
  31.3 1.2 %collective-permute-done.9 = bf16[1,128,384]{2,1,0:T(8,128)(2,1)S(1)} collective-permute-done((bf16[1,128,384]{2,1,0:T(8,128)(2,1)S(1)}, bf16[1,128,384]{2,1,0:T(8,128)(2,1)S(1)}, u32[]{:S(2)}, u32[]{:S(2)}) %collective-permute-start.9) | collective-permute-done | bytes 98336 | tf_op jit(solution)/shard_map/ppermute | solution.py:19
  32.6 1.6 %collective-permute-start.10 = (bf16[1,128,384]{2,1,0:T(8,128)(2,1)S(1)}, bf16[1,128,384]{2,1,0:T(8,128)(2,1)S(1)}, u32[]{:S(2)}, u32[]{:S(2)}) collective-permute-start(bf16[1,128,384]{2,1,0:T(8,128)(2,1)S(1)} %add_convert_fusion.1), channel_id=1, source_target_pairs={{0,2},{2,0},{1,3},{3,1},{4,6},{6,4},{5,7},{7,5},{8,10},{10,8},{9,1... | collective-permute-start | bytes 294920 | tf_op jit(solution)/shard_map/ppermute | solution.py:19
  34.2 0.6 collective-permute-start.7
  34.8 3.5 %collective-permute-done.10 = bf16[1,128,384]{2,1,0:T(8,128)(2,1)S(1)} collective-permute-done((bf16[1,128,384]{2,1,0:T(8,128)(2,1)S(1)}, bf16[1,128,384]{2,1,0:T(8,128)(2,1)S(1)}, u32[]{:S(2)}, u32[]{:S(2)}) %collective-permute-start.10) | collective-permute-done | bytes 98336 | tf_op jit(solution)/shard_map/ppermute | solution.py:19
  38.3 0.5 shard_map.96
  38.7 0.3 collective-permute-start.11
  39.1 1.8 %collective-permute-start.15 = (bf16[64,1152]{1,0:T(8,128)(2,1)S(1)}, bf16[64,1152]{1,0:T(8,128)(2,1)S(1)}, u32[]{:S(2)}, u32[]{:S(2)}) collective-permute-start(bf16[64,1152]{1,0:T(8,128)(2,1)S(1)} %get-tuple-element.56), channel_id=1, source_target_pairs={{0,4},{4,0},{8,12},{12,8},{1,5},{5,1},{9,13},{13,9},{2,6},{6,2},{1... | collective-permute-start | bytes 442376 | tf_op jit(solution)/shard_map/ppermute | solution.py:19
  40.8 0.9 collective-permute-done.7
  41.8 0.6 shard_map.94
  42.4 2.3 %collective-permute-done.11.arrived_ref = bf16[64,1152]{1,0:T(8,128)(2,1)S(1)} collective-permute-done((bf16[64,1152]{1,0:T(8,128)(2,1)S(1)}, bf16[64,1152]{1,0:T(8,128)(2,1)S(1)}, u32[]{:S(2)}, u32[]{:S(2)}) %collective-permute-start.11) | collective-permute-done | bytes 147488 | tf_op jit(solution)/shard_map/ppermute | solution.py:19
  44.7 1.5 %collective-permute-start.12 = (bf16[1,128,384]{2,1,0:T(8,128)(2,1)S(1)}, bf16[1,128,384]{2,1,0:T(8,128)(2,1)S(1)}, u32[]{:S(2)}, u32[]{:S(2)}) collective-permute-start(bf16[1,128,384]{2,1,0:T(8,128)(2,1)S(1)} %add_convert_fusion.2), channel_id=1, source_target_pairs={{0,2},{2,0},{1,3},{3,1},{4,6},{6,4},{5,7},{7,5},{8,10},{10,8},{9,1... | collective-permute-start | bytes 294920 | tf_op jit(solution)/shard_map/ppermute | solution.py:19
  46.2 0.3 collective-permute-start.13
  46.5 1.9 %collective-permute-start.14 = (bf16[64,1152]{1,0:T(8,128)(2,1)S(1)}, bf16[64,1152]{1,0:T(8,128)(2,1)S(1)}, u32[]{:S(2)}, u32[]{:S(2)}) collective-permute-start(bf16[64,1152]{1,0:T(8,128)(2,1)S(1)} %shard_map.98), channel_id=1, source_target_pairs={{0,8},{4,12},{8,0},{12,4},{1,9},{5,13},{9,1},{13,5},{2,10},{6,14},... | collective-permute-start | bytes 442376 | tf_op jit(solution)/shard_map/ppermute | solution.py:19
  48.4 1.1 %collective-permute-done.15.arrived_ref = bf16[64,1152]{1,0:T(8,128)(2,1)S(1)} collective-permute-done((bf16[64,1152]{1,0:T(8,128)(2,1)S(1)}, bf16[64,1152]{1,0:T(8,128)(2,1)S(1)}, u32[]{:S(2)}, u32[]{:S(2)}) %collective-permute-start.15) | collective-permute-done | bytes 147488 | tf_op jit(solution)/shard_map/ppermute | solution.py:19
  49.6 0.1 collective-permute-start.16
  49.7 0.5 shard_map.97
  50.1 5.0 %collective-permute-done.14.refs_1_ = bf16[64,1152]{1,0:T(8,128)(2,1)S(1)} collective-permute-done((bf16[64,1152]{1,0:T(8,128)(2,1)S(1)}, bf16[64,1152]{1,0:T(8,128)(2,1)S(1)}, u32[]{:S(2)}, u32[]{:S(2)}) %collective-permute-start.14) | collective-permute-done | bytes 147488 | tf_op jit(solution)/shard_map/ppermute | solution.py:19
  55.1 3.1 %collective-permute-done.13.refs_0_ = bf16[128,1152]{1,0:T(8,128)(2,1)S(1)} collective-permute-done((bf16[128,1152]{1,0:T(8,128)(2,1)S(1)}, bf16[128,1152]{1,0:T(8,128)(2,1)S(1)}, u32[]{:S(2)}, u32[]{:S(2)}) %collective-permute-start.13) | collective-permute-done | bytes 294944 | tf_op jit(solution)/shard_map/ppermute | solution.py:19
  58.2 0.1 shard_map.99.refs_0_.error_ref
  58.4 2.2 %collective-permute-start.19 = (bf16[64,1152]{1,0:T(8,128)(2,1)S(1)}, bf16[64,1152]{1,0:T(8,128)(2,1)S(1)}, u32[]{:S(2)}, u32[]{:S(2)}) collective-permute-start(bf16[64,1152]{1,0:T(8,128)(2,1)S(1)} %shard_map.99.refs_0_.error_ref), channel_id=1, source_target_pairs={{0,8},{4,12},{8,0},{12,4},{1,9},{5,13},{9,1},{13,5},{2,10},{6,14},... | collective-permute-start | bytes 442376 | tf_op jit(solution)/shard_map/ppermute | solution.py:19
  60.6 0.1 shard_map.101.refs_1_.error_ref
  60.7 0.2 collective-permute-start.22
  60.9 2.6 %collective-permute-start.21 = (bf16[64,1152]{1,0:T(8,128)(2,1)S(1)}, bf16[64,1152]{1,0:T(8,128)(2,1)S(1)}, u32[]{:S(2)}, u32[]{:S(2)}) collective-permute-start(bf16[64,1152]{1,0:T(8,128)(2,1)S(1)} %shard_map.101.refs_1_.error_ref), channel_id=1, source_target_pairs={{0,8},{4,12},{8,0},{12,4},{1,9},{5,13},{9,1},{13,5},{2,10},{6,14},... | collective-permute-start | bytes 442376 | tf_op jit(solution)/shard_map/ppermute | solution.py:19
  63.5 5.2 %collective-permute-done.20.error_ref = bf16[64,1152]{1,0:T(8,128)(2,1)S(1)} collective-permute-done((bf16[64,1152]{1,0:T(8,128)(2,1)S(1)}, bf16[64,1152]{1,0:T(8,128)(2,1)S(1)}, u32[]{:S(2)}, u32[]{:S(2)}) %collective-permute-start.20) | collective-permute-done | bytes 147488 | tf_op jit(solution)/shard_map/ppermute | solution.py:19
  68.7 0.8 collective-permute-done.19.error_ref
  69.5 4.5 %collective-permute-done.22.error_ref = bf16[64,1152]{1,0:T(8,128)(2,1)S(1)} collective-permute-done((bf16[64,1152]{1,0:T(8,128)(2,1)S(1)}, bf16[64,1152]{1,0:T(8,128)(2,1)S(1)}, u32[]{:S(2)}, u32[]{:S(2)}) %collective-permute-start.22) | collective-permute-done | bytes 147488 | tf_op jit(solution)/shard_map/ppermute | solution.py:19
  74.0 2.0 %collective-permute-done.23.error_ref = bf16[64,1152]{1,0:T(8,128)(2,1)S(1)} collective-permute-done((bf16[64,1152]{1,0:T(8,128)(2,1)S(1)}, bf16[64,1152]{1,0:T(8,128)(2,1)S(1)}, u32[]{:S(2)}, u32[]{:S(2)}) %collective-permute-start.23) | collective-permute-done | bytes 147488 | tf_op jit(solution)/shard_map/ppermute | solution.py:19
  76.0 0.3 collective-permute-start.24
  76.3 0.5 collective-permute-start.18
  76.8 0.6 shard_map.103.refs_0_
  77.4 0.6 shard_map.104.refs_1_
  78.0 0.6 shard_map.105.refs_2_
  78.6 0.6 shard_map.107.refs_4_
  79.2 0.6 shard_map.108.refs_5_
  79.7 0.6 shard_map.106.refs_3_
  80.3 0.6 shard_map.109.refs_6_
  80.9 0.2 collective-permute-done.24.error_ref
  81.2 0.6 shard_map.110.refs_7_
  81.8 1.6 %collective-permute-start.26 = (f32[4,192]{1,0:T(4,128)S(1)}, f32[4,192]{1,0:T(4,128)S(1)}, u32[]{:S(2)}, u32[]{:S(2)}) collective-permute-start(f32[4,192]{1,0:T(4,128)S(1)} %get-tuple-element.64), channel_id=1, source_target_pairs={{0,2},{2,0},{1,3},{3,1},{4,6},{6,4},{5,7},{7,5},{8,10},{10,8},{9,1... | collective-permute-start | bytes 9224 | tf_op jit(solution)/shard_map/ppermute | solution.py:19
  83.3 0.6 collective-permute-start.25
  84.0 0.9 shard_map.102
  84.8 0.6 collective-permute-done.26
  85.4 0.9 %collective-permute-done.27 = f32[4,192]{1,0:T(4,128)S(1)} collective-permute-done((f32[4,192]{1,0:T(4,128)S(1)}, f32[4,192]{1,0:T(4,128)S(1)}, u32[]{:S(2)}, u32[]{:S(2)}) %collective-permute-start.27) | collective-permute-done | bytes 3104 | tf_op jit(solution)/shard_map/ppermute | solution.py:25
  86.4 1.3 %shard_map.112 = f32[8,128]{1,0:T(8,128)} custom-call(s32[12]{0:T(128)S(1)} %get-tuple-element.34.pick_ref, f32[4,192]{1,0:T(4,128)S(1)} %add_add_fusion.total_ref), custom_call_target="tpu_custom_call" | custom-call | tf_op jit(solution)/shard_map/pallas_call | solution.py:413
  (29 shorter events, 0.5 us)
Async XLA Ops:
  0.6 16.5 %collective-permute-start.1 = (bf16[1,2304,1024]{2,1,0:T(8,128)(2,1)}, bf16[1,2304,1024]{2,1,0:T(8,128)(2,1)}, u32[]{:S(2)}, u32[]{:S(2)}) collective-permute-start(bf16[1,2304,1024]{2,1,0:T(8,128)(2,1)} %param.8), channel_id=1, source_target_pairs={{0,1},{1,0},{2,3},{3,2},{4,5},{5,4},{6,7},{7,6},{8,9},{9,8},{10,11... | collective-permute-start | bytes 14155784 | tf_op jit(solution)/shard_map/ppermute | solution.py:19
  1.1 21.9 %collective-permute-start.5 = (bf16[1,1024,2304]{2,1,0:T(8,128)(2,1)}, bf16[1,1024,2304]{2,1,0:T(8,128)(2,1)}, u32[]{:S(2)}, u32[]{:S(2)}) collective-permute-start(bf16[1,1024,2304]{2,1,0:T(8,128)(2,1)} %param.10), channel_id=1, source_target_pairs={{0,1},{1,0},{2,3},{3,2},{4,5},{5,4},{6,7},{7,6},{8,9},{9,8},{10,11... | collective-permute-start | bytes 14155784 | tf_op jit(solution)/shard_map/ppermute | solution.py:19
  2.2 19.1 %collective-permute-start = (bf16[128,1152]{1,0:T(8,128)(2,1)S(1)}, bf16[128,1152]{1,0:T(8,128)(2,1)S(1)}, u32[]{:S(2)}, u32[]{:S(2)}) collective-permute-start(bf16[128,1152]{1,0:T(8,128)(2,1)S(1)} %shard_map.86.refs_0_.token_ref), channel_id=1, source_target_pairs={{0,8},{4,12},{8,0},{12,4},{1,9},{5,13},{9,1},{13,5},{2,10},{6,14},... | collective-permute-start | bytes 884744 | tf_op jit(solution)/shard_map/ppermute | solution.py:19
  6.3 15.1 %collective-permute-start.4 = (bf16[128,1152]{1,0:T(8,128)(2,1)S(1)}, bf16[128,1152]{1,0:T(8,128)(2,1)S(1)}, u32[]{:S(2)}, u32[]{:S(2)}) collective-permute-start(bf16[128,1152]{1,0:T(8,128)(2,1)S(1)} %shard_map.86.refs_0_.token_ref), channel_id=1, source_target_pairs={{0,4},{4,0},{8,12},{12,8},{1,5},{5,1},{9,13},{13,9},{2,6},{6,2},{1... | collective-permute-start | bytes 884744 | tf_op jit(solution)/shard_map/ppermute | solution.py:19
  9.9 11.4 %collective-permute-start.2 = (f32[4,192]{1,0:T(4,128)S(1)}, f32[4,192]{1,0:T(4,128)S(1)}, u32[]{:S(2)}, u32[]{:S(2)}) collective-permute-start(f32[4,192]{1,0:T(4,128)S(1)} %get-tuple-element.41.refs_1_), channel_id=1, source_target_pairs={{0,1},{1,0},{2,3},{3,2},{4,5},{5,4},{6,7},{7,6},{8,9},{9,8},{10,11... | collective-permute-start | bytes 9224 | tf_op jit(solution)/shard_map/ppermute | solution.py:19
  21.3 9.4 %collective-permute-start.8 = (bf16[128,1152]{1,0:T(8,128)(2,1)S(1)}, bf16[128,1152]{1,0:T(8,128)(2,1)S(1)}, u32[]{:S(2)}, u32[]{:S(2)}) collective-permute-start(bf16[128,1152]{1,0:T(8,128)(2,1)S(1)} %collective-permute-done.refs_0_), channel_id=1, source_target_pairs={{0,4},{4,0},{8,12},{12,8},{1,5},{5,1},{9,13},{13,9},{2,6},{6,2},{1... | collective-permute-start | bytes 884744 | tf_op jit(solution)/shard_map/ppermute | solution.py:19
  22.0 1.6 %collective-permute-start.6 = (bf16[2,128,384]{2,1,0:T(8,128)(2,1)S(1)}, bf16[2,128,384]{2,1,0:T(8,128)(2,1)S(1)}, u32[]{:S(2)}, u32[]{:S(2)}) collective-permute-start(bf16[2,128,384]{2,1,0:T(8,128)(2,1)S(1)} %shard_map.92), channel_id=1, source_target_pairs={{0,1},{1,0},{2,3},{3,2},{4,5},{5,4},{6,7},{7,6},{8,9},{9,8},{10,11... | collective-permute-start | bytes 589832 | tf_op jit(solution)/shard_map/ppermute | solution.py:19
  22.9 8.3 %collective-permute-start.3 = (bf16[1,128,384]{2,1,0:T(8,128)(2,1)S(1)}, bf16[1,128,384]{2,1,0:T(8,128)(2,1)S(1)}, u32[]{:S(2)}, u32[]{:S(2)}) collective-permute-start(bf16[1,128,384]{2,1,0:T(8,128)(2,1)S(1)} %shard_map.91), channel_id=1, source_target_pairs={{0,1},{1,0},{2,3},{3,2},{4,5},{5,4},{6,7},{7,6},{8,9},{9,8},{10,11... | collective-permute-start | bytes 294920 | tf_op jit(solution)/shard_map/ppermute | solution.py:19
  31.2 1.4 %collective-permute-start.9 = (bf16[1,128,384]{2,1,0:T(8,128)(2,1)S(1)}, bf16[1,128,384]{2,1,0:T(8,128)(2,1)S(1)}, u32[]{:S(2)}, u32[]{:S(2)}) collective-permute-start(bf16[1,128,384]{2,1,0:T(8,128)(2,1)S(1)} %shard_map.95), channel_id=1, source_target_pairs={{0,1},{1,0},{2,3},{3,2},{4,5},{5,4},{6,7},{7,6},{8,9},{9,8},{10,11... | collective-permute-start | bytes 294920 | tf_op jit(solution)/shard_map/ppermute | solution.py:19
  32.6 5.7 %collective-permute-start.10 = (bf16[1,128,384]{2,1,0:T(8,128)(2,1)S(1)}, bf16[1,128,384]{2,1,0:T(8,128)(2,1)S(1)}, u32[]{:S(2)}, u32[]{:S(2)}) collective-permute-start(bf16[1,128,384]{2,1,0:T(8,128)(2,1)S(1)} %add_convert_fusion.1), channel_id=1, source_target_pairs={{0,2},{2,0},{1,3},{3,1},{4,6},{6,4},{5,7},{7,5},{8,10},{10,8},{9,1... | collective-permute-start | bytes 294920 | tf_op jit(solution)/shard_map/ppermute | solution.py:19
  34.2 7.5 %collective-permute-start.7 = (bf16[2,128,384]{2,1,0:T(8,128)(2,1)S(1)}, bf16[2,128,384]{2,1,0:T(8,128)(2,1)S(1)}, u32[]{:S(2)}, u32[]{:S(2)}) collective-permute-start(bf16[2,128,384]{2,1,0:T(8,128)(2,1)S(1)} %add_convert_fusion), channel_id=1, source_target_pairs={{0,2},{2,0},{1,3},{3,1},{4,6},{6,4},{5,7},{7,5},{8,10},{10,8},{9,1... | collective-permute-start | bytes 589832 | tf_op jit(solution)/shard_map/ppermute | solution.py:19
  38.7 5.9 %collective-permute-start.11 = (bf16[64,1152]{1,0:T(8,128)(2,1)S(1)}, bf16[64,1152]{1,0:T(8,128)(2,1)S(1)}, u32[]{:S(2)}, u32[]{:S(2)}) collective-permute-start(bf16[64,1152]{1,0:T(8,128)(2,1)S(1)} %get-tuple-element.49), channel_id=1, source_target_pairs={{0,4},{4,0},{8,12},{12,8},{1,5},{5,1},{9,13},{13,9},{2,6},{6,2},{1... | collective-permute-start | bytes 442376 | tf_op jit(solution)/shard_map/ppermute | solution.py:19
  39.1 10.4 %collective-permute-start.15 = (bf16[64,1152]{1,0:T(8,128)(2,1)S(1)}, bf16[64,1152]{1,0:T(8,128)(2,1)S(1)}, u32[]{:S(2)}, u32[]{:S(2)}) collective-permute-start(bf16[64,1152]{1,0:T(8,128)(2,1)S(1)} %get-tuple-element.56), channel_id=1, source_target_pairs={{0,4},{4,0},{8,12},{12,8},{1,5},{5,1},{9,13},{13,9},{2,6},{6,2},{1... | collective-permute-start | bytes 442376 | tf_op jit(solution)/shard_map/ppermute | solution.py:19
  41.7 16.5 %copy-start = (f32[1,2304]{1,0:T(1,128)S(1)}, f32[1,2304]{1,0:T(1,128)}, u32[]{:S(2)}) copy-start(f32[1,2304]{1,0:T(1,128)} %bias_ref.3) | copy-start | bytes 27652
  44.7 5.0 %collective-permute-start.12 = (bf16[1,128,384]{2,1,0:T(8,128)(2,1)S(1)}, bf16[1,128,384]{2,1,0:T(8,128)(2,1)S(1)}, u32[]{:S(2)}, u32[]{:S(2)}) collective-permute-start(bf16[1,128,384]{2,1,0:T(8,128)(2,1)S(1)} %add_convert_fusion.2), channel_id=1, source_target_pairs={{0,2},{2,0},{1,3},{3,1},{4,6},{6,4},{5,7},{7,5},{8,10},{10,8},{9,1... | collective-permute-start | bytes 294920 | tf_op jit(solution)/shard_map/ppermute | solution.py:19
  46.2 12.0 %collective-permute-start.13 = (bf16[128,1152]{1,0:T(8,128)(2,1)S(1)}, bf16[128,1152]{1,0:T(8,128)(2,1)S(1)}, u32[]{:S(2)}, u32[]{:S(2)}) collective-permute-start(bf16[128,1152]{1,0:T(8,128)(2,1)S(1)} %get-tuple-element.52), channel_id=1, source_target_pairs={{0,4},{4,0},{8,12},{12,8},{1,5},{5,1},{9,13},{13,9},{2,6},{6,2},{1... | collective-permute-start | bytes 884744 | tf_op jit(solution)/shard_map/ppermute | solution.py:19
  46.5 8.6 %collective-permute-start.14 = (bf16[64,1152]{1,0:T(8,128)(2,1)S(1)}, bf16[64,1152]{1,0:T(8,128)(2,1)S(1)}, u32[]{:S(2)}, u32[]{:S(2)}) collective-permute-start(bf16[64,1152]{1,0:T(8,128)(2,1)S(1)} %shard_map.98), channel_id=1, source_target_pairs={{0,8},{4,12},{8,0},{12,4},{1,9},{5,13},{9,1},{13,5},{2,10},{6,14},... | collective-permute-start | bytes 442376 | tf_op jit(solution)/shard_map/ppermute | solution.py:19
  49.6 11.1 %collective-permute-start.16 = (bf16[64,1152]{1,0:T(8,128)(2,1)S(1)}, bf16[64,1152]{1,0:T(8,128)(2,1)S(1)}, u32[]{:S(2)}, u32[]{:S(2)}) collective-permute-start(bf16[64,1152]{1,0:T(8,128)(2,1)S(1)} %shard_map.100), channel_id=1, source_target_pairs={{0,8},{4,12},{8,0},{12,4},{1,9},{5,13},{9,1},{13,5},{2,10},{6,14},... | collective-permute-start | bytes 442376 | tf_op jit(solution)/shard_map/ppermute | solution.py:19
  58.3 10.4 %collective-permute-start.20 = (bf16[64,1152]{1,0:T(8,128)(2,1)S(1)}, bf16[64,1152]{1,0:T(8,128)(2,1)S(1)}, u32[]{:S(2)}, u32[]{:S(2)}) collective-permute-start(bf16[64,1152]{1,0:T(8,128)(2,1)S(1)} %shard_map.99.refs_0_.error_ref), channel_id=1, source_target_pairs={{0,4},{4,0},{8,12},{12,8},{1,5},{5,1},{9,13},{13,9},{2,6},{6,2},{1... | collective-permute-start | bytes 442376 | tf_op jit(solution)/shard_map/ppermute | solution.py:19
  58.4 11.1 %collective-permute-start.19 = (bf16[64,1152]{1,0:T(8,128)(2,1)S(1)}, bf16[64,1152]{1,0:T(8,128)(2,1)S(1)}, u32[]{:S(2)}, u32[]{:S(2)}) collective-permute-start(bf16[64,1152]{1,0:T(8,128)(2,1)S(1)} %shard_map.99.refs_0_.error_ref), channel_id=1, source_target_pairs={{0,8},{4,12},{8,0},{12,4},{1,9},{5,13},{9,1},{13,5},{2,10},{6,14},... | collective-permute-start | bytes 442376 | tf_op jit(solution)/shard_map/ppermute | solution.py:19
  60.7 13.3 %collective-permute-start.22 = (bf16[64,1152]{1,0:T(8,128)(2,1)S(1)}, bf16[64,1152]{1,0:T(8,128)(2,1)S(1)}, u32[]{:S(2)}, u32[]{:S(2)}) collective-permute-start(bf16[64,1152]{1,0:T(8,128)(2,1)S(1)} %shard_map.101.refs_1_.error_ref), channel_id=1, source_target_pairs={{0,4},{4,0},{8,12},{12,8},{1,5},{5,1},{9,13},{13,9},{2,6},{6,2},{1... | collective-permute-start | bytes 442376 | tf_op jit(solution)/shard_map/ppermute | solution.py:19
  60.9 13.1 %collective-permute-start.21 = (bf16[64,1152]{1,0:T(8,128)(2,1)S(1)}, bf16[64,1152]{1,0:T(8,128)(2,1)S(1)}, u32[]{:S(2)}, u32[]{:S(2)}) collective-permute-start(bf16[64,1152]{1,0:T(8,128)(2,1)S(1)} %shard_map.101.refs_1_.error_ref), channel_id=1, source_target_pairs={{0,8},{4,12},{8,0},{12,4},{1,9},{5,13},{9,1},{13,5},{2,10},{6,14},... | collective-permute-start | bytes 442376 | tf_op jit(solution)/shard_map/ppermute | solution.py:19
  69.5 6.5 %collective-permute-start.23 = (bf16[64,1152]{1,0:T(8,128)(2,1)S(1)}, bf16[64,1152]{1,0:T(8,128)(2,1)S(1)}, u32[]{:S(2)}, u32[]{:S(2)}) collective-permute-start(bf16[64,1152]{1,0:T(8,128)(2,1)S(1)} %collective-permute-done.19.error_ref), channel_id=1, source_target_pairs={{0,4},{4,0},{8,12},{12,8},{1,5},{5,1},{9,13},{13,9},{2,6},{6,2},{1... | collective-permute-start | bytes 442376 | tf_op jit(solution)/shard_map/ppermute | solution.py:19
  76.0 5.1 %collective-permute-start.24 = (bf16[64,1152]{1,0:T(8,128)(2,1)S(1)}, bf16[64,1152]{1,0:T(8,128)(2,1)S(1)}, u32[]{:S(2)}, u32[]{:S(2)}) collective-permute-start(bf16[64,1152]{1,0:T(8,128)(2,1)S(1)} %collective-permute-done.21.error_ref), channel_id=1, source_target_pairs={{0,4},{4,0},{8,12},{12,8},{1,5},{5,1},{9,13},{13,9},{2,6},{6,2},{1... | collective-permute-start | bytes 442376 | tf_op jit(solution)/shard_map/ppermute | solution.py:19
  76.3 7.7 %collective-permute-start.17 = (bf16[64,1152]{1,0:T(8,128)(2,1)S(1)}, bf16[64,1152]{1,0:T(8,128)(2,1)S(1)}, u32[]{:S(2)}, u32[]{:S(2)}) collective-permute-start(bf16[64,1152]{1,0:T(8,128)(2,1)S(1)} %shard_map.99.refs_0_.error_ref), channel_id=1, source_target_pairs={{0,1},{1,0},{2,3},{3,2},{4,5},{5,4},{6,7},{7,6},{8,9},{9,8},{10,11... | collective-permute-start | bytes 442376 | tf_op jit(solution)/shard_map/ppermute | solution.py:19
  76.3 7.7 %collective-permute-start.18 = (bf16[64,1152]{1,0:T(8,128)(2,1)S(1)}, bf16[64,1152]{1,0:T(8,128)(2,1)S(1)}, u32[]{:S(2)}, u32[]{:S(2)}) collective-permute-start(bf16[64,1152]{1,0:T(8,128)(2,1)S(1)} %shard_map.101.refs_1_.error_ref), channel_id=1, source_target_pairs={{0,1},{1,0},{2,3},{3,2},{4,5},{5,4},{6,7},{7,6},{8,9},{9,8},{10,11... | collective-permute-start | bytes 442376 | tf_op jit(solution)/shard_map/ppermute | solution.py:19
  81.8 3.7 %collective-permute-start.26 = (f32[4,192]{1,0:T(4,128)S(1)}, f32[4,192]{1,0:T(4,128)S(1)}, u32[]{:S(2)}, u32[]{:S(2)}) collective-permute-start(f32[4,192]{1,0:T(4,128)S(1)} %get-tuple-element.64), channel_id=1, source_target_pairs={{0,2},{2,0},{1,3},{3,1},{4,6},{6,4},{5,7},{7,5},{8,10},{10,8},{9,1... | collective-permute-start | bytes 9224 | tf_op jit(solution)/shard_map/ppermute | solution.py:19
  83.3 3.0 %collective-permute-start.27 = (f32[4,192]{1,0:T(4,128)S(1)}, f32[4,192]{1,0:T(4,128)S(1)}, u32[]{:S(2)}, u32[]{:S(2)}) collective-permute-start(f32[4,192]{1,0:T(4,128)S(1)} %get-tuple-element.65), channel_id=1, source_target_pairs={{0,3},{1,2},{2,1},{3,0},{4,7},{5,6},{6,5},{7,4},{8,11},{9,10},{10,... | collective-permute-start | bytes 9224 | tf_op jit(solution)/shard_map/ppermute | solution.py:25
  83.3 3.0 %collective-permute-start.25 = (f32[4,192]{1,0:T(4,128)S(1)}, f32[4,192]{1,0:T(4,128)S(1)}, u32[]{:S(2)}, u32[]{:S(2)}) collective-permute-start(f32[4,192]{1,0:T(4,128)S(1)} %get-tuple-element.65), channel_id=1, source_target_pairs={{0,1},{1,0},{2,3},{3,2},{4,5},{5,4},{6,7},{7,6},{8,9},{9,8},{10,11... | collective-permute-start | bytes 9224 | tf_op jit(solution)/shard_map/ppermute | solution.py:19

commit v5 on v4

--- a/solution.py
+++ b/solution.py
@@ -12,6 +12,7 @@
 ROW_PARTS = 2
 PARAMS = pltpu.CompilerParams(vmem_limit_bytes=16 * 1024 * 1024)
 SMALL = pl.CostEstimate(flops=0, bytes_accessed=0, transcendentals=0)
+AHEAD = pl.CostEstimate(flops=4000000000, bytes_accessed=0, transcendentals=0)
 
 
 def swap(value, axis, mask):
@@ -344,7 +345,7 @@
     )(core, part, bias, tokens, *arrived)
 
 
-def gradient(error, codes, at, first, weights, offset):
+def gradient(error, codes, at, first, weights, offset, cost=SMALL):
     rows, half = error.shape
 
     def body(error_ref, code_ref, own_ref, other_ref, out_ref):
@@ -364,7 +365,7 @@
         out_specs=whole((2, SLOT)),
         out_shape=jax.ShapeDtypeStruct((2, SLOT), jnp.float32),
         compiler_params=PARAMS,
-        cost_estimate=SMALL,
+        cost_estimate=cost,
     )(error, codes, *slots(weights, [offset]))
 
 
@@ -554,14 +555,14 @@
             if mask == 1:
                 errors[1] = swap(sources.pop(0), "lat", 1)
                 last = max(sources)
-                sources[last], errors[1], before = lax.optimization_barrier(
-                    (sources[last], errors[1], before)
-                )
+                sources[last], errors[1] = lax.optimization_barrier((sources[last], errors[1]))
             for o, error in sources.items():
                 errors[o ^ mask] = swap(error, "lat", mask)
         before = errors[lat_size - 1]
         for o, error in errors.items():
-            terms[o].append(gradient(error, *codes[o], r, dec_two, o))
+            terms[o].append(gradient(
+                error, *codes[o], r, dec_two, o, SMALL if r else AHEAD
+            ))
     own_sum, other_sum = gathered(terms)
     total = own_sum + swap(other_sum, "tok", 1)
     for mask in range(1, lax.axis_size("layer")):

time: 88 us -> 85.3 us (0.969)
  waiting for transfers between devices: 36 us -> 28.8 us
  starting transfers between devices: 23.2 us -> 29.2 us
  Pallas kernels: 27.3 us -> 25.5 us
    ppermute x27, waiting for transfers between devices: 35.1 us -> 27.9 us  [swap(): return lax.ppermute(value, axis, [(i, i ^ mask) for i in range(size)])]
    ppermute x27, starting transfers between devices: 23.2 us -> 29.2 us  [swap(): return lax.ppermute(value, axis, [(i, i ^ mask) for i in range(size)])]
    pallas_call x2, Pallas kernels: 6.09 us -> 5.02 us  [decoder_slots(): pl.pallas_call(body, grid_spec=pltpu.PrefetchScalarGridSpec(num_scalar_pr...]
  transfers between devices with their start and end apart: 28 -> 28, of which waited for: 16 -> 16; matrix products, arithmetic and copies ran while one was open for 0% -> 0% of each run, Pallas kernels for 30% -> 29%
where the time goes in v5:
time: 85.3 us; the launch traced here: 84.6 us
  starting transfers between devices  29.2 us (34%)
  waiting for transfers between devices  28.8 us (34%)
  Pallas kernels  25.5 us (30%)
    ppermute x27, starting transfers between devices, swap(): return lax.ppermute(value, axis, [(i, i ^ mask) for i in range(size)])  29.2 us
    ppermute x27, waiting for transfers between devices, swap(): return lax.ppermute(value, axis, [(i, i ^ mask) for i in range(size)])  27.9 us
    pallas_call x2, Pallas kernels, encoder_slots(): pl.pallas_call(body, grid_spec=pltpu.PrefetchScalarGridSpec(num_scalar_pr...  7.51 us
    pallas_call x2, Pallas kernels, decoder_slots(): pl.pallas_call(body, grid_spec=pltpu.PrefetchScalarGridSpec(num_scalar_pr...  5.02 us
    pallas_call x8, Pallas kernels, gradient(): pl.pallas_call(body, grid=(1,), in_specs=[whole((rows, half)), pl.BlockSp...  4.67 us
    pallas_call x1, Pallas kernels, plan(): pl.pallas_call(body, grid=(1,), in_specs=[smem] * 3 + [whole((latents //...  1.96 us
  transfers between devices with their start and end apart: 28, of which 16 were waited for; matrix products, arithmetic and copies ran while one was open for 0% of the time, Pallas kernels for 29%

profile of v5, /device:TPU:0, one launch (start us, length us, event | category | flops | bytes accessed | tf_op | source)
XLA Modules:
  0.0 84.6 jit_solution(12997388874422936074)
XLA Ops:
  0.6 0.5 collective-permute-start.1
  1.1 0.1 collective-permute-start.5
  1.2 1.0 %shard_map.86.refs_0_.token_ref = bf16[128,1152]{1,0:T(8,128)(2,1)S(1)} custom-call(s32[1]{0:T(128)} %bitcast.core_ref, bf16[128,2304]{1,0:T(8,128)(2,1)} %bitcast.16), custom_call_target="tpu_custom_call" | custom-call | tf_op jit(solution)/shard_map/pallas_call | solution.py:56
  2.2 4.1 %collective-permute-start = (bf16[128,1152]{1,0:T(8,128)(2,1)S(1)}, bf16[128,1152]{1,0:T(8,128)(2,1)S(1)}, u32[]{:S(2)}, u32[]{:S(2)}) collective-permute-start(bf16[128,1152]{1,0:T(8,128)(2,1)S(1)} %shard_map.86.refs_0_.token_ref), channel_id=1, source_target_pairs={{0,8},{4,12},{8,0},{12,4},{1,9},{5,13},{9,1},{13,5},{2,10},{6,14},... | collective-permute-start | bytes 884744 | tf_op jit(solution)/shard_map/ppermute | solution.py:20
  6.3 1.6 %collective-permute-start.4 = (bf16[128,1152]{1,0:T(8,128)(2,1)S(1)}, bf16[128,1152]{1,0:T(8,128)(2,1)S(1)}, u32[]{:S(2)}, u32[]{:S(2)}) collective-permute-start(bf16[128,1152]{1,0:T(8,128)(2,1)S(1)} %shard_map.86.refs_0_.token_ref), channel_id=1, source_target_pairs={{0,4},{4,0},{8,12},{12,8},{1,5},{5,1},{9,13},{13,9},{2,6},{6,2},{1... | collective-permute-start | bytes 884744 | tf_op jit(solution)/shard_map/ppermute | solution.py:20
  7.9 2.0 %shard_map.87 = (s32[12]{0:T(128)S(1)}, s32[12]{0:T(128)S(1)}, f32[4,192]{1,0:T(4,128)S(1)}) custom-call(s32[4,16]{1,0:T(4,128)} %ids_ref.1, s32[4]{0:T(128)} %counts_ref.1, s32[2]{0:T(128)S(1)} %pad_add_fusion.places_ref, f32[8,128]{1,0:T(8,128)} %bitcast.18), custom_call_target="tpu_custom_call" | custom-call | tf_op jit(solution)/shard_map/pallas_call | solution.py:117
  10.0 2.0 %shard_map.90.refs_3_.refs_5_.own_ref = bf16[4,192,1152]{2,1,0:T(8,128)(2,1)S(1)} custom-call(s32[12]{0:T(128)S(1)} %get-tuple-element.34.pick_ref, s32[1]{0:T(128)} %bitcast.core_ref, bf16[1024,2304]{1,0:T(8,128)(2,1)} %bitcast.13, bf16[1024,2304]{1,0:T(8,128)(2,1)} %bitcast.14, bf16[1024,2304]{1,0:T(8,128)(2,1)} %bitcast.15), custom_call_target="tpu_custom_call" | custom-call | tf_op jit(solution)/shard_map/pallas_call | solution.py:181
  12.0 3.4 %shard_map.88.refs_1_.refs_2_.refs_4_ = bf16[4,1152,192]{2,1,0:T(8,128)(2,1)S(1)} custom-call(s32[12]{0:T(128)S(1)} %get-tuple-element.34.pick_ref, s32[1]{0:T(128)} %bitcast.core_ref, bf16[2304,1024]{1,0:T(8,128)(2,1)} %bitcast.10, bf16[2304,1024]{1,0:T(8,128)(2,1)} %bitcast.11, bf16[2304,1024]{1,0:T(8,128)(2,1)} %bitcast.12), custom_call_target="tpu_custom_call" | custom-call | tf_op jit(solution)/shard_map/pallas_call | solution.py:154
  15.4 4.1 %shard_map.89.refs_2_.refs_3_.refs_5_ = bf16[4,1152,192]{2,1,0:T(8,128)(2,1)S(1)} custom-call(s32[12]{0:T(128)S(1)} %get-tuple-element.35.pick_ref, s32[1]{0:T(128)} %bitcast.core_ref, bf16[2304,1024]{1,0:T(8,128)(2,1)} %bitcast.5.refs_0_.refs_1_.refs_2_, bf16[2304,1024]{1,0:T(8,128)(2,1)} %bitcast.5.refs_0_.refs_1_.refs_2_, ...), custom_call_target="tpu_custom_call" | custom-call | tf_op jit(solution)/shard_map/pallas_call | solution.py:154
  19.5 0.4 collective-permute-done.refs_0_
  20.0 1.8 %collective-permute-start.8 = (bf16[128,1152]{1,0:T(8,128)(2,1)S(1)}, bf16[128,1152]{1,0:T(8,128)(2,1)S(1)}, u32[]{:S(2)}, u32[]{:S(2)}) collective-permute-start(bf16[128,1152]{1,0:T(8,128)(2,1)S(1)} %collective-permute-done.refs_0_), channel_id=1, source_target_pairs={{0,4},{4,0},{8,12},{12,8},{1,5},{5,1},{9,13},{13,9},{2,6},{6,2},{1... | collective-permute-start | bytes 884744 | tf_op jit(solution)/shard_map/ppermute | solution.py:20
  21.8 0.6 shard_map.92
  22.4 0.1 collective-permute-start.6
  22.5 0.4 shard_map.91
  22.9 0.5 collective-permute-start.3
  23.4 0.4 collective-permute-done.6
  23.9 3.0 %shard_map.93.refs_4_.refs_6_.other_ref = bf16[4,192,1152]{2,1,0:T(8,128)(2,1)S(1)} custom-call(s32[12]{0:T(128)S(1)} %get-tuple-element.35.pick_ref, s32[1]{0:T(128)} %bitcast.core_ref, bf16[1024,2304]{1,0:T(8,128)(2,1)} %bitcast.7.refs_0_.refs_1_.refs_2_, bf16[1024,2304]{1,0:T(8,128)(2,1)} %bitcast.7.refs_0_.refs_1_.refs_2_, ...), custom_call_target="tpu_custom_call" | custom-call | tf_op jit(solution)/shard_map/pallas_call | solution.py:181
  26.9 2.7 %collective-permute-done.8.refs_0_ = bf16[128,1152]{1,0:T(8,128)(2,1)S(1)} collective-permute-done((bf16[128,1152]{1,0:T(8,128)(2,1)S(1)}, bf16[128,1152]{1,0:T(8,128)(2,1)S(1)}, u32[]{:S(2)}, u32[]{:S(2)}) %collective-permute-start.8) | collective-permute-done | bytes 294944 | tf_op jit(solution)/shard_map/ppermute | solution.py:20
  29.7 0.4 shard_map.95
  30.1 0.2 collective-permute-start.9
  30.3 1.2 %collective-permute-done.9 = bf16[1,128,384]{2,1,0:T(8,128)(2,1)S(1)} collective-permute-done((bf16[1,128,384]{2,1,0:T(8,128)(2,1)S(1)}, bf16[1,128,384]{2,1,0:T(8,128)(2,1)S(1)}, u32[]{:S(2)}, u32[]{:S(2)}) %collective-permute-start.9) | collective-permute-done | bytes 98336 | tf_op jit(solution)/shard_map/ppermute | solution.py:20
  31.5 1.6 %collective-permute-start.10 = (bf16[1,128,384]{2,1,0:T(8,128)(2,1)S(1)}, bf16[1,128,384]{2,1,0:T(8,128)(2,1)S(1)}, u32[]{:S(2)}, u32[]{:S(2)}) collective-permute-start(bf16[1,128,384]{2,1,0:T(8,128)(2,1)S(1)} %add_convert_fusion.1), channel_id=1, source_target_pairs={{0,2},{2,0},{1,3},{3,1},{4,6},{6,4},{5,7},{7,5},{8,10},{10,8},{9,1... | collective-permute-start | bytes 294920 | tf_op jit(solution)/shard_map/ppermute | solution.py:20
  33.2 0.5 collective-permute-start.7
  33.7 3.4 %collective-permute-done.10 = bf16[1,128,384]{2,1,0:T(8,128)(2,1)S(1)} collective-permute-done((bf16[1,128,384]{2,1,0:T(8,128)(2,1)S(1)}, bf16[1,128,384]{2,1,0:T(8,128)(2,1)S(1)}, u32[]{:S(2)}, u32[]{:S(2)}) %collective-permute-start.10) | collective-permute-done | bytes 98336 | tf_op jit(solution)/shard_map/ppermute | solution.py:20
  37.2 0.5 shard_map.96
  37.6 1.5 %collective-permute-start.11 = (bf16[64,1152]{1,0:T(8,128)(2,1)S(1)}, bf16[64,1152]{1,0:T(8,128)(2,1)S(1)}, u32[]{:S(2)}, u32[]{:S(2)}) collective-permute-start(bf16[64,1152]{1,0:T(8,128)(2,1)S(1)} %get-tuple-element.49), channel_id=1, source_target_pairs={{0,4},{4,0},{8,12},{12,8},{1,5},{5,1},{9,13},{13,9},{2,6},{6,2},{1... | collective-permute-start | bytes 442376 | tf_op jit(solution)/shard_map/ppermute | solution.py:20
  39.1 0.6 collective-permute-start.15
  39.7 0.9 %collective-permute-done.7 = bf16[2,128,384]{2,1,0:T(8,128)(2,1)S(1)} collective-permute-done((bf16[2,128,384]{2,1,0:T(8,128)(2,1)S(1)}, bf16[2,128,384]{2,1,0:T(8,128)(2,1)S(1)}, u32[]{:S(2)}, u32[]{:S(2)}) %collective-permute-start.7) | collective-permute-done | bytes 196640 | tf_op jit(solution)/shard_map/ppermute | solution.py:20
  40.7 0.6 shard_map.94
  41.3 2.3 %collective-permute-done.11.arrived_ref = bf16[64,1152]{1,0:T(8,128)(2,1)S(1)} collective-permute-done((bf16[64,1152]{1,0:T(8,128)(2,1)S(1)}, bf16[64,1152]{1,0:T(8,128)(2,1)S(1)}, u32[]{:S(2)}, u32[]{:S(2)}) %collective-permute-start.11) | collective-permute-done | bytes 147488 | tf_op jit(solution)/shard_map/ppermute | solution.py:20
  43.6 1.6 %collective-permute-start.12 = (bf16[1,128,384]{2,1,0:T(8,128)(2,1)S(1)}, bf16[1,128,384]{2,1,0:T(8,128)(2,1)S(1)}, u32[]{:S(2)}, u32[]{:S(2)}) collective-permute-start(bf16[1,128,384]{2,1,0:T(8,128)(2,1)S(1)} %add_convert_fusion.2), channel_id=1, source_target_pairs={{0,2},{2,0},{1,3},{3,1},{4,6},{6,4},{5,7},{7,5},{8,10},{10,8},{9,1... | collective-permute-start | bytes 294920 | tf_op jit(solution)/shard_map/ppermute | solution.py:20
  45.2 1.3 %collective-permute-start.13 = (bf16[128,1152]{1,0:T(8,128)(2,1)S(1)}, bf16[128,1152]{1,0:T(8,128)(2,1)S(1)}, u32[]{:S(2)}, u32[]{:S(2)}) collective-permute-start(bf16[128,1152]{1,0:T(8,128)(2,1)S(1)} %get-tuple-element.52), channel_id=1, source_target_pairs={{0,4},{4,0},{8,12},{12,8},{1,5},{5,1},{9,13},{13,9},{2,6},{6,2},{1... | collective-permute-start | bytes 884744 | tf_op jit(solution)/shard_map/ppermute | solution.py:20
  46.5 1.9 %collective-permute-start.14 = (bf16[64,1152]{1,0:T(8,128)(2,1)S(1)}, bf16[64,1152]{1,0:T(8,128)(2,1)S(1)}, u32[]{:S(2)}, u32[]{:S(2)}) collective-permute-start(bf16[64,1152]{1,0:T(8,128)(2,1)S(1)} %shard_map.98), channel_id=1, source_target_pairs={{0,8},{4,12},{8,0},{12,4},{1,9},{5,13},{9,1},{13,5},{2,10},{6,14},... | collective-permute-start | bytes 442376 | tf_op jit(solution)/shard_map/ppermute | solution.py:20
  48.5 1.1 %collective-permute-start.16 = (bf16[64,1152]{1,0:T(8,128)(2,1)S(1)}, bf16[64,1152]{1,0:T(8,128)(2,1)S(1)}, u32[]{:S(2)}, u32[]{:S(2)}) collective-permute-start(bf16[64,1152]{1,0:T(8,128)(2,1)S(1)} %shard_map.100), channel_id=1, source_target_pairs={{0,8},{4,12},{8,0},{12,4},{1,9},{5,13},{9,1},{13,5},{2,10},{6,14},... | collective-permute-start | bytes 442376 | tf_op jit(solution)/shard_map/ppermute | solution.py:20
  49.6 0.5 shard_map.97
  50.1 5.1 %collective-permute-done.14.refs_1_ = bf16[64,1152]{1,0:T(8,128)(2,1)S(1)} collective-permute-done((bf16[64,1152]{1,0:T(8,128)(2,1)S(1)}, bf16[64,1152]{1,0:T(8,128)(2,1)S(1)}, u32[]{:S(2)}, u32[]{:S(2)}) %collective-permute-start.14) | collective-permute-done | bytes 147488 | tf_op jit(solution)/shard_map/ppermute | solution.py:20
  55.2 1.9 %collective-permute-done.13.refs_0_ = bf16[128,1152]{1,0:T(8,128)(2,1)S(1)} collective-permute-done((bf16[128,1152]{1,0:T(8,128)(2,1)S(1)}, bf16[128,1152]{1,0:T(8,128)(2,1)S(1)}, u32[]{:S(2)}, u32[]{:S(2)}) %collective-permute-start.13) | collective-permute-done | bytes 294944 | tf_op jit(solution)/shard_map/ppermute | solution.py:20
  57.1 0.1 shard_map.99.refs_0_.error_ref
  57.2 0.7 collective-permute-start.20
  57.9 2.9 %collective-permute-start.19 = (bf16[64,1152]{1,0:T(8,128)(2,1)S(1)}, bf16[64,1152]{1,0:T(8,128)(2,1)S(1)}, u32[]{:S(2)}, u32[]{:S(2)}) collective-permute-start(bf16[64,1152]{1,0:T(8,128)(2,1)S(1)} %shard_map.99.refs_0_.error_ref), channel_id=1, source_target_pairs={{0,8},{4,12},{8,0},{12,4},{1,9},{5,13},{9,1},{13,5},{2,10},{6,14},... | collective-permute-start | bytes 442376 | tf_op jit(solution)/shard_map/ppermute | solution.py:20
  60.8 0.1 shard_map.101.refs_1_.error_ref
  60.9 0.1 collective-permute-start.22
  61.0 1.4 %collective-permute-start.21 = (bf16[64,1152]{1,0:T(8,128)(2,1)S(1)}, bf16[64,1152]{1,0:T(8,128)(2,1)S(1)}, u32[]{:S(2)}, u32[]{:S(2)}) collective-permute-start(bf16[64,1152]{1,0:T(8,128)(2,1)S(1)} %shard_map.101.refs_1_.error_ref), channel_id=1, source_target_pairs={{0,8},{4,12},{8,0},{12,4},{1,9},{5,13},{9,1},{13,5},{2,10},{6,14},... | collective-permute-start | bytes 442376 | tf_op jit(solution)/shard_map/ppermute | solution.py:20
  62.4 0.6 shard_map.103.refs_0_
  63.0 0.6 shard_map.104.refs_1_
  63.6 4.3 %collective-permute-done.20.error_ref = bf16[64,1152]{1,0:T(8,128)(2,1)S(1)} collective-permute-done((bf16[64,1152]{1,0:T(8,128)(2,1)S(1)}, bf16[64,1152]{1,0:T(8,128)(2,1)S(1)}, u32[]{:S(2)}, u32[]{:S(2)}) %collective-permute-start.20) | collective-permute-done | bytes 147488 | tf_op jit(solution)/shard_map/ppermute | solution.py:20
  67.9 0.4 collective-permute-done.19.error_ref
  68.3 0.4 collective-permute-start.23
  68.7 3.4 %collective-permute-done.22.error_ref = bf16[64,1152]{1,0:T(8,128)(2,1)S(1)} collective-permute-done((bf16[64,1152]{1,0:T(8,128)(2,1)S(1)}, bf16[64,1152]{1,0:T(8,128)(2,1)S(1)}, u32[]{:S(2)}, u32[]{:S(2)}) %collective-permute-start.22) | collective-permute-done | bytes 147488 | tf_op jit(solution)/shard_map/ppermute | solution.py:20
  72.1 0.4 collective-permute-done.21.error_ref
  72.6 2.5 %collective-permute-start.24 = (bf16[64,1152]{1,0:T(8,128)(2,1)S(1)}, bf16[64,1152]{1,0:T(8,128)(2,1)S(1)}, u32[]{:S(2)}, u32[]{:S(2)}) collective-permute-start(bf16[64,1152]{1,0:T(8,128)(2,1)S(1)} %collective-permute-done.21.error_ref), channel_id=1, source_target_pairs={{0,4},{4,0},{8,12},{12,8},{1,5},{5,1},{9,13},{13,9},{2,6},{6,2},{1... | collective-permute-start | bytes 442376 | tf_op jit(solution)/shard_map/ppermute | solution.py:20
  75.0 0.6 shard_map.105.refs_2_
  75.6 0.6 shard_map.107.refs_4_
  76.2 0.6 shard_map.106.refs_3_
  76.8 0.6 shard_map.108.refs_5_
  77.4 0.6 shard_map.109.refs_6_
  77.9 0.3 collective-permute-done.24.error_ref
  78.2 0.6 shard_map.110.refs_7_
  78.8 1.5 %collective-permute-start.26 = (f32[4,192]{1,0:T(4,128)S(1)}, f32[4,192]{1,0:T(4,128)S(1)}, u32[]{:S(2)}, u32[]{:S(2)}) collective-permute-start(f32[4,192]{1,0:T(4,128)S(1)} %get-tuple-element.64), channel_id=1, source_target_pairs={{0,2},{2,0},{1,3},{3,1},{4,6},{6,4},{5,7},{7,5},{8,10},{10,8},{9,1... | collective-permute-start | bytes 9224 | tf_op jit(solution)/shard_map/ppermute | solution.py:20
  80.3 0.7 collective-permute-start.25
  81.0 0.9 %shard_map.102 = bf16[128,2304]{1,0:T(8,128)(2,1)} custom-call(s32[1]{0:T(128)} %bitcast.core_ref, bf16[64,1152]{1,0:T(8,128)(2,1)S(1)} %shard_map.99.refs_0_.error_ref, bf16[64,1152]{1,0:T(8,128)(2,1)S(1)} %shard_map.101.refs_1_.error_ref, bf16[64,1152]{1,0:T(8,128)(2,1)S(1)} %collective-permute-done.17.refs_2_, ...), custom_call_target="tpu_custom_call" | custom-call | tf_op jit(solution)/shard_map/pallas_call | solution.py:441
  81.9 0.6 collective-permute-done.26
  82.5 0.8 collective-permute-done.27
  83.3 1.3 %shard_map.112 = f32[8,128]{1,0:T(8,128)} custom-call(s32[12]{0:T(128)S(1)} %get-tuple-element.34.pick_ref, f32[4,192]{1,0:T(4,128)S(1)} %add_add_fusion.total_ref), custom_call_target="tpu_custom_call" | custom-call | tf_op jit(solution)/shard_map/pallas_call | solution.py:414
  (29 shorter events, 0.5 us)
Async XLA Ops:
  0.6 14.8 %collective-permute-start.1 = (bf16[1,2304,1024]{2,1,0:T(8,128)(2,1)}, bf16[1,2304,1024]{2,1,0:T(8,128)(2,1)}, u32[]{:S(2)}, u32[]{:S(2)}) collective-permute-start(bf16[1,2304,1024]{2,1,0:T(8,128)(2,1)} %param.8), channel_id=1, source_target_pairs={{0,1},{1,0},{2,3},{3,2},{4,5},{5,4},{6,7},{7,6},{8,9},{9,8},{10,11... | collective-permute-start | bytes 14155784 | tf_op jit(solution)/shard_map/ppermute | solution.py:20
  1.1 22.3 %collective-permute-start.5 = (bf16[1,1024,2304]{2,1,0:T(8,128)(2,1)}, bf16[1,1024,2304]{2,1,0:T(8,128)(2,1)}, u32[]{:S(2)}, u32[]{:S(2)}) collective-permute-start(bf16[1,1024,2304]{2,1,0:T(8,128)(2,1)} %param.10), channel_id=1, source_target_pairs={{0,1},{1,0},{2,3},{3,2},{4,5},{5,4},{6,7},{7,6},{8,9},{9,8},{10,11... | collective-permute-start | bytes 14155784 | tf_op jit(solution)/shard_map/ppermute | solution.py:20
  2.2 17.8 %collective-permute-start = (bf16[128,1152]{1,0:T(8,128)(2,1)S(1)}, bf16[128,1152]{1,0:T(8,128)(2,1)S(1)}, u32[]{:S(2)}, u32[]{:S(2)}) collective-permute-start(bf16[128,1152]{1,0:T(8,128)(2,1)S(1)} %shard_map.86.refs_0_.token_ref), channel_id=1, source_target_pairs={{0,8},{4,12},{8,0},{12,4},{1,9},{5,13},{9,1},{13,5},{2,10},{6,14},... | collective-permute-start | bytes 884744 | tf_op jit(solution)/shard_map/ppermute | solution.py:20
  6.3 15.5 %collective-permute-start.4 = (bf16[128,1152]{1,0:T(8,128)(2,1)S(1)}, bf16[128,1152]{1,0:T(8,128)(2,1)S(1)}, u32[]{:S(2)}, u32[]{:S(2)}) collective-permute-start(bf16[128,1152]{1,0:T(8,128)(2,1)S(1)} %shard_map.86.refs_0_.token_ref), channel_id=1, source_target_pairs={{0,4},{4,0},{8,12},{12,8},{1,5},{5,1},{9,13},{13,9},{2,6},{6,2},{1... | collective-permute-start | bytes 884744 | tf_op jit(solution)/shard_map/ppermute | solution.py:20
  9.9 9.6 %collective-permute-start.2 = (f32[4,192]{1,0:T(4,128)S(1)}, f32[4,192]{1,0:T(4,128)S(1)}, u32[]{:S(2)}, u32[]{:S(2)}) collective-permute-start(f32[4,192]{1,0:T(4,128)S(1)} %get-tuple-element.41.refs_1_), channel_id=1, source_target_pairs={{0,1},{1,0},{2,3},{3,2},{4,5},{5,4},{6,7},{7,6},{8,9},{9,8},{10,11... | collective-permute-start | bytes 9224 | tf_op jit(solution)/shard_map/ppermute | solution.py:20
  20.0 9.7 %collective-permute-start.8 = (bf16[128,1152]{1,0:T(8,128)(2,1)S(1)}, bf16[128,1152]{1,0:T(8,128)(2,1)S(1)}, u32[]{:S(2)}, u32[]{:S(2)}) collective-permute-start(bf16[128,1152]{1,0:T(8,128)(2,1)S(1)} %collective-permute-done.refs_0_), channel_id=1, source_target_pairs={{0,4},{4,0},{8,12},{12,8},{1,5},{5,1},{9,13},{13,9},{2,6},{6,2},{1... | collective-permute-start | bytes 884744 | tf_op jit(solution)/shard_map/ppermute | solution.py:20
  22.4 1.5 %collective-permute-start.6 = (bf16[2,128,384]{2,1,0:T(8,128)(2,1)S(1)}, bf16[2,128,384]{2,1,0:T(8,128)(2,1)S(1)}, u32[]{:S(2)}, u32[]{:S(2)}) collective-permute-start(bf16[2,128,384]{2,1,0:T(8,128)(2,1)S(1)} %shard_map.92), channel_id=1, source_target_pairs={{0,1},{1,0},{2,3},{3,2},{4,5},{5,4},{6,7},{7,6},{8,9},{9,8},{10,11... | collective-permute-start | bytes 589832 | tf_op jit(solution)/shard_map/ppermute | solution.py:20
  22.9 7.3 %collective-permute-start.3 = (bf16[1,128,384]{2,1,0:T(8,128)(2,1)S(1)}, bf16[1,128,384]{2,1,0:T(8,128)(2,1)S(1)}, u32[]{:S(2)}, u32[]{:S(2)}) collective-permute-start(bf16[1,128,384]{2,1,0:T(8,128)(2,1)S(1)} %shard_map.91), channel_id=1, source_target_pairs={{0,1},{1,0},{2,3},{3,2},{4,5},{5,4},{6,7},{7,6},{8,9},{9,8},{10,11... | collective-permute-start | bytes 294920 | tf_op jit(solution)/shard_map/ppermute | solution.py:20
  30.1 1.4 %collective-permute-start.9 = (bf16[1,128,384]{2,1,0:T(8,128)(2,1)S(1)}, bf16[1,128,384]{2,1,0:T(8,128)(2,1)S(1)}, u32[]{:S(2)}, u32[]{:S(2)}) collective-permute-start(bf16[1,128,384]{2,1,0:T(8,128)(2,1)S(1)} %shard_map.95), channel_id=1, source_target_pairs={{0,1},{1,0},{2,3},{3,2},{4,5},{5,4},{6,7},{7,6},{8,9},{9,8},{10,11... | collective-permute-start | bytes 294920 | tf_op jit(solution)/shard_map/ppermute | solution.py:20
  31.5 5.7 %collective-permute-start.10 = (bf16[1,128,384]{2,1,0:T(8,128)(2,1)S(1)}, bf16[1,128,384]{2,1,0:T(8,128)(2,1)S(1)}, u32[]{:S(2)}, u32[]{:S(2)}) collective-permute-start(bf16[1,128,384]{2,1,0:T(8,128)(2,1)S(1)} %add_convert_fusion.1), channel_id=1, source_target_pairs={{0,2},{2,0},{1,3},{3,1},{4,6},{6,4},{5,7},{7,5},{8,10},{10,8},{9,1... | collective-permute-start | bytes 294920 | tf_op jit(solution)/shard_map/ppermute | solution.py:20
  33.2 7.4 %collective-permute-start.7 = (bf16[2,128,384]{2,1,0:T(8,128)(2,1)S(1)}, bf16[2,128,384]{2,1,0:T(8,128)(2,1)S(1)}, u32[]{:S(2)}, u32[]{:S(2)}) collective-permute-start(bf16[2,128,384]{2,1,0:T(8,128)(2,1)S(1)} %add_convert_fusion), channel_id=1, source_target_pairs={{0,2},{2,0},{1,3},{3,1},{4,6},{6,4},{5,7},{7,5},{8,10},{10,8},{9,1... | collective-permute-start | bytes 589832 | tf_op jit(solution)/shard_map/ppermute | solution.py:20
  37.6 6.0 %collective-permute-start.11 = (bf16[64,1152]{1,0:T(8,128)(2,1)S(1)}, bf16[64,1152]{1,0:T(8,128)(2,1)S(1)}, u32[]{:S(2)}, u32[]{:S(2)}) collective-permute-start(bf16[64,1152]{1,0:T(8,128)(2,1)S(1)} %get-tuple-element.49), channel_id=1, source_target_pairs={{0,4},{4,0},{8,12},{12,8},{1,5},{5,1},{9,13},{13,9},{2,6},{6,2},{1... | collective-permute-start | bytes 442376 | tf_op jit(solution)/shard_map/ppermute | solution.py:20
  39.1 9.4 %collective-permute-start.15 = (bf16[64,1152]{1,0:T(8,128)(2,1)S(1)}, bf16[64,1152]{1,0:T(8,128)(2,1)S(1)}, u32[]{:S(2)}, u32[]{:S(2)}) collective-permute-start(bf16[64,1152]{1,0:T(8,128)(2,1)S(1)} %get-tuple-element.56), channel_id=1, source_target_pairs={{0,4},{4,0},{8,12},{12,8},{1,5},{5,1},{9,13},{13,9},{2,6},{6,2},{1... | collective-permute-start | bytes 442376 | tf_op jit(solution)/shard_map/ppermute | solution.py:20
  40.7 16.5 %copy-start = (f32[1,2304]{1,0:T(1,128)S(1)}, f32[1,2304]{1,0:T(1,128)}, u32[]{:S(2)}) copy-start(f32[1,2304]{1,0:T(1,128)} %bias_ref.3) | copy-start | bytes 27652
  43.6 6.0 %collective-permute-start.12 = (bf16[1,128,384]{2,1,0:T(8,128)(2,1)S(1)}, bf16[1,128,384]{2,1,0:T(8,128)(2,1)S(1)}, u32[]{:S(2)}, u32[]{:S(2)}) collective-permute-start(bf16[1,128,384]{2,1,0:T(8,128)(2,1)S(1)} %add_convert_fusion.2), channel_id=1, source_target_pairs={{0,2},{2,0},{1,3},{3,1},{4,6},{6,4},{5,7},{7,5},{8,10},{10,8},{9,1... | collective-permute-start | bytes 294920 | tf_op jit(solution)/shard_map/ppermute | solution.py:20
  45.2 11.9 %collective-permute-start.13 = (bf16[128,1152]{1,0:T(8,128)(2,1)S(1)}, bf16[128,1152]{1,0:T(8,128)(2,1)S(1)}, u32[]{:S(2)}, u32[]{:S(2)}) collective-permute-start(bf16[128,1152]{1,0:T(8,128)(2,1)S(1)} %get-tuple-element.52), channel_id=1, source_target_pairs={{0,4},{4,0},{8,12},{12,8},{1,5},{5,1},{9,13},{13,9},{2,6},{6,2},{1... | collective-permute-start | bytes 884744 | tf_op jit(solution)/shard_map/ppermute | solution.py:20
  46.5 8.7 %collective-permute-start.14 = (bf16[64,1152]{1,0:T(8,128)(2,1)S(1)}, bf16[64,1152]{1,0:T(8,128)(2,1)S(1)}, u32[]{:S(2)}, u32[]{:S(2)}) collective-permute-start(bf16[64,1152]{1,0:T(8,128)(2,1)S(1)} %shard_map.98), channel_id=1, source_target_pairs={{0,8},{4,12},{8,0},{12,4},{1,9},{5,13},{9,1},{13,5},{2,10},{6,14},... | collective-permute-start | bytes 442376 | tf_op jit(solution)/shard_map/ppermute | solution.py:20
  48.5 12.3 %collective-permute-start.16 = (bf16[64,1152]{1,0:T(8,128)(2,1)S(1)}, bf16[64,1152]{1,0:T(8,128)(2,1)S(1)}, u32[]{:S(2)}, u32[]{:S(2)}) collective-permute-start(bf16[64,1152]{1,0:T(8,128)(2,1)S(1)} %shard_map.100), channel_id=1, source_target_pairs={{0,8},{4,12},{8,0},{12,4},{1,9},{5,13},{9,1},{13,5},{2,10},{6,14},... | collective-permute-start | bytes 442376 | tf_op jit(solution)/shard_map/ppermute | solution.py:20
  57.2 10.7 %collective-permute-start.20 = (bf16[64,1152]{1,0:T(8,128)(2,1)S(1)}, bf16[64,1152]{1,0:T(8,128)(2,1)S(1)}, u32[]{:S(2)}, u32[]{:S(2)}) collective-permute-start(bf16[64,1152]{1,0:T(8,128)(2,1)S(1)} %shard_map.99.refs_0_.error_ref), channel_id=1, source_target_pairs={{0,4},{4,0},{8,12},{12,8},{1,5},{5,1},{9,13},{13,9},{2,6},{6,2},{1... | collective-permute-start | bytes 442376 | tf_op jit(solution)/shard_map/ppermute | solution.py:20
  57.9 10.4 %collective-permute-start.19 = (bf16[64,1152]{1,0:T(8,128)(2,1)S(1)}, bf16[64,1152]{1,0:T(8,128)(2,1)S(1)}, u32[]{:S(2)}, u32[]{:S(2)}) collective-permute-start(bf16[64,1152]{1,0:T(8,128)(2,1)S(1)} %shard_map.99.refs_0_.error_ref), channel_id=1, source_target_pairs={{0,8},{4,12},{8,0},{12,4},{1,9},{5,13},{9,1},{13,5},{2,10},{6,14},... | collective-permute-start | bytes 442376 | tf_op jit(solution)/shard_map/ppermute | solution.py:20
  60.9 11.2 %collective-permute-start.22 = (bf16[64,1152]{1,0:T(8,128)(2,1)S(1)}, bf16[64,1152]{1,0:T(8,128)(2,1)S(1)}, u32[]{:S(2)}, u32[]{:S(2)}) collective-permute-start(bf16[64,1152]{1,0:T(8,128)(2,1)S(1)} %shard_map.101.refs_1_.error_ref), channel_id=1, source_target_pairs={{0,4},{4,0},{8,12},{12,8},{1,5},{5,1},{9,13},{13,9},{2,6},{6,2},{1... | collective-permute-start | bytes 442376 | tf_op jit(solution)/shard_map/ppermute | solution.py:20
  61.0 11.5 %collective-permute-start.21 = (bf16[64,1152]{1,0:T(8,128)(2,1)S(1)}, bf16[64,1152]{1,0:T(8,128)(2,1)S(1)}, u32[]{:S(2)}, u32[]{:S(2)}) collective-permute-start(bf16[64,1152]{1,0:T(8,128)(2,1)S(1)} %shard_map.101.refs_1_.error_ref), channel_id=1, source_target_pairs={{0,8},{4,12},{8,0},{12,4},{1,9},{5,13},{9,1},{13,5},{2,10},{6,14},... | collective-permute-start | bytes 442376 | tf_op jit(solution)/shard_map/ppermute | solution.py:20
  63.6 17.5 %collective-permute-start.17 = (bf16[64,1152]{1,0:T(8,128)(2,1)S(1)}, bf16[64,1152]{1,0:T(8,128)(2,1)S(1)}, u32[]{:S(2)}, u32[]{:S(2)}) collective-permute-start(bf16[64,1152]{1,0:T(8,128)(2,1)S(1)} %shard_map.99.refs_0_.error_ref), channel_id=1, source_target_pairs={{0,1},{1,0},{2,3},{3,2},{4,5},{5,4},{6,7},{7,6},{8,9},{9,8},{10,11... | collective-permute-start | bytes 442376 | tf_op jit(solution)/shard_map/ppermute | solution.py:20
  67.9 13.1 %collective-permute-start.18 = (bf16[64,1152]{1,0:T(8,128)(2,1)S(1)}, bf16[64,1152]{1,0:T(8,128)(2,1)S(1)}, u32[]{:S(2)}, u32[]{:S(2)}) collective-permute-start(bf16[64,1152]{1,0:T(8,128)(2,1)S(1)} %shard_map.101.refs_1_.error_ref), channel_id=1, source_target_pairs={{0,1},{1,0},{2,3},{3,2},{4,5},{5,4},{6,7},{7,6},{8,9},{9,8},{10,11... | collective-permute-start | bytes 442376 | tf_op jit(solution)/shard_map/ppermute | solution.py:20
  68.3 9.0 %collective-permute-start.23 = (bf16[64,1152]{1,0:T(8,128)(2,1)S(1)}, bf16[64,1152]{1,0:T(8,128)(2,1)S(1)}, u32[]{:S(2)}, u32[]{:S(2)}) collective-permute-start(bf16[64,1152]{1,0:T(8,128)(2,1)S(1)} %collective-permute-done.19.error_ref), channel_id=1, source_target_pairs={{0,4},{4,0},{8,12},{12,8},{1,5},{5,1},{9,13},{13,9},{2,6},{6,2},{1... | collective-permute-start | bytes 442376 | tf_op jit(solution)/shard_map/ppermute | solution.py:20
  72.6 5.7 %collective-permute-start.24 = (bf16[64,1152]{1,0:T(8,128)(2,1)S(1)}, bf16[64,1152]{1,0:T(8,128)(2,1)S(1)}, u32[]{:S(2)}, u32[]{:S(2)}) collective-permute-start(bf16[64,1152]{1,0:T(8,128)(2,1)S(1)} %collective-permute-done.21.error_ref), channel_id=1, source_target_pairs={{0,4},{4,0},{8,12},{12,8},{1,5},{5,1},{9,13},{13,9},{2,6},{6,2},{1... | collective-permute-start | bytes 442376 | tf_op jit(solution)/shard_map/ppermute | solution.py:20
  78.8 3.7 %collective-permute-start.26 = (f32[4,192]{1,0:T(4,128)S(1)}, f32[4,192]{1,0:T(4,128)S(1)}, u32[]{:S(2)}, u32[]{:S(2)}) collective-permute-start(f32[4,192]{1,0:T(4,128)S(1)} %get-tuple-element.64), channel_id=1, source_target_pairs={{0,2},{2,0},{1,3},{3,1},{4,6},{6,4},{5,7},{7,5},{8,10},{10,8},{9,1... | collective-permute-start | bytes 9224 | tf_op jit(solution)/shard_map/ppermute | solution.py:20
  80.3 3.0 %collective-permute-start.27 = (f32[4,192]{1,0:T(4,128)S(1)}, f32[4,192]{1,0:T(4,128)S(1)}, u32[]{:S(2)}, u32[]{:S(2)}) collective-permute-start(f32[4,192]{1,0:T(4,128)S(1)} %get-tuple-element.65), channel_id=1, source_target_pairs={{0,3},{1,2},{2,1},{3,0},{4,7},{5,6},{6,5},{7,4},{8,11},{9,10},{10,... | collective-permute-start | bytes 9224 | tf_op jit(solution)/shard_map/ppermute | solution.py:26
  80.3 3.0 %collective-permute-start.25 = (f32[4,192]{1,0:T(4,128)S(1)}, f32[4,192]{1,0:T(4,128)S(1)}, u32[]{:S(2)}, u32[]{:S(2)}) collective-permute-start(f32[4,192]{1,0:T(4,128)S(1)} %get-tuple-element.65), channel_id=1, source_target_pairs={{0,1},{1,0},{2,3},{3,2},{4,5},{5,4},{6,7},{7,6},{8,9},{9,8},{10,11... | collective-permute-start | bytes 9224 | tf_op jit(solution)/shard_map/ppermute | solution.py:20

commit v6 on v5

--- a/solution.py
+++ b/solution.py
@@ -350,9 +350,11 @@
 
     def body(error_ref, code_ref, own_ref, other_ref, out_ref):
         for i, weight_ref in enumerate((own_ref, other_ref)):
-            code = code_ref[:, i * SLOT : (i + 1) * SLOT].astype(jnp.float32)
-            grad = across(error_ref[...], weight_ref[...])
-            out_ref[i : i + 1, :] = jnp.sum(code * grad, axis=0, keepdims=True)
+            moment = lax.dot_general(
+                code_ref[:, i * SLOT : (i + 1) * SLOT], error_ref[...], (((0,), (0,)), ((), ())),
+                preferred_element_type=jnp.float32,
+            )
+            out_ref[i, :] = jnp.sum(moment * weight_ref[...].astype(jnp.float32), axis=1)
 
     return pl.pallas_call(
         body,

time: 85.3 us -> 85.2 us (level)
  starting transfers between devices: 29.2 us -> 23.7 us
  waiting for transfers between devices: 28.8 us -> 33.8 us
  Pallas kernels: 25.5 us -> 26.6 us
    ppermute x27, starting transfers between devices: 29.2 us -> 23.7 us  [swap(): return lax.ppermute(value, axis, [(i, i ^ mask) for i in range(size)])]
    ppermute x27, waiting for transfers between devices: 27.9 us -> 33 us  [swap(): return lax.ppermute(value, axis, [(i, i ^ mask) for i in range(size)])]
    pallas_call x2, Pallas kernels: 5.02 us -> 6.03 us  [decoder_slots(): pl.pallas_call(body, grid_spec=pltpu.PrefetchScalarGridSpec(num_scalar_pr...]
  transfers between devices with their start and end apart: 28 -> 28, of which waited for: 16 -> 16; matrix products, arithmetic and copies ran while one was open for 0% -> 0% of each run, Pallas kernels for 29% -> 30%
where the time goes in v6:
time: 85.2 us; the launch traced here: 85.3 us
  waiting for transfers between devices  33.8 us (40%)
  Pallas kernels  26.6 us (31%)
  starting transfers between devices  23.7 us (28%)
  between operations  0.89 us (1%)
    ppermute x27, waiting for transfers between devices, swap(): return lax.ppermute(value, axis, [(i, i ^ mask) for i in range(size)])  33 us
    ppermute x27, starting transfers between devices, swap(): return lax.ppermute(value, axis, [(i, i ^ mask) for i in range(size)])  23.7 us
    pallas_call x2, Pallas kernels, encoder_slots(): pl.pallas_call(body, grid_spec=pltpu.PrefetchScalarGridSpec(num_scalar_pr...  8.24 us
    pallas_call x2, Pallas kernels, decoder_slots(): pl.pallas_call(body, grid_spec=pltpu.PrefetchScalarGridSpec(num_scalar_pr...  6.03 us
    pallas_call x8, Pallas kernels, gradient(): pl.pallas_call(body, grid=(1,), in_specs=[whole((rows, half)), pl.BlockSp...  4.1 us
    pallas_call x1, Pallas kernels, plan(): pl.pallas_call(body, grid=(1,), in_specs=[smem] * 3 + [whole((latents //...  1.96 us
  transfers between devices with their start and end apart: 28, of which 16 were waited for; matrix products, arithmetic and copies ran while one was open for 0% of the time, Pallas kernels for 30%

profile of v6, /device:TPU:0, one launch (start us, length us, event | category | flops | bytes accessed | tf_op | source)
XLA Modules:
  0.0 85.3 jit_solution(5092517161752532171)
XLA Ops:
  0.6 0.5 collective-permute-start.1
  1.1 0.1 collective-permute-start.5
  1.2 1.0 %shard_map.86.refs_0_.token_ref = bf16[128,1152]{1,0:T(8,128)(2,1)S(1)} custom-call(s32[1]{0:T(128)} %bitcast.core_ref, bf16[128,2304]{1,0:T(8,128)(2,1)} %bitcast.16), custom_call_target="tpu_custom_call" | custom-call | tf_op jit(solution)/shard_map/pallas_call | solution.py:56
  2.2 4.1 %collective-permute-start = (bf16[128,1152]{1,0:T(8,128)(2,1)S(1)}, bf16[128,1152]{1,0:T(8,128)(2,1)S(1)}, u32[]{:S(2)}, u32[]{:S(2)}) collective-permute-start(bf16[128,1152]{1,0:T(8,128)(2,1)S(1)} %shard_map.86.refs_0_.token_ref), channel_id=1, source_target_pairs={{0,8},{4,12},{8,0},{12,4},{1,9},{5,13},{9,1},{13,5},{2,10},{6,14},... | collective-permute-start | bytes 884744 | tf_op jit(solution)/shard_map/ppermute | solution.py:20
  6.3 1.6 %collective-permute-start.4 = (bf16[128,1152]{1,0:T(8,128)(2,1)S(1)}, bf16[128,1152]{1,0:T(8,128)(2,1)S(1)}, u32[]{:S(2)}, u32[]{:S(2)}) collective-permute-start(bf16[128,1152]{1,0:T(8,128)(2,1)S(1)} %shard_map.86.refs_0_.token_ref), channel_id=1, source_target_pairs={{0,4},{4,0},{8,12},{12,8},{1,5},{5,1},{9,13},{13,9},{2,6},{6,2},{1... | collective-permute-start | bytes 884744 | tf_op jit(solution)/shard_map/ppermute | solution.py:20
  7.9 0.1 pad_add_fusion.places_ref
  7.9 2.0 %shard_map.87 = (s32[12]{0:T(128)S(1)}, s32[12]{0:T(128)S(1)}, f32[4,192]{1,0:T(4,128)S(1)}) custom-call(s32[4,16]{1,0:T(4,128)} %ids_ref.1, s32[4]{0:T(128)} %counts_ref.1, s32[2]{0:T(128)S(1)} %pad_add_fusion.places_ref, f32[8,128]{1,0:T(8,128)} %bitcast.18), custom_call_target="tpu_custom_call" | custom-call | tf_op jit(solution)/shard_map/pallas_call | solution.py:117
  9.9 0.1 collective-permute-start.2
  10.0 3.1 %shard_map.90.refs_3_.refs_5_.own_ref = bf16[4,192,1152]{2,1,0:T(8,128)(2,1)S(1)} custom-call(s32[12]{0:T(128)S(1)} %get-tuple-element.34.pick_ref, s32[1]{0:T(128)} %bitcast.core_ref, bf16[1024,2304]{1,0:T(8,128)(2,1)} %bitcast.13, bf16[1024,2304]{1,0:T(8,128)(2,1)} %bitcast.14, bf16[1024,2304]{1,0:T(8,128)(2,1)} %bitcast.15), custom_call_target="tpu_custom_call" | custom-call | tf_op jit(solution)/shard_map/pallas_call | solution.py:181
  13.1 4.1 %shard_map.88.refs_1_.refs_2_.refs_4_ = bf16[4,1152,192]{2,1,0:T(8,128)(2,1)S(1)} custom-call(s32[12]{0:T(128)S(1)} %get-tuple-element.34.pick_ref, s32[1]{0:T(128)} %bitcast.core_ref, bf16[2304,1024]{1,0:T(8,128)(2,1)} %bitcast.10, bf16[2304,1024]{1,0:T(8,128)(2,1)} %bitcast.11, bf16[2304,1024]{1,0:T(8,128)(2,1)} %bitcast.12), custom_call_target="tpu_custom_call" | custom-call | tf_op jit(solution)/shard_map/pallas_call | solution.py:154
  17.2 4.2 %shard_map.89.refs_2_.refs_3_.refs_5_ = bf16[4,1152,192]{2,1,0:T(8,128)(2,1)S(1)} custom-call(s32[12]{0:T(128)S(1)} %get-tuple-element.35.pick_ref, s32[1]{0:T(128)} %bitcast.core_ref, bf16[2304,1024]{1,0:T(8,128)(2,1)} %bitcast.5.refs_0_.refs_1_.refs_2_, bf16[2304,1024]{1,0:T(8,128)(2,1)} %bitcast.5.refs_0_.refs_1_.refs_2_, ...), custom_call_target="tpu_custom_call" | custom-call | tf_op jit(solution)/shard_map/pallas_call | solution.py:154
  21.3 0.1 collective-permute-start.8
  21.4 0.6 shard_map.92
  22.0 0.4 collective-permute-start.6
  22.4 0.4 shard_map.91
  22.8 0.3 collective-permute-start.3
  23.1 0.5 collective-permute-done.6
  23.5 3.0 %shard_map.93.refs_4_.refs_6_.other_ref = bf16[4,192,1152]{2,1,0:T(8,128)(2,1)S(1)} custom-call(s32[12]{0:T(128)S(1)} %get-tuple-element.35.pick_ref, s32[1]{0:T(128)} %bitcast.core_ref, bf16[1024,2304]{1,0:T(8,128)(2,1)} %bitcast.7.refs_0_.refs_1_.refs_2_, bf16[1024,2304]{1,0:T(8,128)(2,1)} %bitcast.7.refs_0_.refs_1_.refs_2_, ...), custom_call_target="tpu_custom_call" | custom-call | tf_op jit(solution)/shard_map/pallas_call | solution.py:181
  26.5 4.1 %collective-permute-done.8.refs_0_ = bf16[128,1152]{1,0:T(8,128)(2,1)S(1)} collective-permute-done((bf16[128,1152]{1,0:T(8,128)(2,1)S(1)}, bf16[128,1152]{1,0:T(8,128)(2,1)S(1)}, u32[]{:S(2)}, u32[]{:S(2)}) %collective-permute-start.8) | collective-permute-done | bytes 294944 | tf_op jit(solution)/shard_map/ppermute | solution.py:20
  30.6 0.4 shard_map.95
  31.2 1.2 %collective-permute-done.9 = bf16[1,128,384]{2,1,0:T(8,128)(2,1)S(1)} collective-permute-done((bf16[1,128,384]{2,1,0:T(8,128)(2,1)S(1)}, bf16[1,128,384]{2,1,0:T(8,128)(2,1)S(1)}, u32[]{:S(2)}, u32[]{:S(2)}) %collective-permute-start.9) | collective-permute-done | bytes 98336 | tf_op jit(solution)/shard_map/ppermute | solution.py:20
  32.4 1.6 %collective-permute-start.10 = (bf16[1,128,384]{2,1,0:T(8,128)(2,1)S(1)}, bf16[1,128,384]{2,1,0:T(8,128)(2,1)S(1)}, u32[]{:S(2)}, u32[]{:S(2)}) collective-permute-start(bf16[1,128,384]{2,1,0:T(8,128)(2,1)S(1)} %add_convert_fusion.1), channel_id=1, source_target_pairs={{0,2},{2,0},{1,3},{3,1},{4,6},{6,4},{5,7},{7,5},{8,10},{10,8},{9,1... | collective-permute-start | bytes 294920 | tf_op jit(solution)/shard_map/ppermute | solution.py:20
  34.1 0.6 collective-permute-start.7
  34.7 3.5 %collective-permute-done.10 = bf16[1,128,384]{2,1,0:T(8,128)(2,1)S(1)} collective-permute-done((bf16[1,128,384]{2,1,0:T(8,128)(2,1)S(1)}, bf16[1,128,384]{2,1,0:T(8,128)(2,1)S(1)}, u32[]{:S(2)}, u32[]{:S(2)}) %collective-permute-start.10) | collective-permute-done | bytes 98336 | tf_op jit(solution)/shard_map/ppermute | solution.py:20
  38.2 0.5 shard_map.96
  38.6 0.3 collective-permute-start.11
  39.0 1.8 %collective-permute-start.15 = (bf16[64,1152]{1,0:T(8,128)(2,1)S(1)}, bf16[64,1152]{1,0:T(8,128)(2,1)S(1)}, u32[]{:S(2)}, u32[]{:S(2)}) collective-permute-start(bf16[64,1152]{1,0:T(8,128)(2,1)S(1)} %get-tuple-element.56), channel_id=1, source_target_pairs={{0,4},{4,0},{8,12},{12,8},{1,5},{5,1},{9,13},{13,9},{2,6},{6,2},{1... | collective-permute-start | bytes 442376 | tf_op jit(solution)/shard_map/ppermute | solution.py:20
  40.7 0.9 %collective-permute-done.7 = bf16[2,128,384]{2,1,0:T(8,128)(2,1)S(1)} collective-permute-done((bf16[2,128,384]{2,1,0:T(8,128)(2,1)S(1)}, bf16[2,128,384]{2,1,0:T(8,128)(2,1)S(1)}, u32[]{:S(2)}, u32[]{:S(2)}) %collective-permute-start.7) | collective-permute-done | bytes 196640 | tf_op jit(solution)/shard_map/ppermute | solution.py:20
  41.6 0.6 shard_map.94
  42.3 2.3 %collective-permute-done.11.arrived_ref = bf16[64,1152]{1,0:T(8,128)(2,1)S(1)} collective-permute-done((bf16[64,1152]{1,0:T(8,128)(2,1)S(1)}, bf16[64,1152]{1,0:T(8,128)(2,1)S(1)}, u32[]{:S(2)}, u32[]{:S(2)}) %collective-permute-start.11) | collective-permute-done | bytes 147488 | tf_op jit(solution)/shard_map/ppermute | solution.py:20
  44.6 1.5 %collective-permute-start.12 = (bf16[1,128,384]{2,1,0:T(8,128)(2,1)S(1)}, bf16[1,128,384]{2,1,0:T(8,128)(2,1)S(1)}, u32[]{:S(2)}, u32[]{:S(2)}) collective-permute-start(bf16[1,128,384]{2,1,0:T(8,128)(2,1)S(1)} %add_convert_fusion.2), channel_id=1, source_target_pairs={{0,2},{2,0},{1,3},{3,1},{4,6},{6,4},{5,7},{7,5},{8,10},{10,8},{9,1... | collective-permute-start | bytes 294920 | tf_op jit(solution)/shard_map/ppermute | solution.py:20
  46.1 0.3 collective-permute-start.13
  46.4 2.1 %collective-permute-start.14 = (bf16[64,1152]{1,0:T(8,128)(2,1)S(1)}, bf16[64,1152]{1,0:T(8,128)(2,1)S(1)}, u32[]{:S(2)}, u32[]{:S(2)}) collective-permute-start(bf16[64,1152]{1,0:T(8,128)(2,1)S(1)} %shard_map.98), channel_id=1, source_target_pairs={{0,8},{4,12},{8,0},{12,4},{1,9},{5,13},{9,1},{13,5},{2,10},{6,14},... | collective-permute-start | bytes 442376 | tf_op jit(solution)/shard_map/ppermute | solution.py:20
  48.5 1.0 %collective-permute-start.16 = (bf16[64,1152]{1,0:T(8,128)(2,1)S(1)}, bf16[64,1152]{1,0:T(8,128)(2,1)S(1)}, u32[]{:S(2)}, u32[]{:S(2)}) collective-permute-start(bf16[64,1152]{1,0:T(8,128)(2,1)S(1)} %shard_map.100), channel_id=1, source_target_pairs={{0,8},{4,12},{8,0},{12,4},{1,9},{5,13},{9,1},{13,5},{2,10},{6,14},... | collective-permute-start | bytes 442376 | tf_op jit(solution)/shard_map/ppermute | solution.py:20
  49.5 0.5 shard_map.97
  50.0 5.0 %collective-permute-done.14.refs_1_ = bf16[64,1152]{1,0:T(8,128)(2,1)S(1)} collective-permute-done((bf16[64,1152]{1,0:T(8,128)(2,1)S(1)}, bf16[64,1152]{1,0:T(8,128)(2,1)S(1)}, u32[]{:S(2)}, u32[]{:S(2)}) %collective-permute-start.14) | collective-permute-done | bytes 147488 | tf_op jit(solution)/shard_map/ppermute | solution.py:20
  55.0 3.1 %collective-permute-done.13.refs_0_ = bf16[128,1152]{1,0:T(8,128)(2,1)S(1)} collective-permute-done((bf16[128,1152]{1,0:T(8,128)(2,1)S(1)}, bf16[128,1152]{1,0:T(8,128)(2,1)S(1)}, u32[]{:S(2)}, u32[]{:S(2)}) %collective-permute-start.13) | collective-permute-done | bytes 294944 | tf_op jit(solution)/shard_map/ppermute | solution.py:20
  58.2 0.1 shard_map.99.refs_0_.error_ref
  58.3 2.3 %collective-permute-start.19 = (bf16[64,1152]{1,0:T(8,128)(2,1)S(1)}, bf16[64,1152]{1,0:T(8,128)(2,1)S(1)}, u32[]{:S(2)}, u32[]{:S(2)}) collective-permute-start(bf16[64,1152]{1,0:T(8,128)(2,1)S(1)} %shard_map.99.refs_0_.error_ref), channel_id=1, source_target_pairs={{0,8},{4,12},{8,0},{12,4},{1,9},{5,13},{9,1},{13,5},{2,10},{6,14},... | collective-permute-start | bytes 442376 | tf_op jit(solution)/shard_map/ppermute | solution.py:20
  60.6 0.1 shard_map.101.refs_1_.error_ref
  60.7 0.1 collective-permute-start.22
  60.9 2.6 %collective-permute-start.21 = (bf16[64,1152]{1,0:T(8,128)(2,1)S(1)}, bf16[64,1152]{1,0:T(8,128)(2,1)S(1)}, u32[]{:S(2)}, u32[]{:S(2)}) collective-permute-start(bf16[64,1152]{1,0:T(8,128)(2,1)S(1)} %shard_map.101.refs_1_.error_ref), channel_id=1, source_target_pairs={{0,8},{4,12},{8,0},{12,4},{1,9},{5,13},{9,1},{13,5},{2,10},{6,14},... | collective-permute-start | bytes 442376 | tf_op jit(solution)/shard_map/ppermute | solution.py:20
  63.4 0.5 shard_map.103.refs_0_
  64.0 0.5 shard_map.104.refs_1_
  64.5 0.1 collective-permute-start.17
  64.6 4.0 %collective-permute-done.20.error_ref = bf16[64,1152]{1,0:T(8,128)(2,1)S(1)} collective-permute-done((bf16[64,1152]{1,0:T(8,128)(2,1)S(1)}, bf16[64,1152]{1,0:T(8,128)(2,1)S(1)}, u32[]{:S(2)}, u32[]{:S(2)}) %collective-permute-start.20) | collective-permute-done | bytes 147488 | tf_op jit(solution)/shard_map/ppermute | solution.py:20
  68.6 0.9 %collective-permute-done.19.error_ref = bf16[64,1152]{1,0:T(8,128)(2,1)S(1)} collective-permute-done((bf16[64,1152]{1,0:T(8,128)(2,1)S(1)}, bf16[64,1152]{1,0:T(8,128)(2,1)S(1)}, u32[]{:S(2)}, u32[]{:S(2)}) %collective-permute-start.19) | collective-permute-done | bytes 147488 | tf_op jit(solution)/shard_map/ppermute | solution.py:20
  69.5 2.3 %collective-permute-done.22.error_ref = bf16[64,1152]{1,0:T(8,128)(2,1)S(1)} collective-permute-done((bf16[64,1152]{1,0:T(8,128)(2,1)S(1)}, bf16[64,1152]{1,0:T(8,128)(2,1)S(1)}, u32[]{:S(2)}, u32[]{:S(2)}) %collective-permute-start.22) | collective-permute-done | bytes 147488 | tf_op jit(solution)/shard_map/ppermute | solution.py:20
  71.7 2.2 %collective-permute-done.21.error_ref = bf16[64,1152]{1,0:T(8,128)(2,1)S(1)} collective-permute-done((bf16[64,1152]{1,0:T(8,128)(2,1)S(1)}, bf16[64,1152]{1,0:T(8,128)(2,1)S(1)}, u32[]{:S(2)}, u32[]{:S(2)}) %collective-permute-start.21) | collective-permute-done | bytes 147488 | tf_op jit(solution)/shard_map/ppermute | solution.py:20
  73.9 0.2 collective-permute-start.24
  74.1 0.5 shard_map.105.refs_2_
  74.7 0.5 shard_map.107.refs_4_
  75.2 0.5 shard_map.106.refs_3_
  75.7 0.5 shard_map.108.refs_5_
  76.2 0.5 collective-permute-done.23.error_ref
  76.7 0.5 shard_map.109.refs_6_
  77.3 1.9 %collective-permute-done.24.error_ref = bf16[64,1152]{1,0:T(8,128)(2,1)S(1)} collective-permute-done((bf16[64,1152]{1,0:T(8,128)(2,1)S(1)}, bf16[64,1152]{1,0:T(8,128)(2,1)S(1)}, u32[]{:S(2)}, u32[]{:S(2)}) %collective-permute-start.24) | collective-permute-done | bytes 147488 | tf_op jit(solution)/shard_map/ppermute | solution.py:20
  79.1 0.5 shard_map.110.refs_7_
  79.6 1.4 %collective-permute-start.26 = (f32[4,192]{1,0:T(4,128)S(1)}, f32[4,192]{1,0:T(4,128)S(1)}, u32[]{:S(2)}, u32[]{:S(2)}) collective-permute-start(f32[4,192]{1,0:T(4,128)S(1)} %get-tuple-element.64), channel_id=1, source_target_pairs={{0,2},{2,0},{1,3},{3,1},{4,6},{6,4},{5,7},{7,5},{8,10},{10,8},{9,1... | collective-permute-start | bytes 9224 | tf_op jit(solution)/shard_map/ppermute | solution.py:20
  81.1 0.8 collective-permute-start.25
  81.9 0.9 %shard_map.102 = bf16[128,2304]{1,0:T(8,128)(2,1)} custom-call(s32[1]{0:T(128)} %bitcast.core_ref, bf16[64,1152]{1,0:T(8,128)(2,1)S(1)} %shard_map.99.refs_0_.error_ref, bf16[64,1152]{1,0:T(8,128)(2,1)S(1)} %shard_map.101.refs_1_.error_ref, bf16[64,1152]{1,0:T(8,128)(2,1)S(1)} %collective-permute-done.17.refs_2_, ...), custom_call_target="tpu_custom_call" | custom-call | tf_op jit(solution)/shard_map/pallas_call | solution.py:443
  82.7 0.6 collective-permute-done.26
  83.3 0.8 collective-permute-done.27
  84.1 1.2 %shard_map.112 = f32[8,128]{1,0:T(8,128)} custom-call(s32[12]{0:T(128)S(1)} %get-tuple-element.34.pick_ref, f32[4,192]{1,0:T(4,128)S(1)} %add_add_fusion.total_ref), custom_call_target="tpu_custom_call" | custom-call | tf_op jit(solution)/shard_map/pallas_call | solution.py:416
  (29 shorter events, 0.5 us)
Async XLA Ops:
  0.6 16.5 %collective-permute-start.1 = (bf16[1,2304,1024]{2,1,0:T(8,128)(2,1)}, bf16[1,2304,1024]{2,1,0:T(8,128)(2,1)}, u32[]{:S(2)}, u32[]{:S(2)}) collective-permute-start(bf16[1,2304,1024]{2,1,0:T(8,128)(2,1)} %param.8), channel_id=1, source_target_pairs={{0,1},{1,0},{2,3},{3,2},{4,5},{5,4},{6,7},{7,6},{8,9},{9,8},{10,11... | collective-permute-start | bytes 14155784 | tf_op jit(solution)/shard_map/ppermute | solution.py:20
  1.1 21.9 %collective-permute-start.5 = (bf16[1,1024,2304]{2,1,0:T(8,128)(2,1)}, bf16[1,1024,2304]{2,1,0:T(8,128)(2,1)}, u32[]{:S(2)}, u32[]{:S(2)}) collective-permute-start(bf16[1,1024,2304]{2,1,0:T(8,128)(2,1)} %param.10), channel_id=1, source_target_pairs={{0,1},{1,0},{2,3},{3,2},{4,5},{5,4},{6,7},{7,6},{8,9},{9,8},{10,11... | collective-permute-start | bytes 14155784 | tf_op jit(solution)/shard_map/ppermute | solution.py:20
  2.2 19.1 %collective-permute-start = (bf16[128,1152]{1,0:T(8,128)(2,1)S(1)}, bf16[128,1152]{1,0:T(8,128)(2,1)S(1)}, u32[]{:S(2)}, u32[]{:S(2)}) collective-permute-start(bf16[128,1152]{1,0:T(8,128)(2,1)S(1)} %shard_map.86.refs_0_.token_ref), channel_id=1, source_target_pairs={{0,8},{4,12},{8,0},{12,4},{1,9},{5,13},{9,1},{13,5},{2,10},{6,14},... | collective-permute-start | bytes 884744 | tf_op jit(solution)/shard_map/ppermute | solution.py:20
  6.3 15.1 %collective-permute-start.4 = (bf16[128,1152]{1,0:T(8,128)(2,1)S(1)}, bf16[128,1152]{1,0:T(8,128)(2,1)S(1)}, u32[]{:S(2)}, u32[]{:S(2)}) collective-permute-start(bf16[128,1152]{1,0:T(8,128)(2,1)S(1)} %shard_map.86.refs_0_.token_ref), channel_id=1, source_target_pairs={{0,4},{4,0},{8,12},{12,8},{1,5},{5,1},{9,13},{13,9},{2,6},{6,2},{1... | collective-permute-start | bytes 884744 | tf_op jit(solution)/shard_map/ppermute | solution.py:20
  9.9 11.4 %collective-permute-start.2 = (f32[4,192]{1,0:T(4,128)S(1)}, f32[4,192]{1,0:T(4,128)S(1)}, u32[]{:S(2)}, u32[]{:S(2)}) collective-permute-start(f32[4,192]{1,0:T(4,128)S(1)} %get-tuple-element.41.refs_1_), channel_id=1, source_target_pairs={{0,1},{1,0},{2,3},{3,2},{4,5},{5,4},{6,7},{7,6},{8,9},{9,8},{10,11... | collective-permute-start | bytes 9224 | tf_op jit(solution)/shard_map/ppermute | solution.py:20
  21.3 9.3 %collective-permute-start.8 = (bf16[128,1152]{1,0:T(8,128)(2,1)S(1)}, bf16[128,1152]{1,0:T(8,128)(2,1)S(1)}, u32[]{:S(2)}, u32[]{:S(2)}) collective-permute-start(bf16[128,1152]{1,0:T(8,128)(2,1)S(1)} %collective-permute-done.refs_0_), channel_id=1, source_target_pairs={{0,4},{4,0},{8,12},{12,8},{1,5},{5,1},{9,13},{13,9},{2,6},{6,2},{1... | collective-permute-start | bytes 884744 | tf_op jit(solution)/shard_map/ppermute | solution.py:20
  22.0 1.5 %collective-permute-start.6 = (bf16[2,128,384]{2,1,0:T(8,128)(2,1)S(1)}, bf16[2,128,384]{2,1,0:T(8,128)(2,1)S(1)}, u32[]{:S(2)}, u32[]{:S(2)}) collective-permute-start(bf16[2,128,384]{2,1,0:T(8,128)(2,1)S(1)} %shard_map.92), channel_id=1, source_target_pairs={{0,1},{1,0},{2,3},{3,2},{4,5},{5,4},{6,7},{7,6},{8,9},{9,8},{10,11... | collective-permute-start | bytes 589832 | tf_op jit(solution)/shard_map/ppermute | solution.py:20
  22.8 8.3 %collective-permute-start.3 = (bf16[1,128,384]{2,1,0:T(8,128)(2,1)S(1)}, bf16[1,128,384]{2,1,0:T(8,128)(2,1)S(1)}, u32[]{:S(2)}, u32[]{:S(2)}) collective-permute-start(bf16[1,128,384]{2,1,0:T(8,128)(2,1)S(1)} %shard_map.91), channel_id=1, source_target_pairs={{0,1},{1,0},{2,3},{3,2},{4,5},{5,4},{6,7},{7,6},{8,9},{9,8},{10,11... | collective-permute-start | bytes 294920 | tf_op jit(solution)/shard_map/ppermute | solution.py:20
  31.1 1.4 %collective-permute-start.9 = (bf16[1,128,384]{2,1,0:T(8,128)(2,1)S(1)}, bf16[1,128,384]{2,1,0:T(8,128)(2,1)S(1)}, u32[]{:S(2)}, u32[]{:S(2)}) collective-permute-start(bf16[1,128,384]{2,1,0:T(8,128)(2,1)S(1)} %shard_map.95), channel_id=1, source_target_pairs={{0,1},{1,0},{2,3},{3,2},{4,5},{5,4},{6,7},{7,6},{8,9},{9,8},{10,11... | collective-permute-start | bytes 294920 | tf_op jit(solution)/shard_map/ppermute | solution.py:20
  32.4 5.7 %collective-permute-start.10 = (bf16[1,128,384]{2,1,0:T(8,128)(2,1)S(1)}, bf16[1,128,384]{2,1,0:T(8,128)(2,1)S(1)}, u32[]{:S(2)}, u32[]{:S(2)}) collective-permute-start(bf16[1,128,384]{2,1,0:T(8,128)(2,1)S(1)} %add_convert_fusion.1), channel_id=1, source_target_pairs={{0,2},{2,0},{1,3},{3,1},{4,6},{6,4},{5,7},{7,5},{8,10},{10,8},{9,1... | collective-permute-start | bytes 294920 | tf_op jit(solution)/shard_map/ppermute | solution.py:20
  34.1 7.5 %collective-permute-start.7 = (bf16[2,128,384]{2,1,0:T(8,128)(2,1)S(1)}, bf16[2,128,384]{2,1,0:T(8,128)(2,1)S(1)}, u32[]{:S(2)}, u32[]{:S(2)}) collective-permute-start(bf16[2,128,384]{2,1,0:T(8,128)(2,1)S(1)} %add_convert_fusion), channel_id=1, source_target_pairs={{0,2},{2,0},{1,3},{3,1},{4,6},{6,4},{5,7},{7,5},{8,10},{10,8},{9,1... | collective-permute-start | bytes 589832 | tf_op jit(solution)/shard_map/ppermute | solution.py:20
  38.6 6.0 %collective-permute-start.11 = (bf16[64,1152]{1,0:T(8,128)(2,1)S(1)}, bf16[64,1152]{1,0:T(8,128)(2,1)S(1)}, u32[]{:S(2)}, u32[]{:S(2)}) collective-permute-start(bf16[64,1152]{1,0:T(8,128)(2,1)S(1)} %get-tuple-element.49), channel_id=1, source_target_pairs={{0,4},{4,0},{8,12},{12,8},{1,5},{5,1},{9,13},{13,9},{2,6},{6,2},{1... | collective-permute-start | bytes 442376 | tf_op jit(solution)/shard_map/ppermute | solution.py:20
  39.0 9.5 %collective-permute-start.15 = (bf16[64,1152]{1,0:T(8,128)(2,1)S(1)}, bf16[64,1152]{1,0:T(8,128)(2,1)S(1)}, u32[]{:S(2)}, u32[]{:S(2)}) collective-permute-start(bf16[64,1152]{1,0:T(8,128)(2,1)S(1)} %get-tuple-element.56), channel_id=1, source_target_pairs={{0,4},{4,0},{8,12},{12,8},{1,5},{5,1},{9,13},{13,9},{2,6},{6,2},{1... | collective-permute-start | bytes 442376 | tf_op jit(solution)/shard_map/ppermute | solution.py:20
  41.6 16.5 %copy-start = (f32[1,2304]{1,0:T(1,128)S(1)}, f32[1,2304]{1,0:T(1,128)}, u32[]{:S(2)}) copy-start(f32[1,2304]{1,0:T(1,128)} %bias_ref.3) | copy-start | bytes 27652
  44.6 4.9 %collective-permute-start.12 = (bf16[1,128,384]{2,1,0:T(8,128)(2,1)S(1)}, bf16[1,128,384]{2,1,0:T(8,128)(2,1)S(1)}, u32[]{:S(2)}, u32[]{:S(2)}) collective-permute-start(bf16[1,128,384]{2,1,0:T(8,128)(2,1)S(1)} %add_convert_fusion.2), channel_id=1, source_target_pairs={{0,2},{2,0},{1,3},{3,1},{4,6},{6,4},{5,7},{7,5},{8,10},{10,8},{9,1... | collective-permute-start | bytes 294920 | tf_op jit(solution)/shard_map/ppermute | solution.py:20
  46.1 12.1 %collective-permute-start.13 = (bf16[128,1152]{1,0:T(8,128)(2,1)S(1)}, bf16[128,1152]{1,0:T(8,128)(2,1)S(1)}, u32[]{:S(2)}, u32[]{:S(2)}) collective-permute-start(bf16[128,1152]{1,0:T(8,128)(2,1)S(1)} %get-tuple-element.52), channel_id=1, source_target_pairs={{0,4},{4,0},{8,12},{12,8},{1,5},{5,1},{9,13},{13,9},{2,6},{6,2},{1... | collective-permute-start | bytes 884744 | tf_op jit(solution)/shard_map/ppermute | solution.py:20
  46.4 8.6 %collective-permute-start.14 = (bf16[64,1152]{1,0:T(8,128)(2,1)S(1)}, bf16[64,1152]{1,0:T(8,128)(2,1)S(1)}, u32[]{:S(2)}, u32[]{:S(2)}) collective-permute-start(bf16[64,1152]{1,0:T(8,128)(2,1)S(1)} %shard_map.98), channel_id=1, source_target_pairs={{0,8},{4,12},{8,0},{12,4},{1,9},{5,13},{9,1},{13,5},{2,10},{6,14},... | collective-permute-start | bytes 442376 | tf_op jit(solution)/shard_map/ppermute | solution.py:20
  48.5 12.1 %collective-permute-start.16 = (bf16[64,1152]{1,0:T(8,128)(2,1)S(1)}, bf16[64,1152]{1,0:T(8,128)(2,1)S(1)}, u32[]{:S(2)}, u32[]{:S(2)}) collective-permute-start(bf16[64,1152]{1,0:T(8,128)(2,1)S(1)} %shard_map.100), channel_id=1, source_target_pairs={{0,8},{4,12},{8,0},{12,4},{1,9},{5,13},{9,1},{13,5},{2,10},{6,14},... | collective-permute-start | bytes 442376 | tf_op jit(solution)/shard_map/ppermute | solution.py:20
  58.3 10.3 %collective-permute-start.20 = (bf16[64,1152]{1,0:T(8,128)(2,1)S(1)}, bf16[64,1152]{1,0:T(8,128)(2,1)S(1)}, u32[]{:S(2)}, u32[]{:S(2)}) collective-permute-start(bf16[64,1152]{1,0:T(8,128)(2,1)S(1)} %shard_map.99.refs_0_.error_ref), channel_id=1, source_target_pairs={{0,4},{4,0},{8,12},{12,8},{1,5},{5,1},{9,13},{13,9},{2,6},{6,2},{1... | collective-permute-start | bytes 442376 | tf_op jit(solution)/shard_map/ppermute | solution.py:20
  58.3 11.1 %collective-permute-start.19 = (bf16[64,1152]{1,0:T(8,128)(2,1)S(1)}, bf16[64,1152]{1,0:T(8,128)(2,1)S(1)}, u32[]{:S(2)}, u32[]{:S(2)}) collective-permute-start(bf16[64,1152]{1,0:T(8,128)(2,1)S(1)} %shard_map.99.refs_0_.error_ref), channel_id=1, source_target_pairs={{0,8},{4,12},{8,0},{12,4},{1,9},{5,13},{9,1},{13,5},{2,10},{6,14},... | collective-permute-start | bytes 442376 | tf_op jit(solution)/shard_map/ppermute | solution.py:20
  60.7 11.0 %collective-permute-start.22 = (bf16[64,1152]{1,0:T(8,128)(2,1)S(1)}, bf16[64,1152]{1,0:T(8,128)(2,1)S(1)}, u32[]{:S(2)}, u32[]{:S(2)}) collective-permute-start(bf16[64,1152]{1,0:T(8,128)(2,1)S(1)} %shard_map.101.refs_1_.error_ref), channel_id=1, source_target_pairs={{0,4},{4,0},{8,12},{12,8},{1,5},{5,1},{9,13},{13,9},{2,6},{6,2},{1... | collective-permute-start | bytes 442376 | tf_op jit(solution)/shard_map/ppermute | solution.py:20
  60.9 13.1 %collective-permute-start.21 = (bf16[64,1152]{1,0:T(8,128)(2,1)S(1)}, bf16[64,1152]{1,0:T(8,128)(2,1)S(1)}, u32[]{:S(2)}, u32[]{:S(2)}) collective-permute-start(bf16[64,1152]{1,0:T(8,128)(2,1)S(1)} %shard_map.101.refs_1_.error_ref), channel_id=1, source_target_pairs={{0,8},{4,12},{8,0},{12,4},{1,9},{5,13},{9,1},{13,5},{2,10},{6,14},... | collective-permute-start | bytes 442376 | tf_op jit(solution)/shard_map/ppermute | solution.py:20
  64.5 17.4 %collective-permute-start.17 = (bf16[64,1152]{1,0:T(8,128)(2,1)S(1)}, bf16[64,1152]{1,0:T(8,128)(2,1)S(1)}, u32[]{:S(2)}, u32[]{:S(2)}) collective-permute-start(bf16[64,1152]{1,0:T(8,128)(2,1)S(1)} %shard_map.99.refs_0_.error_ref), channel_id=1, source_target_pairs={{0,1},{1,0},{2,3},{3,2},{4,5},{5,4},{6,7},{7,6},{8,9},{9,8},{10,11... | collective-permute-start | bytes 442376 | tf_op jit(solution)/shard_map/ppermute | solution.py:20
  68.6 13.3 %collective-permute-start.18 = (bf16[64,1152]{1,0:T(8,128)(2,1)S(1)}, bf16[64,1152]{1,0:T(8,128)(2,1)S(1)}, u32[]{:S(2)}, u32[]{:S(2)}) collective-permute-start(bf16[64,1152]{1,0:T(8,128)(2,1)S(1)} %shard_map.101.refs_1_.error_ref), channel_id=1, source_target_pairs={{0,1},{1,0},{2,3},{3,2},{4,5},{5,4},{6,7},{7,6},{8,9},{9,8},{10,11... | collective-permute-start | bytes 442376 | tf_op jit(solution)/shard_map/ppermute | solution.py:20
  69.5 7.3 %collective-permute-start.23 = (bf16[64,1152]{1,0:T(8,128)(2,1)S(1)}, bf16[64,1152]{1,0:T(8,128)(2,1)S(1)}, u32[]{:S(2)}, u32[]{:S(2)}) collective-permute-start(bf16[64,1152]{1,0:T(8,128)(2,1)S(1)} %collective-permute-done.19.error_ref), channel_id=1, source_target_pairs={{0,4},{4,0},{8,12},{12,8},{1,5},{5,1},{9,13},{13,9},{2,6},{6,2},{1... | collective-permute-start | bytes 442376 | tf_op jit(solution)/shard_map/ppermute | solution.py:20
  73.9 5.2 %collective-permute-start.24 = (bf16[64,1152]{1,0:T(8,128)(2,1)S(1)}, bf16[64,1152]{1,0:T(8,128)(2,1)S(1)}, u32[]{:S(2)}, u32[]{:S(2)}) collective-permute-start(bf16[64,1152]{1,0:T(8,128)(2,1)S(1)} %collective-permute-done.21.error_ref), channel_id=1, source_target_pairs={{0,4},{4,0},{8,12},{12,8},{1,5},{5,1},{9,13},{13,9},{2,6},{6,2},{1... | collective-permute-start | bytes 442376 | tf_op jit(solution)/shard_map/ppermute | solution.py:20
  79.6 3.7 %collective-permute-start.26 = (f32[4,192]{1,0:T(4,128)S(1)}, f32[4,192]{1,0:T(4,128)S(1)}, u32[]{:S(2)}, u32[]{:S(2)}) collective-permute-start(f32[4,192]{1,0:T(4,128)S(1)} %get-tuple-element.64), channel_id=1, source_target_pairs={{0,2},{2,0},{1,3},{3,1},{4,6},{6,4},{5,7},{7,5},{8,10},{10,8},{9,1... | collective-permute-start | bytes 9224 | tf_op jit(solution)/shard_map/ppermute | solution.py:20
  81.1 3.0 %collective-permute-start.27 = (f32[4,192]{1,0:T(4,128)S(1)}, f32[4,192]{1,0:T(4,128)S(1)}, u32[]{:S(2)}, u32[]{:S(2)}) collective-permute-start(f32[4,192]{1,0:T(4,128)S(1)} %get-tuple-element.65), channel_id=1, source_target_pairs={{0,3},{1,2},{2,1},{3,0},{4,7},{5,6},{6,5},{7,4},{8,11},{9,10},{10,... | collective-permute-start | bytes 9224 | tf_op jit(solution)/shard_map/ppermute | solution.py:26
  81.1 3.0 %collective-permute-start.25 = (f32[4,192]{1,0:T(4,128)S(1)}, f32[4,192]{1,0:T(4,128)S(1)}, u32[]{:S(2)}, u32[]{:S(2)}) collective-permute-start(f32[4,192]{1,0:T(4,128)S(1)} %get-tuple-element.65), channel_id=1, source_target_pairs={{0,1},{1,0},{2,3},{3,2},{4,5},{5,4},{6,7},{7,6},{8,9},{9,8},{10,11... | collective-permute-start | bytes 9224 | tf_op jit(solution)/shard_map/ppermute | solution.py:20
